TPU v7x, 32 devices: a whole 2x2x4 slice. The times are simulated.
32 devices in a mesh: src: 4 (over y, x), tgt: 8 (over z, core).
Axes of the slice: x: 2, y: 2, z: 4, core: 2. Of those that a mesh axis runs over, the one named last changes fastest.
Arguments:
- residual: bfloat16 [4, 512, 2304], replicated, may hold values from -6 to 6
- targets: bfloat16 [4, 2304, 512], P(None, 'tgt'), may hold values from -6 to 6
- enc_weight: bfloat16 [4, 2304, 16384], P(None, None, ('src', 'tgt')), may hold values from -0.125 to 0.125
- enc_bias: float32 [4, 16384], P(None, ('src', 'tgt')), may hold values from -3 to 3
- active: int32 [4, 512, 16384], P(None, None, ('src', 'tgt')), may hold values 0 or 1
- dec_weight: bfloat16 [40, 2304, 4096], P('src', 'tgt'), may hold values from -0.046875 to 0.046875
- dec_bias: float32 [4, 2304], P(None, 'tgt'), may hold values from -3 to 3
- tile_pairs: int32 [40, 2], P('src'), may hold values from 0 to 3, as said below
Outputs:
- dec_grad: bfloat16 [40, 2304, 4096], P('src', 'tgt')
- enc_grad: bfloat16 [4, 2304, 16384], P(None, None, ('src', 'tgt'))
- bias_grad: float32 [4, 16384], P(None, ('src', 'tgt'))
Inputs may be any that keep to these rules, and one draw needn't show every extreme that they name: `tile_pairs`: rows b * 10 to (b + 1) * 10 - 1 serve latent block b; among them each pair (source, target) with source <= target appears exactly once, source in column 0 and target in column 1.
All inputs are finite; a program needn't handle non-finite values. No bound on the sum of `active` on one device may be relied on, other than what follows from the above.
Results may differ from a plain program's by a relative error of at most 0.019.
Values may be sent and summed in bfloat16 or wider, within the bound.
No kernel may reach another device: no remote copies, remote signals or barrier semaphores. Data moves between devices by JAX's collectives and lax.ppermute only.
A program may use at most 192 MiB of HBM per device.

v0:
```python
import jax
import jax.numpy as jnp
from jax import lax
from jax.sharding import PartitionSpec as P


def select_layer(array, index):
    return lax.dynamic_index_in_dim(array, index, 0, keepdims=False)


def add_layer(total, index, value):
    current = lax.dynamic_slice_in_dim(total, index, 1, 0)
    return lax.dynamic_update_slice_in_dim(total, current + value[None], index, 0)


def decoder_term(error_rows, lat_block):
    product = lax.dot_general(
        error_rows, lat_block, (((1,), (0,)), ((), ())), preferred_element_type=jnp.float32
    )
    return product.astype(jnp.bfloat16)


def shards(residual, targets, enc_weight, enc_bias, active, dec_weight, dec_bias, tile_pairs):
    layers = residual.shape[0]
    tok_all = residual.shape[1]
    width_part = targets.shape[1]
    block_width = dec_weight.shape[2]
    mask_own = active.astype(jnp.float32)
    preact = jnp.einsum("lrd,ldc->lrc", residual, enc_weight, preferred_element_type=jnp.float32)
    latent = ((preact + enc_bias[:, None, :]) * mask_own).astype(jnp.bfloat16)
    blocks = lax.all_gather(latent, "tgt", axis=2, tiled=True)
    source_ids = tile_pairs[:, 0]
    target_ids = tile_pairs[:, 1]

    def add_recon(recon_sum, slot_data):
        weight, source, target = slot_data
        lat_block = select_layer(blocks, source)
        recon_term = lax.dot_general(
            weight, lat_block, (((1,), (1,)), ((), ())), preferred_element_type=jnp.float32
        )
        return (add_layer(recon_sum, target, recon_term), None)

    recon_zero = jnp.zeros((layers, width_part, tok_all), jnp.float32)
    recon_sum = lax.scan(add_recon, recon_zero, (dec_weight, source_ids, target_ids))[0]
    whole_sum = lax.psum(recon_sum.astype(jnp.bfloat16), "src").astype(jnp.float32)
    error_part = (whole_sum + dec_bias[:, :, None] - targets.astype(jnp.float32)).astype(
        jnp.bfloat16
    )

    def step_partial(grad_sum, slot_data):
        weight, source, target = slot_data
        error_rows = select_layer(error_part, target)
        lat_block = select_layer(blocks, source)
        lat_term = lax.dot_general(
            error_rows, weight, (((0,), (0,)), ((), ())), preferred_element_type=jnp.float32
        )
        return (add_layer(grad_sum, source, lat_term), decoder_term(error_rows, lat_block))

    grad_zero = jnp.zeros((layers, tok_all, block_width), jnp.float32)
    grad_sum, dec_grad = lax.scan(step_partial, grad_zero, (dec_weight, source_ids, target_ids))
    owned_grad = lax.psum_scatter(
        grad_sum.astype(jnp.bfloat16), "tgt", scatter_dimension=2, tiled=True
    ).astype(jnp.float32)
    pre_grad = (owned_grad * mask_own).astype(jnp.bfloat16)
    enc_grad = jnp.einsum(
        "lrd,lrc->ldc", residual, pre_grad, preferred_element_type=jnp.float32
    ).astype(jnp.bfloat16)
    bias_grad = jnp.sum(pre_grad.astype(jnp.float32), axis=1)
    return (dec_grad, enc_grad, bias_grad)


def solution(mesh):
    in_specs = (
        P(),
        P(None, "tgt", None),
        P(None, None, ("src", "tgt")),
        P(None, ("src", "tgt")),
        P(None, None, ("src", "tgt")),
        P("src", "tgt", None),
        P(None, "tgt"),
        P("src", None),
    )
    out_specs = (P("src", "tgt", None), P(None, None, ("src", "tgt")), P(None, ("src", "tgt")))
    return jax.shard_map(shards, mesh=mesh, in_specs=in_specs, out_specs=out_specs, check_vma=False)
```

profile of v0, /device:TPU:0, one launch (start us, length us, event | category | flops | bytes accessed | tf_op | source)
XLA Modules:
  0.0 753.0 jit_solution(15101205394260344513)
XLA Ops:
  7.2 12.0 %multiply_convert_fusion.1 = bf16[4,512,512]{2,1,0:T(8,128)(2,1)} fusion(s32[4,512,512]{2,1,0:T(8,128)} %param.16, f32[4,512]{1,0:T(4,128)} %param.15, bf16[4,512,2304]{2,1,0:T(8,128)(2,1)} %param.12, bf16[4,2304,512]{2,1,0:T(8,128)(2,1)} %param.14), kind=kOutput, calls=%fused_computation.27 | convolution fusion | flops 4836032512 | bytes 25174016 | tf_op jit(solution)/shard_map/lrd,ldc->lrc/dot_general | solution.py:29
  19.3 153.9 %all-gather.2.cloned.1.call-done = bf16[4,512,4096]{2,1,0:T(8,128)(2,1)} async-done(((bf16[4,512,512]{2,1,0:T(8,128)(2,1)}), bf16[4,512,4096]{2,1,0:T(8,128)(2,1)}) %all-gather.2.cloned.1.call-update) | async-done | bytes 16777232 | tf_op jit(solution)/shard_map/all_gather | solution.py:31
  173.5 94.1 %while.22 = (s32[]{:T(128)}, f32[4,288,512]{2,1,0:T(8,128)S(1)}, s32[10]{0:T(128)S(1)}, bf16[10,288,4096]{2,1,0:T(8,128)(2,1)}, s32[10]{0:T(128)S(1)}, /*index=5...) while((s32[]{:T(128)}, f32[4,288,512]{2,1,0:T(8,128)S(1)}, s32[10]{0:T(128)S(1)}, ...), condition=%wide.region_1.2_spmd, body=%wide.region_0.1_spmd.sunk | while | flops 1208107008 | bytes 7733453 | solution.py:44
  176.0 0.6 dynamic_slice.91
  178.6 4.3 fusion.48
  188.0 4.3 fusion.48
  194.9 0.6 dynamic_slice.91
  197.4 4.3 fusion.48
  206.8 4.3 fusion.48
  213.7 0.6 dynamic_slice.91
  216.2 4.3 fusion.48
  225.6 4.3 fusion.48
  232.5 0.6 dynamic_slice.91
  235.1 4.3 fusion.48
  244.5 4.3 fusion.48
  251.3 0.6 dynamic_slice.91
  253.9 4.3 fusion.48
  263.3 4.3 fusion.48
  267.7 1.2 convert_element_type.41
  269.1 52.6 %all-reduce.2.cloned.1.call-done = bf16[4,288,512]{2,1,0:T(8,128)(2,1)} async-done(((bf16[4,288,512]{2,1,0:T(8,128)(2,1)}), bf16[4,288,512]{2,1,0:T(8,128)(2,1)}) %all-reduce.2.cloned.1.call-update) | async-done | bytes 1179664 | tf_op jit(solution)/shard_map/psum | solution.py:45
  321.7 1.7 subtract_convert_fusion
  323.4 11.2 %broadcast_in_dim.21 = f32[4,512,4096]{2,1,0:T(8,128)} broadcast(f32[]{:T(128)} %constant.31.clone.1), dimensions={} | broadcast | bytes 33554436 | tf_op jit(solution)/shard_map/broadcast_in_dim | solution.py:59
  334.6 197.6 %while.23 = (s32[]{:T(128)}, f32[4,512,4096]{2,1,0:T(8,128)}, bf16[10,288,4096]{2,1,0:T(8,128)(2,1)}, s32[10]{0:T(128)S(1)}, s32[10]{0:T(128)S(1)}, /*index=5*/b...) while((s32[]{:T(128)}, f32[4,512,4096]{2,1,0:T(8,128)}, ...), condition=%wide.region_4.5_spmd, body=%wide.region_3.4_spmd.sunk | while | flops 2419195904 | bytes 26280168 | solution.py:60
  339.6 5.0 fusion.54
  344.6 9.7 %fusion.53 = f32[4,512,4096]{2,1,0:T(8,128)} fusion(f32[4,512,4096]{2,1,0:T(8,128)} %get-tuple-element.239, s32[]{:T(128)S(6)} %select_n.23, bf16[10,288,4096]{2,1,0:T(8,128)(2,1)} %get-tuple-element.255, s32[]{:T(128)S(6)} %copy.27, bf16[4,288,512]{2,1,0:T(8,128)(2,1)S(1)} %get-tuple-element.254, s32[]{:T(128)S(6)} %select_n.24), kind=kOutput, calls=%fused_computation.10.clone.1 | convolution fusion | flops 1210056704 | bytes 19431436 | tf_op jit(solution)/shard_map/while/body/eval_jaxpr/dot_general | solution.py:54
  359.4 5.0 fusion.54
  364.4 9.7 %fusion.53 = f32[4,512,4096]{2,1,0:T(8,128)} fusion(f32[4,512,4096]{2,1,0:T(8,128)} %get-tuple-element.239, s32[]{:T(128)S(6)} %select_n.23, bf16[10,288,4096]{2,1,0:T(8,128)(2,1)} %get-tuple-element.255, s32[]{:T(128)S(6)} %copy.27, bf16[4,288,512]{2,1,0:T(8,128)(2,1)S(1)} %get-tuple-element.254, s32[]{:T(128)S(6)} %select_n.24), kind=kOutput, calls=%fused_computation.10.clone.1 | convolution fusion | flops 1210056704 | bytes 19431436 | tf_op jit(solution)/shard_map/while/body/eval_jaxpr/dot_general | solution.py:54
  379.2 5.0 fusion.54
  384.2 9.7 %fusion.53 = f32[4,512,4096]{2,1,0:T(8,128)} fusion(f32[4,512,4096]{2,1,0:T(8,128)} %get-tuple-element.239, s32[]{:T(128)S(6)} %select_n.23, bf16[10,288,4096]{2,1,0:T(8,128)(2,1)} %get-tuple-element.255, s32[]{:T(128)S(6)} %copy.27, bf16[4,288,512]{2,1,0:T(8,128)(2,1)S(1)} %get-tuple-element.254, s32[]{:T(128)S(6)} %select_n.24), kind=kOutput, calls=%fused_computation.10.clone.1 | convolution fusion | flops 1210056704 | bytes 19431436 | tf_op jit(solution)/shard_map/while/body/eval_jaxpr/dot_general | solution.py:54
  398.9 5.0 fusion.54
  403.9 9.7 %fusion.53 = f32[4,512,4096]{2,1,0:T(8,128)} fusion(f32[4,512,4096]{2,1,0:T(8,128)} %get-tuple-element.239, s32[]{:T(128)S(6)} %select_n.23, bf16[10,288,4096]{2,1,0:T(8,128)(2,1)} %get-tuple-element.255, s32[]{:T(128)S(6)} %copy.27, bf16[4,288,512]{2,1,0:T(8,128)(2,1)S(1)} %get-tuple-element.254, s32[]{:T(128)S(6)} %select_n.24), kind=kOutput, calls=%fused_computation.10.clone.1 | convolution fusion | flops 1210056704 | bytes 19431436 | tf_op jit(solution)/shard_map/while/body/eval_jaxpr/dot_general | solution.py:54
  418.7 5.0 fusion.54
  423.7 9.7 %fusion.53 = f32[4,512,4096]{2,1,0:T(8,128)} fusion(f32[4,512,4096]{2,1,0:T(8,128)} %get-tuple-element.239, s32[]{:T(128)S(6)} %select_n.23, bf16[10,288,4096]{2,1,0:T(8,128)(2,1)} %get-tuple-element.255, s32[]{:T(128)S(6)} %copy.27, bf16[4,288,512]{2,1,0:T(8,128)(2,1)S(1)} %get-tuple-element.254, s32[]{:T(128)S(6)} %select_n.24), kind=kOutput, calls=%fused_computation.10.clone.1 | convolution fusion | flops 1210056704 | bytes 19431436 | tf_op jit(solution)/shard_map/while/body/eval_jaxpr/dot_general | solution.py:54
  438.5 5.0 fusion.54
  443.4 9.7 %fusion.53 = f32[4,512,4096]{2,1,0:T(8,128)} fusion(f32[4,512,4096]{2,1,0:T(8,128)} %get-tuple-element.239, s32[]{:T(128)S(6)} %select_n.23, bf16[10,288,4096]{2,1,0:T(8,128)(2,1)} %get-tuple-element.255, s32[]{:T(128)S(6)} %copy.27, bf16[4,288,512]{2,1,0:T(8,128)(2,1)S(1)} %get-tuple-element.254, s32[]{:T(128)S(6)} %select_n.24), kind=kOutput, calls=%fused_computation.10.clone.1 | convolution fusion | flops 1210056704 | bytes 19431436 | tf_op jit(solution)/shard_map/while/body/eval_jaxpr/dot_general | solution.py:54
  458.2 5.0 fusion.54
  463.2 9.7 %fusion.53 = f32[4,512,4096]{2,1,0:T(8,128)} fusion(f32[4,512,4096]{2,1,0:T(8,128)} %get-tuple-element.239, s32[]{:T(128)S(6)} %select_n.23, bf16[10,288,4096]{2,1,0:T(8,128)(2,1)} %get-tuple-element.255, s32[]{:T(128)S(6)} %copy.27, bf16[4,288,512]{2,1,0:T(8,128)(2,1)S(1)} %get-tuple-element.254, s32[]{:T(128)S(6)} %select_n.24), kind=kOutput, calls=%fused_computation.10.clone.1 | convolution fusion | flops 1210056704 | bytes 19431436 | tf_op jit(solution)/shard_map/while/body/eval_jaxpr/dot_general | solution.py:54
  478.0 5.0 fusion.54
  483.0 9.7 %fusion.53 = f32[4,512,4096]{2,1,0:T(8,128)} fusion(f32[4,512,4096]{2,1,0:T(8,128)} %get-tuple-element.239, s32[]{:T(128)S(6)} %select_n.23, bf16[10,288,4096]{2,1,0:T(8,128)(2,1)} %get-tuple-element.255, s32[]{:T(128)S(6)} %copy.27, bf16[4,288,512]{2,1,0:T(8,128)(2,1)S(1)} %get-tuple-element.254, s32[]{:T(128)S(6)} %select_n.24), kind=kOutput, calls=%fused_computation.10.clone.1 | convolution fusion | flops 1210056704 | bytes 19431436 | tf_op jit(solution)/shard_map/while/body/eval_jaxpr/dot_general | solution.py:54
  497.7 5.0 fusion.54
  502.7 9.7 %fusion.53 = f32[4,512,4096]{2,1,0:T(8,128)} fusion(f32[4,512,4096]{2,1,0:T(8,128)} %get-tuple-element.239, s32[]{:T(128)S(6)} %select_n.23, bf16[10,288,4096]{2,1,0:T(8,128)(2,1)} %get-tuple-element.255, s32[]{:T(128)S(6)} %copy.27, bf16[4,288,512]{2,1,0:T(8,128)(2,1)S(1)} %get-tuple-element.254, s32[]{:T(128)S(6)} %select_n.24), kind=kOutput, calls=%fused_computation.10.clone.1 | convolution fusion | flops 1210056704 | bytes 19431436 | tf_op jit(solution)/shard_map/while/body/eval_jaxpr/dot_general | solution.py:54
  517.5 5.0 fusion.54
  522.5 9.7 %fusion.53 = f32[4,512,4096]{2,1,0:T(8,128)} fusion(f32[4,512,4096]{2,1,0:T(8,128)} %get-tuple-element.239, s32[]{:T(128)S(6)} %select_n.23, bf16[10,288,4096]{2,1,0:T(8,128)(2,1)} %get-tuple-element.255, s32[]{:T(128)S(6)} %copy.27, bf16[4,288,512]{2,1,0:T(8,128)(2,1)S(1)} %get-tuple-element.254, s32[]{:T(128)S(6)} %select_n.24), kind=kOutput, calls=%fused_computation.10.clone.1 | convolution fusion | flops 1210056704 | bytes 19431436 | tf_op jit(solution)/shard_map/while/body/eval_jaxpr/dot_general | solution.py:54
  532.2 17.4 %convert_element_type.45 = bf16[4,512,4096]{2,1,0:T(8,128)(2,1)} convert(f32[4,512,4096]{2,1,0:T(8,128)} %get-tuple-element.80) | non-fusion elementwise | flops 8388608 | bytes 50331648 | tf_op jit(solution)/shard_map/convert_element_type | solution.py:62
  549.6 168.4 %reduce-scatter.2.cloned.1.call-done = bf16[4,512,512]{2,1,0:T(8,128)(2,1)} async-done(((bf16[4,512,4096]{2,1,0:T(8,128)(2,1)}), bf16[4,512,512]{2,1,0:T(8,128)(2,1)}) %reduce-scatter.2.cloned.1.call-update) | async-done | bytes 2097168 | tf_op jit(solution)/shard_map/reduce_scatter | solution.py:61
  718.0 12.2 %convert_bitcast_fusion = bf16[4,2304,512]{1,2,0:T(8,128)(2,1)} fusion(bf16[4,512,2304]{2,1,0:T(8,128)(2,1)} %param.12, bf16[4,512,512]{2,1,0:T(8,128)(2,1)} %reduce-scatter.2.cloned.1.call-done, s32[4,512,512]{2,1,0:T(8,128)} %param.16), kind=kOutput, calls=%fused_computation.24 | convolution fusion | flops 4840751104 | bytes 25165824 | tf_op jit(solution)/shard_map/lrd,lrc->ldc/dot_general | solution.py:65
  730.3 12.8 %copy.12 = bf16[4,2304,512]{2,1,0:T(8,128)(2,1)} copy(bf16[4,2304,512]{1,2,0:T(8,128)(2,1)} %convert_bitcast_fusion) | data formatting | bytes 18874368
  743.0 3.5 convert_reduce_fusion
  (52 shorter events, 21.2 us)
Async XLA Ops:
  7.2 12.1 %copy-start.3 = (s32[10,2]{0,1:T(2,128)S(1)}, s32[10,2]{0,1:T(2,128)}, u32[]{:S(2)}) copy-start(s32[10,2]{0,1:T(2,128)} %param.19) | copy-start | bytes 244
  7.2 166.0 %all-gather.2.cloned.1.call-start = ((), (), s32[]{:S(2)}) async-start(), calls=%async_computation.1 | async-start | bytes 18874368 | tf_op jit(solution)/shard_map/all_gather | solution.py:31
  19.2 302.4 %all-reduce.2.cloned.1.call-start = ((), (), s32[]{:S(2)}) async-start(), calls=%async_computation.2 | async-start | bytes 2359296 | tf_op jit(solution)/shard_map/psum | solution.py:45
  267.6 54.0 %copy-start.1 = (bf16[4,288,512]{2,1,0:T(8,128)(2,1)S(1)}, bf16[4,288,512]{2,1,0:T(8,128)(2,1)}, u32[]{:S(2)}) copy-start(bf16[4,288,512]{2,1,0:T(8,128)(2,1)} %param.13) | copy-start | bytes 3538948
  267.7 54.0 %copy-start.2 = (f32[4,288]{1,0:T(4,128)S(1)}, f32[4,288]{1,0:T(4,128)}, u32[]{:S(2)}) copy-start(f32[4,288]{1,0:T(4,128)} %param.18) | copy-start | bytes 13828
  268.9 449.1 %reduce-scatter.2.cloned.1.call-start = ((), (), s32[]{:S(2)}) async-start(), calls=%async_computation.3 | async-start | bytes 18874368 | tf_op jit(solution)/shard_map/reduce_scatter | solution.py:61
  730.3 12.8 %copy-start = (bf16[4,512,512]{2,1,0:T(8,128)(2,1)S(1)}, bf16[4,512,512]{2,1,0:T(8,128)(2,1)}, u32[]{:S(2)}) copy-start(bf16[4,512,512]{2,1,0:T(8,128)(2,1)} %reduce-scatter.2.cloned.1.call-done) | copy-start | bytes 6291460
Sparse Core Ops, SparseCore 0:
  19.4 153.7 all-gather.1
  269.0 52.6 all-reduce.1
  549.7 168.2 reduce-scatter.1
where the time goes:
time: 755 us; the launch traced here: 753 us
  waiting for transfers between devices  375 us (50%)
  matrix products  215 us (28%)
  loops' own time  78 us (10%)
  local copies, waits for them, and re-layouts  47.8 us (6%)
  other arithmetic  23.7 us (3%)
  between operations  13.8 us (2%)
    reduce_scatter x1, waiting for transfers between devices, shards(): lax.psum_scatter(grad_sum.astype(jnp.bfloat16), 'tgt', scatter_dimension=...  168 us
    all_gather x1, waiting for transfers between devices, shards(): blocks = lax.all_gather(latent, 'tgt', axis=2, tiled=True)  154 us
    dot_general x10, matrix products, step_partial(): lax.dot_general(error_rows, weight, (((0,), (0,)), ((), ())), preferred_e...  97.1 us
    psum x1, waiting for transfers between devices, shards(): lax.psum(recon_sum.astype(jnp.bfloat16), 'src').astype(jnp.float32)  52.6 us
    dot_general x10, matrix products, decoder_term(): lax.dot_general(error_rows, lat_block, (((1,), (0,)), ((), ())), preferre...  50 us
    dot_general x10, matrix products, add_recon(): lax.dot_general(weight, lat_block, (((1,), (1,)), ((), ())), preferred_el...  43.3 us
    another operation x1, loops' own time, shards(): lax.scan(add_recon, recon_zero, (dec_weight, source_ids, target_ids))[0]  39.1 us
    another operation x1, loops' own time, shards(): lax.scan(step_partial, grad_zero, (dec_weight, source_ids, target_ids))  38.9 us
  transfers between devices with their start and end apart: 3, of which 3 were waited for; matrix products, arithmetic and copies ran while one was open for 0% of the time, Pallas kernels for 0%

commit v1 on v0

v1 whole, which is shorter than its diff:
```python
import functools

import jax
import jax.numpy as jnp
import numpy as np
from jax import lax
from jax.experimental import pallas as pl
from jax.experimental.pallas import tpu as pltpu
from jax.sharding import PartitionSpec as P

F32 = jnp.float32
BF16 = jnp.bfloat16
NT = (((1,), (1,)), ((), ()))
NN = (((1,), (0,)), ((), ()))


def dot(a, b, dims=NN):
    return lax.dot_general(a, b, dims, preferred_element_type=F32)


def params(limit_mib):
    return pltpu.CompilerParams(vmem_limit_bytes=limit_mib * 2**20)


def pair_list(layers):
    return [(s, t) for s in range(layers) for t in range(s, layers)]


def gather_table(chips):
    table = np.full((2 * chips, 2 * chips - 1, 2), -1, np.int32)
    for me in range(2 * chips):
        chip, core = divmod(me, 2)
        way = 1 - 2 * core
        places = [(chip, core)]
        places += [(chip - way * j, core) for j in range(1, chips)]
        places += [(chip + way * j, 1 - core) for j in range(1, chips)]
        for piece, (place, order) in enumerate(places):
            if 0 <= place < chips:
                for half in range(2):
                    table[me, piece, half] = 2 * place + (order ^ half)
    return table.reshape(2 * chips, -1)


def scatter_table(chips):
    table = np.zeros((2 * chips, 3, 2 * chips), np.int32)
    last = 2 * (chips - 1)
    for me in range(2 * chips):
        chip, core = divmod(me, 2)
        way = 1 - 2 * core
        gives, keeps = [], []
        for dist in range(chips - 1, 0, -1):
            slot = 2 * (chips - 1 - dist)
            for half in range(2):
                if 0 <= chip - way * dist < chips:
                    gives.append((2 * (chip - way * dist) + ((1 - core) ^ half), slot + half))
                if 0 <= chip + way * dist < chips:
                    keeps.append((2 * (chip + way * dist) + (core ^ half), slot + half))
        gives.append((2 * chip + 1 - core, last))
        keeps.append((2 * chip + core, last))
        for step, (tile, slot) in enumerate(gives):
            table[me, :, step] = (tile, slot, keeps[0][1])
        for step, (tile, slot) in enumerate(keeps):
            table[me, :, len(gives) + step] = (tile, gives[-1][1], slot)
    return table.reshape(2 * chips, -1)


def encode_kernel(res_ref, weight_ref, bias_ref, active_ref, out_ref):
    pre = dot(res_ref[0], weight_ref[0]) + bias_ref[0]
    out_ref[0] = (pre * active_ref[0].astype(F32)).astype(BF16)


def encode(residual, enc_weight, bias, active, start, rows):
    layers, _, width = residual.shape
    own = enc_weight.shape[2]
    at = start // rows
    return pl.pallas_call(
        encode_kernel,
        grid=(layers,),
        in_specs=[
            pl.BlockSpec((1, rows, width), lambda s: (s, at, 0)),
            pl.BlockSpec((1, width, own), lambda s: (s, 0, 0)),
            pl.BlockSpec((1, 1, own), lambda s: (s, 0, 0)),
            pl.BlockSpec((1, rows, own), lambda s: (s, at, 0)),
        ],
        out_specs=pl.BlockSpec((1, rows, own), lambda s: (s, 0, 0)),
        out_shape=jax.ShapeDtypeStruct((layers, rows, own), BF16),
        compiler_params=params(32),
        name="encode",
    )(residual, enc_weight, bias, active)


def recon_kernel(pairs, pieces, layers, start, aliased, meta, *refs):
    npairs = len(pairs)
    weights = refs[:npairs]
    piece_refs = refs[npairs : npairs + pieces]
    rest = refs[npairs + pieces + aliased :]
    low_ref, high_ref, lat_out, lat, total, in_sem, out_sem = rest
    step = pl.program_id(0)
    rows = lat.shape[2]

    def fetch(piece, half):
        slot = meta[npairs + 2 * piece + half]
        return slot, pltpu.make_async_copy(
            piece_refs[piece].at[half], lat.at[jnp.maximum(slot, 0)], in_sem.at[2 * piece + half]
        )

    def keep():
        return pltpu.make_async_copy(lat, lat_out.at[:, :, pl.ds(start, rows)], out_sem)

    @pl.when(step == 0)
    def _():
        for piece in range(pieces):
            for half in range(2):
                slot, copy = fetch(piece, half)
                pl.when(slot >= 0)(copy.start)
        total[...] = jnp.zeros_like(total)
        for piece in range(pieces):
            for half in range(2):
                slot, copy = fetch(piece, half)
                pl.when(slot >= 0)(copy.wait)
        keep().start()

    for t in range(layers):
        term = total[t]
        for p, (source, target) in enumerate(pairs):
            if target == t:
                term = term + dot(weights[p][0], lat[step, source], NT)
        total[t] = term

    @pl.when(step == pl.num_programs(0) - 1)
    def _():
        half = low_ref.shape[0]
        low_ref[...] = total[:half].astype(BF16)
        high_ref[...] = total[half:].astype(BF16)
        keep().wait()


def weight_specs(npairs, feat, own, column):
    return [
        pl.BlockSpec((1, feat, own), functools.partial(lambda p, i, meta: (meta[p], 0, column(i, meta)), p))
        for p in range(npairs)
    ]


def recon(meta, dec_weight, pieces, lat_all, tok, start):
    npairs, feat, cols = dec_weight.shape
    _, layers, rows, own = pieces[0].shape
    tiles = cols // own
    pairs = pair_list(layers)
    any_spec = pl.BlockSpec(memory_space=pl.ANY)
    half = layers // 2
    extra = [] if lat_all is None else [lat_all]
    outs = (
        jax.ShapeDtypeStruct((half, feat, rows), BF16),
        jax.ShapeDtypeStruct((layers - half, feat, rows), BF16),
        jax.ShapeDtypeStruct((tiles, layers, tok, own), BF16),
    )
    return pl.pallas_call(
        functools.partial(recon_kernel, pairs, len(pieces), layers, start, len(extra)),
        grid_spec=pltpu.PrefetchScalarGridSpec(
            num_scalar_prefetch=1,
            grid=(tiles,),
            in_specs=weight_specs(npairs, feat, own, lambda i, meta: i) + [any_spec] * (len(pieces) + len(extra)),
            out_specs=[
                pl.BlockSpec(outs[0].shape, lambda i, meta: (0, 0, 0)),
                pl.BlockSpec(outs[1].shape, lambda i, meta: (0, 0, 0)),
                any_spec,
            ],
            scratch_shapes=[
                pltpu.VMEM((tiles, layers, rows, own), BF16),
                pltpu.VMEM((layers, feat, rows), F32),
                pltpu.SemaphoreType.DMA((2 * len(pieces),)),
                pltpu.SemaphoreType.DMA,
            ],
        ),
        out_shape=outs,
        input_output_aliases={} if lat_all is None else {1 + npairs + len(pieces): 2},
        compiler_params=params(40),
        cost_estimate=pl.CostEstimate(
            flops=2 * npairs * feat * cols * rows, bytes_accessed=2 * npairs * feat * cols, transcendentals=0
        ),
        name="recon",
    )(meta, *([dec_weight] * npairs), *pieces, *extra)


def grad_kernel(pairs, layers, aliased, meta, *refs):
    npairs = len(pairs)
    weights = refs[:npairs]
    low_ref, high_ref, bias_ref, target_ref = refs[npairs : npairs + 4]
    give_ref, keep_ref, error_out, error_t, error_rest = refs[npairs + 4 + aliased :]
    step = pl.program_id(0)
    feat, rows = target_ref.shape[1:]
    main = feat // 256 * 256
    rest = feat - main

    @pl.when(step == 0)
    def _():
        half = low_ref.shape[0]
        for t in range(layers):
            whole = low_ref[t] if t < half else high_ref[t - half]
            error = (whole.astype(F32) + bias_ref[t] - target_ref[t].astype(F32)).astype(BF16)
            error_out[t] = error
            turned = error.astype(F32).T.astype(BF16)
            if main:
                error_t[t] = turned[:, :main]
            if rest:
                for s in range(layers):
                    piece = turned[:, main:]
                    error_rest[s, :, t * rest : (t + 1) * rest] = piece if t >= s else jnp.zeros_like(piece)

    tiles = []
    for s in range(layers):
        total = None
        mine = [(p, t) for p, (source, t) in enumerate(pairs) if source == s]
        if main:
            for p, t in mine:
                term = dot(error_t[t], weights[p][0, :main])
                total = term if total is None else total + term
        if rest:
            stack = [weights[p][0, main:] for p, _ in mine]
            term = dot(error_rest[s][:, s * rest :], jnp.concatenate(stack, 0))
            total = term if total is None else total + term
        tiles.append(total.astype(BF16))

    gives = meta[npairs + 3 * pl.num_programs(0)]

    @pl.when(step < gives)
    def _():
        for s in range(layers):
            give_ref[0, s] = tiles[s]

    @pl.when(step >= gives)
    def _():
        for s in range(layers):
            keep_ref[0, s] = tiles[s]


def grad(meta, dec_weight, low, high, bias, targets, error_all, start, own):
    npairs, feat, cols = dec_weight.shape
    layers, _, tok = targets.shape
    rows = low.shape[2]
    tiles = cols // own
    pairs = pair_list(layers)
    main = feat // 256 * 256
    rest = feat - main
    at = start // rows
    extra = [] if error_all is None else [error_all]
    slots = jax.ShapeDtypeStruct((tiles - 1, layers, rows, own), BF16)
    outs = (slots, slots, jax.ShapeDtypeStruct((layers, feat, tok), BF16))
    whole = lambda shape: pl.BlockSpec(shape, lambda i, meta: (0,) * len(shape))
    return pl.pallas_call(
        functools.partial(grad_kernel, pairs, layers, len(extra)),
        grid_spec=pltpu.PrefetchScalarGridSpec(
            num_scalar_prefetch=1,
            grid=(tiles,),
            in_specs=weight_specs(npairs, feat, own, lambda i, meta: meta[npairs + i])
            + [
                whole(low.shape),
                whole(high.shape),
                whole(bias.shape),
                pl.BlockSpec((layers, feat, rows), lambda i, meta: (0, 0, at)),
            ]
            + [pl.BlockSpec(memory_space=pl.ANY)] * len(extra),
            out_specs=[
                pl.BlockSpec((1, layers, rows, own), lambda i, meta: (meta[npairs + tiles + i], 0, 0, 0)),
                pl.BlockSpec((1, layers, rows, own), lambda i, meta: (meta[npairs + 2 * tiles + i], 0, 0, 0)),
                pl.BlockSpec((layers, feat, rows), lambda i, meta: (0, 0, at)),
            ],
            scratch_shapes=[
                pltpu.VMEM((layers, rows, max(main, 128)), BF16),
                pltpu.VMEM((layers, rows, max(layers * rest, 128)), BF16),
            ],
        ),
        out_shape=outs,
        input_output_aliases={} if error_all is None else {1 + npairs + 4: 2},
        compiler_params=params(40),
        cost_estimate=pl.CostEstimate(
            flops=2 * npairs * feat * cols * rows, bytes_accessed=2 * npairs * feat * cols, transcendentals=0
        ),
        name="latent_grad",
    )(meta, *([dec_weight] * npairs), low, high, bias, targets, *extra)


def dec_grad_kernel(meta, sources, targets, error_ref, lat_ref, out_ref):
    own = lat_ref.shape[3]
    for tile in range(lat_ref.shape[0]):
        out_ref[0, :, tile * own : (tile + 1) * own] = dot(error_ref[0], lat_ref[tile, 0]).astype(BF16)


def decoder_grad(perm, error_all, lat_all):
    layers, feat, tok = error_all.shape
    tiles, _, _, own = lat_all.shape
    pairs = pair_list(layers)
    npairs = len(pairs)
    sources = jnp.asarray(np.array([s for s, _ in pairs], np.int32))
    targets = jnp.asarray(np.array([t for _, t in pairs], np.int32))
    return pl.pallas_call(
        dec_grad_kernel,
        grid_spec=pltpu.PrefetchScalarGridSpec(
            num_scalar_prefetch=3,
            grid=(npairs,),
            in_specs=[
                pl.BlockSpec((1, feat, tok), lambda p, m, s, t: (t[p], 0, 0)),
                pl.BlockSpec((tiles, 1, tok, own), lambda p, m, s, t: (0, s[p], 0, 0)),
            ],
            out_specs=pl.BlockSpec((1, feat, tiles * own), lambda p, m, s, t: (m[p], 0, 0)),
        ),
        out_shape=jax.ShapeDtypeStruct((npairs, feat, tiles * own), BF16),
        compiler_params=params(40),
        cost_estimate=pl.CostEstimate(
            flops=2 * npairs * feat * tok * tiles * own, bytes_accessed=2 * npairs * feat * tiles * own, transcendentals=0
        ),
        name="dec_grad",
    )(perm, sources, targets, error_all, lat_all)


def enc_grad_kernel(parts, *refs):
    res_ref = refs[0]
    grads = refs[1 : 1 + parts]
    out_ref, bias_ref = refs[1 + parts :]
    whole = jnp.concatenate([g[0] for g in grads], 0)
    out_ref[0] = dot(res_ref[0], whole).astype(BF16)
    bias_ref[0] = jnp.sum(whole.astype(F32), axis=0, keepdims=True)


def encoder_grad(residual_t, grads):
    layers, width, tok = residual_t.shape
    _, rows, own = grads[0].shape
    return pl.pallas_call(
        functools.partial(enc_grad_kernel, len(grads)),
        grid=(layers,),
        in_specs=[pl.BlockSpec((1, width, tok), lambda s: (s, 0, 0))]
        + [pl.BlockSpec((1, rows, own), lambda s: (s, 0, 0))] * len(grads),
        out_specs=[
            pl.BlockSpec((1, width, own), lambda s: (s, 0, 0)),
            pl.BlockSpec((1, 1, own), lambda s: (s, 0, 0)),
        ],
        out_shape=(
            jax.ShapeDtypeStruct((layers, width, own), BF16),
            jax.ShapeDtypeStruct((layers, 1, own), F32),
        ),
        compiler_params=params(40),
        name="enc_grad",
    )(residual_t, *grads)


def swap_cores(value, devices):
    return lax.ppermute(value, "tgt", [(i, i ^ 1) for i in range(devices)])


def hop(value, chips, first):
    perm = []
    for chip in first:
        if chip + 1 < chips:
            perm.append((2 * chip, 2 * chip + 2))
            other = chips - 1 - chip
            perm.append((2 * other + 1, 2 * other - 1))
    return lax.ppermute(value, "tgt", perm)


def add(*values):
    total = values[0].astype(F32)
    for value in values[1:]:
        total = total + value.astype(F32)
    return total.astype(BF16)


def sum_over_src(value, size, bits):
    if size & (size - 1):
        return lax.psum(value, "src")
    for bit in bits:
        value = add(value, lax.ppermute(value, "src", [(i, i ^ (1 << bit)) for i in range(size)]))
    return value


def shards(blocks, devices, residual, targets, enc_weight, enc_bias, active, dec_weight, dec_bias, tile_pairs):
    layers, tok, _ = residual.shape
    own = enc_weight.shape[2]
    chips = devices // 2
    rows = 128
    starts = list(range(0, tok, rows))
    pairs = np.array(pair_list(layers), np.int32)
    me = lax.axis_index("tgt")

    same = jnp.all(tile_pairs[None, :, :] == pairs[:, None, :], axis=2)
    perm = jnp.sum(jnp.where(same, jnp.arange(len(pairs), dtype=jnp.int32)[None, :], 0), axis=1, dtype=jnp.int32)
    chip, core = me // 2, me % 2
    gives = 1 + 2 * jnp.where(core == 0, chip, chips - 1 - chip)
    gather_meta = jnp.concatenate([perm, jnp.asarray(gather_table(chips))[me]])
    scatter_meta = jnp.concatenate([perm, jnp.asarray(scatter_table(chips))[me], gives[None].astype(jnp.int32)])
    enc_bias3 = enc_bias[:, None, :]
    dec_bias3 = dec_bias[:, :, None]
    residual_t = jnp.swapaxes(residual, 1, 2)
    bits = [b for b in range(blocks.bit_length()) if (1 << b) < blocks]

    lat_all = error_all = None
    grads = []
    for start in starts:
        mine = encode(residual, enc_weight, enc_bias3, active, start, rows)
        block = jnp.stack([mine, swap_cores(mine, devices)])
        moved = [block]
        for j in range(1, chips):
            moved.append(hop(moved[-1], chips, range(j - 1, chips - 1)))
        pieces = moved + [swap_cores(value, devices) for value in moved[1:]]
        low, high, lat_all = recon(gather_meta, dec_weight, pieces, lat_all, tok, start)
        low = sum_over_src(low, blocks, bits)
        high = sum_over_src(high, blocks, bits[::-1])
        give, keep, error_all = grad(scatter_meta, dec_weight, low, high, dec_bias3, targets, error_all, start, own)
        given = swap_cores(give, devices)
        last = 2 * (chips - 1)
        carry = None
        for j in range(1, chips):
            at = slice(2 * (j - 1), 2 * j)
            terms = [keep[at], given[at]] + ([] if carry is None else [carry])
            carry = hop(add(*terms), chips, range(0, j))
        total = sum(v.astype(F32) for v in (keep[last], given[last], carry[0], swap_cores(carry[1], devices)))
        grads.append((total * active[:, start : start + rows].astype(F32)).astype(BF16))

    dec_grad = decoder_grad(perm, error_all, lat_all)
    enc_grad, bias_grad = encoder_grad(residual_t, grads)
    return (dec_grad, enc_grad, bias_grad[:, 0])


def solution(mesh):
    in_specs = (
        P(),
        P(None, "tgt", None),
        P(None, None, ("src", "tgt")),
        P(None, ("src", "tgt")),
        P(None, None, ("src", "tgt")),
        P("src", "tgt", None),
        P(None, "tgt"),
        P("src", None),
    )
    out_specs = (P("src", "tgt", None), P(None, None, ("src", "tgt")), P(None, ("src", "tgt")))
    body = functools.partial(shards, mesh.shape["src"], mesh.shape["tgt"])
    return jax.shard_map(body, mesh=mesh, in_specs=in_specs, out_specs=out_specs, check_vma=False)
```

time: 755 us -> 516 us (0.68)
  waiting for transfers between devices: 375 us -> 99.5 us
  matrix products: 215 us -> 0 us
  Pallas kernels: 0 us -> 171 us
  starting transfers between devices: 0.3 us -> 164 us
  loops' own time: 78 us -> 0 us
  between operations: 13.8 us -> 1.52 us
    dot_general x32 -> x0, matrix products: 215 us -> none  [the longest x10 97.1 us: step_partial(): lax.dot_general(error_rows, weight, (((0,), (0,)), ((), ())), preferred_e...]
    pallas_call x0 -> x14, Pallas kernels: none -> 171 us  [the longest x4 63.1 us: recon(): pl.pallas_call(functools.partial(recon_kernel, pairs, len(pieces), layers...]
    reduce_scatter x1 -> x0, waiting for transfers between devices: 168 us -> none  [shards(): lax.psum_scatter(grad_sum.astype(jnp.bfloat16), 'tgt', scatter_dimension=...]
    ppermute x0 -> x64, starting transfers between devices: none -> 164 us  [the longest x24 74.8 us: swap_cores(): return lax.ppermute(value, 'tgt', [(i, i ^ 1) for i in range(devices)])]
    all_gather x1 -> x0, waiting for transfers between devices: 154 us -> none  [shards(): blocks = lax.all_gather(latent, 'tgt', axis=2, tiled=True)]
    ppermute x0 -> x64, waiting for transfers between devices: none -> 99.5 us  [the longest x24 91.1 us: hop(): return lax.ppermute(value, 'tgt', perm)]
    another operation x2 -> x0, loops' own time: 78 us -> none  [the longest x1 39.1 us: shards(): lax.scan(add_recon, recon_zero, (dec_weight, source_ids, target_ids))[0]]
    psum x1 -> x0, waiting for transfers between devices: 52.6 us -> none  [shards(): lax.psum(recon_sum.astype(jnp.bfloat16), 'src').astype(jnp.float32)]
  transfers between devices with their start and end apart: 3 -> 64, of which waited for: 3 -> 19; matrix products, arithmetic and copies ran while one was open for 0% -> 9% of each run, Pallas kernels for 0% -> 31%
where the time goes in v1:
time: 516 us; the launch traced here: 510 us
  Pallas kernels  171 us (33%)
  starting transfers between devices  164 us (32%)
  waiting for transfers between devices  99.5 us (19%)
  local copies, waits for them, and re-layouts  43.6 us (8%)
  other arithmetic  29.7 us (6%)
    ppermute x24, waiting for transfers between devices, hop(): return lax.ppermute(value, 'tgt', perm)  91.1 us
    ppermute x24, starting transfers between devices, swap_cores(): return lax.ppermute(value, 'tgt', [(i, i ^ 1) for i in range(devices)])  74.8 us
    ppermute x24, starting transfers between devices, hop(): return lax.ppermute(value, 'tgt', perm)  70.1 us
    pallas_call x4, Pallas kernels, recon(): pl.pallas_call(functools.partial(recon_kernel, pairs, len(pieces), layers...  63.1 us
    pallas_call x4, Pallas kernels, grad(): pl.pallas_call(functools.partial(grad_kernel, pairs, layers, len(extra)),...  54.4 us
    unnamed x88, local copies, waits for them, and re-layouts  38 us
    pallas_call x1, Pallas kernels, decoder_grad(): pl.pallas_call(dec_grad_kernel, grid_spec=pltpu.PrefetchScalarGridSpec(nu...  26.1 us
    convert_element_type x28, other arithmetic, add(): return total.astype(BF16)  23.7 us
  transfers between devices with their start and end apart: 64, of which 19 were waited for; matrix products, arithmetic and copies ran while one was open for 9% of the time, Pallas kernels for 31%

profile of v1, /device:TPU:0, one launch (start us, length us, event | category | flops | bytes accessed | tf_op | source)
XLA Modules:
  0.0 509.6 jit_solution(5722298785723740951)
XLA Ops:
  1.3 3.7 copy-done
  7.2 5.2 %encode.7 = bf16[4,128,512]{2,1,0:T(8,128)(2,1)S(1)} custom-call(bf16[4,512,2304]{2,1,0:T(8,128)(2,1)S(1)} %copy-done, bf16[4,2304,512]{2,1,0:T(8,128)(2,1)} %weight_ref.7, f32[4,1,512]{2,1,0:T(1,128)S(1)} %broadcast_in_dim.26.bias_ref, s32[4,512,512]{2,1,0:T(8,128)S(1)} %copy-done.1), custom_call_target="tpu_custom_call" | custom-call | tf_op jit(solution)/shard_map/encode/pallas_call | solution.py:76
  12.9 5.2 %encode.6 = bf16[4,128,512]{2,1,0:T(8,128)(2,1)S(1)} custom-call(bf16[4,512,2304]{2,1,0:T(8,128)(2,1)S(1)} %copy-done, bf16[4,2304,512]{2,1,0:T(8,128)(2,1)} %weight_ref.7, f32[4,1,512]{2,1,0:T(1,128)S(1)} %broadcast_in_dim.26.bias_ref, s32[4,512,512]{2,1,0:T(8,128)S(1)} %copy-done.1), custom_call_target="tpu_custom_call" | custom-call | tf_op jit(solution)/shard_map/encode/pallas_call | solution.py:76
  18.2 5.2 %encode.5 = bf16[4,128,512]{2,1,0:T(8,128)(2,1)S(1)} custom-call(bf16[4,512,2304]{2,1,0:T(8,128)(2,1)S(1)} %copy-done, bf16[4,2304,512]{2,1,0:T(8,128)(2,1)} %weight_ref.7, f32[4,1,512]{2,1,0:T(1,128)S(1)} %broadcast_in_dim.26.bias_ref, s32[4,512,512]{2,1,0:T(8,128)S(1)} %copy-done.1), custom_call_target="tpu_custom_call" | custom-call | tf_op jit(solution)/shard_map/encode/pallas_call | solution.py:76
  23.9 5.2 %encode.4 = bf16[4,128,512]{2,1,0:T(8,128)(2,1)S(1)} custom-call(bf16[4,512,2304]{2,1,0:T(8,128)(2,1)S(1)} %copy-done, bf16[4,2304,512]{2,1,0:T(8,128)(2,1)} %weight_ref.7, f32[4,1,512]{2,1,0:T(1,128)S(1)} %broadcast_in_dim.26.bias_ref, s32[4,512,512]{2,1,0:T(8,128)S(1)} %copy-done.1), custom_call_target="tpu_custom_call" | custom-call | tf_op jit(solution)/shard_map/encode/pallas_call | solution.py:76
  29.4 5.1 %collective-permute-start.22 = (bf16[2,4,128,512]{3,2,1,0:T(8,128)(2,1)S(1)}, bf16[2,4,128,512]{3,2,1,0:T(8,128)(2,1)S(1)}, u32[]{:S(2)}, u32[]{:S(2)}) collective-permute-start(bf16[2,4,128,512]{3,2,1,0:T(8,128)(2,1)S(1)} %pad_maximum_fusion.3.refs_10_), channel_id=1, source_target_pairs={{0,2},{7,5},{2,4},{5,3},{4,6},{3,1},{8,10},{15,13},{10,12},{13,11}... | collective-permute-start | bytes 3145736 | tf_op jit(solution)/shard_map/ppermute | solution.py:358
  34.7 3.5 collective-permute-start.15
  38.3 3.5 collective-permute-start.8
  48.7 9.3 %collective-permute-done.15.refs_11_ = bf16[2,4,128,512]{3,2,1,0:T(8,128)(2,1)S(1)} collective-permute-done((bf16[2,4,128,512]{3,2,1,0:T(8,128)(2,1)S(1)}, bf16[2,4,128,512]{3,2,1,0:T(8,128)(2,1)S(1)}, u32[]{:S(2)}, u32[]{:S(2)}) %collective-permute-start.15) | collective-permute-done | bytes 1048608 | tf_op jit(solution)/shard_map/ppermute | solution.py:358
  59.7 9.6 %collective-permute-done.8.refs_11_ = bf16[2,4,128,512]{3,2,1,0:T(8,128)(2,1)S(1)} collective-permute-done((bf16[2,4,128,512]{3,2,1,0:T(8,128)(2,1)S(1)}, bf16[2,4,128,512]{3,2,1,0:T(8,128)(2,1)S(1)}, u32[]{:S(2)}, u32[]{:S(2)}) %collective-permute-start.8) | collective-permute-done | bytes 1048608 | tf_op jit(solution)/shard_map/ppermute | solution.py:358
  70.3 10.2 %collective-permute-done.1.refs_11_ = bf16[2,4,128,512]{3,2,1,0:T(8,128)(2,1)S(1)} collective-permute-done((bf16[2,4,128,512]{3,2,1,0:T(8,128)(2,1)S(1)}, bf16[2,4,128,512]{3,2,1,0:T(8,128)(2,1)S(1)}, u32[]{:S(2)}, u32[]{:S(2)}) %collective-permute-start.1) | collective-permute-done | bytes 1048608 | tf_op jit(solution)/shard_map/ppermute | solution.py:358
  82.1 9.2 %collective-permute-start.11 = (bf16[2,4,128,512]{3,2,1,0:T(8,128)(2,1)S(1)}, bf16[2,4,128,512]{3,2,1,0:T(8,128)(2,1)S(1)}, u32[]{:S(2)}, u32[]{:S(2)}) collective-permute-start(bf16[2,4,128,512]{3,2,1,0:T(8,128)(2,1)S(1)} %collective-permute-done.8.refs_11_), channel_id=1, source_target_pairs={{0,1},{1,0},{2,3},{3,2},{4,5},{5,4},{6,7},{7,6},{8,9},{9,8},{10,11... | collective-permute-start | bytes 3145736 | tf_op jit(solution)/shard_map/ppermute | solution.py:348
  97.6 7.4 %collective-permute-start.26 = (bf16[2,4,128,512]{3,2,1,0:T(8,128)(2,1)S(1)}, bf16[2,4,128,512]{3,2,1,0:T(8,128)(2,1)S(1)}, u32[]{:S(2)}, u32[]{:S(2)}) collective-permute-start(bf16[2,4,128,512]{3,2,1,0:T(8,128)(2,1)S(1)} %collective-permute-done.23.refs_12_), channel_id=1, source_target_pairs={{0,1},{1,0},{2,3},{3,2},{4,5},{5,4},{6,7},{7,6},{8,9},{9,8},{10,11... | collective-permute-start | bytes 3145736 | tf_op jit(solution)/shard_map/ppermute | solution.py:348
  108.6 7.6 %collective-permute-start.19 = (bf16[2,4,128,512]{3,2,1,0:T(8,128)(2,1)}, bf16[2,4,128,512]{3,2,1,0:T(8,128)(2,1)}, u32[]{:S(2)}, u32[]{:S(2)}) collective-permute-start(bf16[2,4,128,512]{3,2,1,0:T(8,128)(2,1)} %collective-permute-done.16.refs_12_), channel_id=1, source_target_pairs={{0,1},{1,0},{2,3},{3,2},{4,5},{5,4},{6,7},{7,6},{8,9},{9,8},{10,11... | collective-permute-start | bytes 3145736 | tf_op jit(solution)/shard_map/ppermute | solution.py:348
  120.5 18.4 %collective-permute-start.27 = (bf16[2,4,128,512]{3,2,1,0:T(8,128)(2,1)}, bf16[2,4,128,512]{3,2,1,0:T(8,128)(2,1)}, u32[]{:S(2)}, u32[]{:S(2)}) collective-permute-start(bf16[2,4,128,512]{3,2,1,0:T(8,128)(2,1)} %collective-permute-done.24.refs_13_), channel_id=1, source_target_pairs={{0,1},{1,0},{2,3},{3,2},{4,5},{5,4},{6,7},{7,6},{8,9},{9,8},{10,11... | collective-permute-start | bytes 3145736 | tf_op jit(solution)/shard_map/ppermute | solution.py:348
  138.9 8.8 %collective-permute-start.20 = (bf16[2,4,128,512]{3,2,1,0:T(8,128)(2,1)}, bf16[2,4,128,512]{3,2,1,0:T(8,128)(2,1)}, u32[]{:S(2)}, u32[]{:S(2)}) collective-permute-start(bf16[2,4,128,512]{3,2,1,0:T(8,128)(2,1)} %collective-permute-done.17.refs_13_), channel_id=1, source_target_pairs={{0,1},{1,0},{2,3},{3,2},{4,5},{5,4},{6,7},{7,6},{8,9},{9,8},{10,11... | collective-permute-start | bytes 3145736 | tf_op jit(solution)/shard_map/ppermute | solution.py:348
  148.3 10.5 %collective-permute-start.13 = (bf16[2,4,128,512]{3,2,1,0:T(8,128)(2,1)}, bf16[2,4,128,512]{3,2,1,0:T(8,128)(2,1)}, u32[]{:S(2)}, u32[]{:S(2)}) collective-permute-start(bf16[2,4,128,512]{3,2,1,0:T(8,128)(2,1)} %collective-permute-done.10.refs_13_), channel_id=1, source_target_pairs={{0,1},{1,0},{2,3},{3,2},{4,5},{5,4},{6,7},{7,6},{8,9},{9,8},{10,11... | collective-permute-start | bytes 3145736 | tf_op jit(solution)/shard_map/ppermute | solution.py:348
  160.0 10.1 %collective-permute-start.4 = (bf16[2,4,128,512]{3,2,1,0:T(8,128)(2,1)}, bf16[2,4,128,512]{3,2,1,0:T(8,128)(2,1)}, u32[]{:S(2)}, u32[]{:S(2)}) collective-permute-start(bf16[2,4,128,512]{3,2,1,0:T(8,128)(2,1)} %copy-done.13), channel_id=1, source_target_pairs={{0,1},{1,0},{2,3},{3,2},{4,5},{5,4},{6,7},{7,6},{8,9},{9,8},{10,11... | collective-permute-start | bytes 3145736 | tf_op jit(solution)/shard_map/ppermute | solution.py:348
  176.9 15.4 %recon.4 = (bf16[2,288,128]{2,1,0:T(8,128)(2,1)S(1)}, bf16[2,288,128]{2,1,0:T(8,128)(2,1)S(1)}, bf16[8,4,512,512]{3,2,1,0:T(8,128)(2,1)}) custom-call(s32[24]{0:T(128)S(1)} %pad_add_fusion.1.meta, bf16[10,288,4096]{2,1,0:T(8,128)(2,1)} %refs_9_.15, bf16[10,288,4096]{2,1,0:T(8,128)(2,1)} %refs_9_.15, bf16[10,288,4096]{2,1,0:T(8,128)(2,1)} %refs_9_.15, ...), custom_call_target="tpu_custom_call" | custom-call | flops 3019898880 | bytes 23592960 | tf_op jit(solution)/shard_map/recon/pallas_call | solution.py:158
  192.3 15.6 %recon.5 = (bf16[2,288,128]{2,1,0:T(8,128)(2,1)S(1)}, bf16[2,288,128]{2,1,0:T(8,128)(2,1)S(1)}, bf16[8,4,512,512]{3,2,1,0:T(8,128)(2,1)}) custom-call(s32[24]{0:T(128)S(1)} %pad_add_fusion.1.meta, bf16[10,288,4096]{2,1,0:T(8,128)(2,1)} %refs_9_.15, bf16[10,288,4096]{2,1,0:T(8,128)(2,1)} %refs_9_.15, ...), custom_call_target="tpu_custom_call", output_to_operand_aliasing={{2}: (18, {})} | custom-call | flops 3019898880 | bytes 23592960 | tf_op jit(solution)/shard_map/recon/pallas_call | solution.py:158
  211.2 15.6 %recon.6 = (bf16[2,288,128]{2,1,0:T(8,128)(2,1)S(1)}, bf16[2,288,128]{2,1,0:T(8,128)(2,1)S(1)}, bf16[8,4,512,512]{3,2,1,0:T(8,128)(2,1)}) custom-call(s32[24]{0:T(128)S(1)} %pad_add_fusion.1.meta, bf16[10,288,4096]{2,1,0:T(8,128)(2,1)} %refs_9_.15, bf16[10,288,4096]{2,1,0:T(8,128)(2,1)} %refs_9_.15, ...), custom_call_target="tpu_custom_call", output_to_operand_aliasing={{2}: (18, {})} | custom-call | flops 3019898880 | bytes 23592960 | tf_op jit(solution)/shard_map/recon/pallas_call | solution.py:158
  229.5 16.5 %recon.7 = (bf16[2,288,128]{2,1,0:T(8,128)(2,1)}, bf16[2,288,128]{2,1,0:T(8,128)(2,1)}, bf16[8,4,512,512]{3,2,1,0:T(8,128)(2,1)}) custom-call(s32[24]{0:T(128)S(1)} %pad_add_fusion.1.meta, bf16[10,288,4096]{2,1,0:T(8,128)(2,1)} %refs_9_.15, bf16[10,288,4096]{2,1,0:T(8,128)(2,1)} %refs_9_.15, ...), custom_call_target="tpu_custom_call", output_to_operand_aliasing={{2}: (18, {})} | custom-call | flops 3019898880 | bytes 23592960 | tf_op jit(solution)/shard_map/recon/pallas_call | solution.py:158
  254.4 3.9 collective-permute-done.43
  261.1 13.2 %latent_grad.4 = (bf16[7,4,128,512]{3,2,1,0:T(8,128)(2,1)S(1)}, bf16[7,4,128,512]{3,2,1,0:T(8,128)(2,1)S(1)}, bf16[4,288,512]{2,1,0:T(8,128)(2,1)S(1)}) custom-call(s32[35]{0:T(128)S(1)} %pad_add_fusion.meta, bf16[10,288,4096]{2,1,0:T(8,128)(2,1)} %refs_9_.15, bf16[10,288,4096]{2,1,0:T(8,128)(2,1)} %refs_9_.15, bf16[10,288,4096]{2,1,0:T(8,128)(2,1)} %refs_9_.15, ...), custom_call_target="tpu_custom_call" | custom-call | flops 3019898880 | bytes 23592960 | tf_op jit(solution)/shard_map/latent_grad/pallas_call | solution.py:251
  275.3 13.9 %latent_grad.5 = (bf16[7,4,128,512]{3,2,1,0:T(8,128)(2,1)}, bf16[7,4,128,512]{3,2,1,0:T(8,128)(2,1)S(1)}, bf16[4,288,512]{2,1,0:T(8,128)(2,1)S(1)}) custom-call(s32[35]{0:T(128)S(1)} %pad_add_fusion.meta, bf16[10,288,4096]{2,1,0:T(8,128)(2,1)} %refs_9_.15, bf16[10,288,4096]{2,1,0:T(8,128)(2,1)} %refs_9_.15, ...), custom_call_target="tpu_custom_call", output_to_operand_aliasing={{2}: (15, {})} | custom-call | flops 3019898880 | bytes 23592960 | tf_op jit(solution)/shard_map/latent_grad/pallas_call | solution.py:251
  291.2 13.9 %latent_grad.6 = (bf16[7,4,128,512]{3,2,1,0:T(8,128)(2,1)}, bf16[7,4,128,512]{3,2,1,0:T(8,128)(2,1)S(1)}, bf16[4,288,512]{2,1,0:T(8,128)(2,1)S(1)}) custom-call(s32[35]{0:T(128)S(1)} %pad_add_fusion.meta, bf16[10,288,4096]{2,1,0:T(8,128)(2,1)} %refs_9_.15, bf16[10,288,4096]{2,1,0:T(8,128)(2,1)} %refs_9_.15, ...), custom_call_target="tpu_custom_call", output_to_operand_aliasing={{2}: (15, {})} | custom-call | flops 3019898880 | bytes 23592960 | tf_op jit(solution)/shard_map/latent_grad/pallas_call | solution.py:251
  314.0 13.4 %latent_grad.7 = (bf16[7,4,128,512]{3,2,1,0:T(8,128)(2,1)S(1)}, bf16[7,4,128,512]{3,2,1,0:T(8,128)(2,1)S(1)}, bf16[4,288,512]{2,1,0:T(8,128)(2,1)S(1)}) custom-call(s32[35]{0:T(128)S(1)} %pad_add_fusion.meta, bf16[10,288,4096]{2,1,0:T(8,128)(2,1)} %refs_9_.15, bf16[10,288,4096]{2,1,0:T(8,128)(2,1)} %refs_9_.15, ...), custom_call_target="tpu_custom_call", output_to_operand_aliasing={{2}: (15, {})} | custom-call | flops 3019898880 | bytes 23592960 | tf_op jit(solution)/shard_map/latent_grad/pallas_call | solution.py:251
  340.9 4.7 collective-permute-done.55
  347.3 4.5 collective-permute-start.56
  351.7 5.1 %collective-permute-done.45 = bf16[2,4,128,512]{3,2,1,0:T(8,128)(2,1)S(1)} collective-permute-done((bf16[2,4,128,512]{3,2,1,0:T(8,128)(2,1)S(1)}, bf16[2,4,128,512]{3,2,1,0:T(8,128)(2,1)S(1)}, u32[]{:S(2)}, u32[]{:S(2)}) %collective-permute-start.45) | collective-permute-done | bytes 1048608 | tf_op jit(solution)/shard_map/ppermute | solution.py:358
  358.5 4.5 collective-permute-start.46
  363.0 5.1 collective-permute-done.50
  369.7 4.5 collective-permute-start.51
  374.2 5.1 %collective-permute-done.60 = bf16[2,4,128,512]{3,2,1,0:T(8,128)(2,1)S(1)} collective-permute-done((bf16[2,4,128,512]{3,2,1,0:T(8,128)(2,1)S(1)}, bf16[2,4,128,512]{3,2,1,0:T(8,128)(2,1)S(1)}, u32[]{:S(2)}, u32[]{:S(2)}) %collective-permute-start.60) | collective-permute-done | bytes 1048608 | tf_op jit(solution)/shard_map/ppermute | solution.py:358
  379.8 4.5 collective-permute-start.61
  384.2 6.3 %collective-permute-done.56 = bf16[2,4,128,512]{3,2,1,0:T(8,128)(2,1)S(1)} collective-permute-done((bf16[2,4,128,512]{3,2,1,0:T(8,128)(2,1)S(1)}, bf16[2,4,128,512]{3,2,1,0:T(8,128)(2,1)S(1)}, u32[]{:S(2)}, u32[]{:S(2)}) %collective-permute-start.56) | collective-permute-done | bytes 1048608 | tf_op jit(solution)/shard_map/ppermute | solution.py:358
  393.2 4.4 collective-permute-start.57
  397.6 4.1 collective-permute-done.46
  404.4 5.4 %collective-permute-start.47 = (bf16[2,4,128,512]{3,2,1,0:T(8,128)(2,1)}, bf16[2,4,128,512]{3,2,1,0:T(8,128)(2,1)}, u32[]{:S(2)}, u32[]{:S(2)}) collective-permute-start(bf16[2,4,128,512]{3,2,1,0:T(8,128)(2,1)} %add_convert_fusion.9), channel_id=1, source_target_pairs={{0,2},{7,5},{2,4},{5,3},{4,6},{3,1},{8,10},{15,13},{10,12},{13,11}... | collective-permute-start | bytes 3145736 | tf_op jit(solution)/shard_map/ppermute | solution.py:358
  409.8 3.2 collective-permute-done.51
  415.7 5.3 %collective-permute-start.52 = (bf16[2,4,128,512]{3,2,1,0:T(8,128)(2,1)}, bf16[2,4,128,512]{3,2,1,0:T(8,128)(2,1)}, u32[]{:S(2)}, u32[]{:S(2)}) collective-permute-start(bf16[2,4,128,512]{3,2,1,0:T(8,128)(2,1)} %add_convert_fusion.6), channel_id=1, source_target_pairs={{0,2},{7,5},{2,4},{5,3},{4,6},{3,1},{8,10},{15,13},{10,12},{13,11}... | collective-permute-start | bytes 3145736 | tf_op jit(solution)/shard_map/ppermute | solution.py:358
  425.7 5.4 %collective-permute-start.62 = (bf16[2,4,128,512]{3,2,1,0:T(8,128)(2,1)}, bf16[2,4,128,512]{3,2,1,0:T(8,128)(2,1)}, u32[]{:S(2)}, u32[]{:S(2)}) collective-permute-start(bf16[2,4,128,512]{3,2,1,0:T(8,128)(2,1)} %add_convert_fusion), channel_id=1, source_target_pairs={{0,2},{7,5},{2,4},{5,3},{4,6},{3,1},{8,10},{15,13},{10,12},{13,11}... | collective-permute-start | bytes 3145736 | tf_op jit(solution)/shard_map/ppermute | solution.py:358
  431.1 12.6 %copy.34 = bf16[4,512,2304]{1,2,0:T(8,128)(2,1)} copy(bf16[4,512,2304]{2,1,0:T(8,128)(2,1)} %res_ref.7) | data formatting | bytes 18874368 | tf_op args[0]
  448.0 10.1 %collective-permute-done.52 = bf16[2,4,128,512]{3,2,1,0:T(8,128)(2,1)} collective-permute-done((bf16[2,4,128,512]{3,2,1,0:T(8,128)(2,1)}, bf16[2,4,128,512]{3,2,1,0:T(8,128)(2,1)}, u32[]{:S(2)}, u32[]{:S(2)}) %collective-permute-start.52) | collective-permute-done | bytes 1048608 | tf_op jit(solution)/shard_map/ppermute | solution.py:358
  459.2 10.1 %collective-permute-done.62 = bf16[2,4,128,512]{3,2,1,0:T(8,128)(2,1)} collective-permute-done((bf16[2,4,128,512]{3,2,1,0:T(8,128)(2,1)}, bf16[2,4,128,512]{3,2,1,0:T(8,128)(2,1)}, u32[]{:S(2)}, u32[]{:S(2)}) %collective-permute-start.62) | collective-permute-done | bytes 1048608 | tf_op jit(solution)/shard_map/ppermute | solution.py:358
  470.5 26.1 %dec_grad.1 = bf16[10,288,4096]{2,1,0:T(8,128)(2,1)} custom-call(s32[10]{0:T(128)S(1)} %copy-done.32, s32[10]{0:T(128)S(1)} %copy-done.34, s32[10]{0:T(128)S(1)} %copy-done.35, bf16[4,288,512]{2,1,0:T(8,128)(2,1)S(1)} %get-tuple-element.43.error_ref, bf16[8,4,512,512]{3,2,1,0:T(8,128)(2,1)} %get-tuple-element.44.lat_ref), custom_call_target="tpu_custom_call" | custom-call | flops 12079595520 | bytes 23592960 | tf_op jit(solution)/shard_map/dec_grad/pallas_call | solution.py:297
  498.3 3.6 fusion.1
  502.0 7.0 %enc_grad.1 = (bf16[4,2304,512]{2,1,0:T(8,128)(2,1)}, f32[4,1,512]{2,1,0:T(1,128)S(1)}) custom-call(bf16[4,2304,512]{2,1,0:T(8,128)(2,1)S(1)} %bitcast.52, bf16[4,128,512]{2,1,0:T(8,128)(2,1)S(1)} %get-tuple-element.57.refs_1_, bf16[4,128,512]{2,1,0:T(8,128)(2,1)S(1)} %get-tuple-element.56.refs_2_, bf16[4,128,512]{2,1,0:T(8,128)(2,1)S(1)} %fusion.3.refs_3_, ...), custom_call_target="tpu_custom_call" | custom-call | tf_op jit(solution)/shard_map/enc_grad/pallas_call | solution.py:329
  (229 shorter events, 107.6 us)
Async XLA Ops:
  34.7 23.4 %collective-permute-start.15 = (bf16[2,4,128,512]{3,2,1,0:T(8,128)(2,1)S(1)}, bf16[2,4,128,512]{3,2,1,0:T(8,128)(2,1)S(1)}, u32[]{:S(2)}, u32[]{:S(2)}) collective-permute-start(bf16[2,4,128,512]{3,2,1,0:T(8,128)(2,1)S(1)} %pad_maximum_fusion.2.refs_10_), channel_id=1, source_target_pairs={{0,2},{7,5},{2,4},{5,3},{4,6},{3,1},{8,10},{15,13},{10,12},{13,11}... | collective-permute-start | bytes 3145736 | tf_op jit(solution)/shard_map/ppermute | solution.py:358
  38.3 31.0 %collective-permute-start.8 = (bf16[2,4,128,512]{3,2,1,0:T(8,128)(2,1)S(1)}, bf16[2,4,128,512]{3,2,1,0:T(8,128)(2,1)S(1)}, u32[]{:S(2)}, u32[]{:S(2)}) collective-permute-start(bf16[2,4,128,512]{3,2,1,0:T(8,128)(2,1)S(1)} %pad_maximum_fusion.1.refs_10_), channel_id=1, source_target_pairs={{0,2},{7,5},{2,4},{5,3},{4,6},{3,1},{8,10},{15,13},{10,12},{13,11}... | collective-permute-start | bytes 3145736 | tf_op jit(solution)/shard_map/ppermute | solution.py:358
  41.9 38.6 %collective-permute-start.1 = (bf16[2,4,128,512]{3,2,1,0:T(8,128)(2,1)S(1)}, bf16[2,4,128,512]{3,2,1,0:T(8,128)(2,1)S(1)}, u32[]{:S(2)}, u32[]{:S(2)}) collective-permute-start(bf16[2,4,128,512]{3,2,1,0:T(8,128)(2,1)S(1)} %pad_maximum_fusion.refs_10_), channel_id=1, source_target_pairs={{0,2},{7,5},{2,4},{5,3},{4,6},{3,1},{8,10},{15,13},{10,12},{13,11}... | collective-permute-start | bytes 3145736 | tf_op jit(solution)/shard_map/ppermute | solution.py:358
  46.8 35.3 %collective-permute-start.23 = (bf16[2,4,128,512]{3,2,1,0:T(8,128)(2,1)S(1)}, bf16[2,4,128,512]{3,2,1,0:T(8,128)(2,1)S(1)}, u32[]{:S(2)}, u32[]{:S(2)}) collective-permute-start(bf16[2,4,128,512]{3,2,1,0:T(8,128)(2,1)S(1)} %collective-permute-done.22.refs_11_), channel_id=1, source_target_pairs={{2,4},{5,3},{4,6},{3,1},{10,12},{13,11},{12,14},{11,9},{18,20},{21... | collective-permute-start | bytes 3145736 | tf_op jit(solution)/shard_map/ppermute | solution.py:358
  47.5 44.8 %collective-permute-start.25 = (bf16[2,4,128,512]{3,2,1,0:T(8,128)(2,1)S(1)}, bf16[2,4,128,512]{3,2,1,0:T(8,128)(2,1)S(1)}, u32[]{:S(2)}, u32[]{:S(2)}) collective-permute-start(bf16[2,4,128,512]{3,2,1,0:T(8,128)(2,1)S(1)} %collective-permute-done.22.refs_11_), channel_id=1, source_target_pairs={{0,1},{1,0},{2,3},{3,2},{4,5},{5,4},{6,7},{7,6},{8,9},{9,8},{10,11... | collective-permute-start | bytes 3145736 | tf_op jit(solution)/shard_map/ppermute | solution.py:348
  58.0 37.0 %collective-permute-start.16 = (bf16[2,4,128,512]{3,2,1,0:T(8,128)(2,1)S(1)}, bf16[2,4,128,512]{3,2,1,0:T(8,128)(2,1)}, u32[]{:S(2)}, u32[]{:S(2)}) collective-permute-start(bf16[2,4,128,512]{3,2,1,0:T(8,128)(2,1)S(1)} %collective-permute-done.15.refs_11_), channel_id=1, source_target_pairs={{2,4},{5,3},{4,6},{3,1},{10,12},{13,11},{12,14},{11,9},{18,20},{21... | collective-permute-start | bytes 3145736 | tf_op jit(solution)/shard_map/ppermute | solution.py:358
  69.3 27.4 %collective-permute-start.18 = (bf16[2,4,128,512]{3,2,1,0:T(8,128)(2,1)S(1)}, bf16[2,4,128,512]{3,2,1,0:T(8,128)(2,1)S(1)}, u32[]{:S(2)}, u32[]{:S(2)}) collective-permute-start(bf16[2,4,128,512]{3,2,1,0:T(8,128)(2,1)S(1)} %collective-permute-done.15.refs_11_), channel_id=1, source_target_pairs={{0,1},{1,0},{2,3},{3,2},{4,5},{5,4},{6,7},{7,6},{8,9},{9,8},{10,11... | collective-permute-start | bytes 3145736 | tf_op jit(solution)/shard_map/ppermute | solution.py:348
  80.5 25.5 %collective-permute-start.9 = (bf16[2,4,128,512]{3,2,1,0:T(8,128)(2,1)S(1)}, bf16[2,4,128,512]{3,2,1,0:T(8,128)(2,1)}, u32[]{:S(2)}, u32[]{:S(2)}) collective-permute-start(bf16[2,4,128,512]{3,2,1,0:T(8,128)(2,1)S(1)} %collective-permute-done.8.refs_11_), channel_id=1, source_target_pairs={{2,4},{5,3},{4,6},{3,1},{10,12},{13,11},{12,14},{11,9},{18,20},{21... | collective-permute-start | bytes 3145736 | tf_op jit(solution)/shard_map/ppermute | solution.py:358
  82.1 25.5 %collective-permute-start.11 = (bf16[2,4,128,512]{3,2,1,0:T(8,128)(2,1)S(1)}, bf16[2,4,128,512]{3,2,1,0:T(8,128)(2,1)S(1)}, u32[]{:S(2)}, u32[]{:S(2)}) collective-permute-start(bf16[2,4,128,512]{3,2,1,0:T(8,128)(2,1)S(1)} %collective-permute-done.8.refs_11_), channel_id=1, source_target_pairs={{0,1},{1,0},{2,3},{3,2},{4,5},{5,4},{6,7},{7,6},{8,9},{9,8},{10,11... | collective-permute-start | bytes 3145736 | tf_op jit(solution)/shard_map/ppermute | solution.py:348
  93.3 22.9 %collective-permute-start.2 = (bf16[2,4,128,512]{3,2,1,0:T(8,128)(2,1)S(1)}, bf16[2,4,128,512]{3,2,1,0:T(8,128)(2,1)}, u32[]{:S(2)}, u32[]{:S(2)}) collective-permute-start(bf16[2,4,128,512]{3,2,1,0:T(8,128)(2,1)S(1)} %collective-permute-done.1.refs_11_), channel_id=1, source_target_pairs={{2,4},{5,3},{4,6},{3,1},{10,12},{13,11},{12,14},{11,9},{18,20},{21... | collective-permute-start | bytes 3145736 | tf_op jit(solution)/shard_map/ppermute | solution.py:358
  95.0 22.8 %collective-permute-start.24 = (bf16[2,4,128,512]{3,2,1,0:T(8,128)(2,1)S(1)}, bf16[2,4,128,512]{3,2,1,0:T(8,128)(2,1)}, u32[]{:S(2)}, u32[]{:S(2)}) collective-permute-start(bf16[2,4,128,512]{3,2,1,0:T(8,128)(2,1)S(1)} %collective-permute-done.23.refs_12_), channel_id=1, source_target_pairs={{4,6},{3,1},{12,14},{11,9},{20,22},{19,17},{28,30},{27,25}} | collective-permute-start | bytes 3145736 | tf_op jit(solution)/shard_map/ppermute | solution.py:358
  97.6 21.9 %collective-permute-start.26 = (bf16[2,4,128,512]{3,2,1,0:T(8,128)(2,1)S(1)}, bf16[2,4,128,512]{3,2,1,0:T(8,128)(2,1)S(1)}, u32[]{:S(2)}, u32[]{:S(2)}) collective-permute-start(bf16[2,4,128,512]{3,2,1,0:T(8,128)(2,1)S(1)} %collective-permute-done.23.refs_12_), channel_id=1, source_target_pairs={{0,1},{1,0},{2,3},{3,2},{4,5},{5,4},{6,7},{7,6},{8,9},{9,8},{10,11... | collective-permute-start | bytes 3145736 | tf_op jit(solution)/shard_map/ppermute | solution.py:348
  106.0 32.9 %collective-permute-start.17 = (bf16[2,4,128,512]{3,2,1,0:T(8,128)(2,1)}, bf16[2,4,128,512]{3,2,1,0:T(8,128)(2,1)}, u32[]{:S(2)}, u32[]{:S(2)}) collective-permute-start(bf16[2,4,128,512]{3,2,1,0:T(8,128)(2,1)} %collective-permute-done.16.refs_12_), channel_id=1, source_target_pairs={{4,6},{3,1},{12,14},{11,9},{20,22},{19,17},{28,30},{27,25}} | collective-permute-start | bytes 3145736 | tf_op jit(solution)/shard_map/ppermute | solution.py:358
  108.6 39.7 %collective-permute-start.19 = (bf16[2,4,128,512]{3,2,1,0:T(8,128)(2,1)}, bf16[2,4,128,512]{3,2,1,0:T(8,128)(2,1)}, u32[]{:S(2)}, u32[]{:S(2)}) collective-permute-start(bf16[2,4,128,512]{3,2,1,0:T(8,128)(2,1)} %collective-permute-done.16.refs_12_), channel_id=1, source_target_pairs={{0,1},{1,0},{2,3},{3,2},{4,5},{5,4},{6,7},{7,6},{8,9},{9,8},{10,11... | collective-permute-start | bytes 3145736 | tf_op jit(solution)/shard_map/ppermute | solution.py:348
  116.2 32.1 %collective-permute-start.10 = (bf16[2,4,128,512]{3,2,1,0:T(8,128)(2,1)}, bf16[2,4,128,512]{3,2,1,0:T(8,128)(2,1)}, u32[]{:S(2)}, u32[]{:S(2)}) collective-permute-start(bf16[2,4,128,512]{3,2,1,0:T(8,128)(2,1)} %collective-permute-done.9.refs_12_), channel_id=1, source_target_pairs={{4,6},{3,1},{12,14},{11,9},{20,22},{19,17},{28,30},{27,25}} | collective-permute-start | bytes 3145736 | tf_op jit(solution)/shard_map/ppermute | solution.py:358
  117.8 42.2 %collective-permute-start.3 = (bf16[2,4,128,512]{3,2,1,0:T(8,128)(2,1)}, bf16[2,4,128,512]{3,2,1,0:T(8,128)(2,1)}, u32[]{:S(2)}, u32[]{:S(2)}) collective-permute-start(bf16[2,4,128,512]{3,2,1,0:T(8,128)(2,1)} %collective-permute-done.2.refs_12_), channel_id=1, source_target_pairs={{4,6},{3,1},{12,14},{11,9},{20,22},{19,17},{28,30},{27,25}} | collective-permute-start | bytes 3145736 | tf_op jit(solution)/shard_map/ppermute | solution.py:358
  120.5 49.6 %collective-permute-start.27 = (bf16[2,4,128,512]{3,2,1,0:T(8,128)(2,1)}, bf16[2,4,128,512]{3,2,1,0:T(8,128)(2,1)}, u32[]{:S(2)}, u32[]{:S(2)}) collective-permute-start(bf16[2,4,128,512]{3,2,1,0:T(8,128)(2,1)} %collective-permute-done.24.refs_13_), channel_id=1, source_target_pairs={{0,1},{1,0},{2,3},{3,2},{4,5},{5,4},{6,7},{7,6},{8,9},{9,8},{10,11... | collective-permute-start | bytes 3145736 | tf_op jit(solution)/shard_map/ppermute | solution.py:348
  138.9 31.2 %collective-permute-start.20 = (bf16[2,4,128,512]{3,2,1,0:T(8,128)(2,1)}, bf16[2,4,128,512]{3,2,1,0:T(8,128)(2,1)}, u32[]{:S(2)}, u32[]{:S(2)}) collective-permute-start(bf16[2,4,128,512]{3,2,1,0:T(8,128)(2,1)} %collective-permute-done.17.refs_13_), channel_id=1, source_target_pairs={{0,1},{1,0},{2,3},{3,2},{4,5},{5,4},{6,7},{7,6},{8,9},{9,8},{10,11... | collective-permute-start | bytes 3145736 | tf_op jit(solution)/shard_map/ppermute | solution.py:348
  148.3 59.6 %collective-permute-start.12 = (bf16[2,4,128,512]{3,2,1,0:T(8,128)(2,1)}, bf16[2,4,128,512]{3,2,1,0:T(8,128)(2,1)}, u32[]{:S(2)}, u32[]{:S(2)}) collective-permute-start(bf16[2,4,128,512]{3,2,1,0:T(8,128)(2,1)} %collective-permute-done.9.refs_12_), channel_id=1, source_target_pairs={{0,1},{1,0},{2,3},{3,2},{4,5},{5,4},{6,7},{7,6},{8,9},{9,8},{10,11... | collective-permute-start | bytes 3145736 | tf_op jit(solution)/shard_map/ppermute | solution.py:348
  148.3 61.4 %collective-permute-start.13 = (bf16[2,4,128,512]{3,2,1,0:T(8,128)(2,1)}, bf16[2,4,128,512]{3,2,1,0:T(8,128)(2,1)}, u32[]{:S(2)}, u32[]{:S(2)}) collective-permute-start(bf16[2,4,128,512]{3,2,1,0:T(8,128)(2,1)} %collective-permute-done.10.refs_13_), channel_id=1, source_target_pairs={{0,1},{1,0},{2,3},{3,2},{4,5},{5,4},{6,7},{7,6},{8,9},{9,8},{10,11... | collective-permute-start | bytes 3145736 | tf_op jit(solution)/shard_map/ppermute | solution.py:348
  160.0 66.8 %collective-permute-start.4 = (bf16[2,4,128,512]{3,2,1,0:T(8,128)(2,1)}, bf16[2,4,128,512]{3,2,1,0:T(8,128)(2,1)}, u32[]{:S(2)}, u32[]{:S(2)}) collective-permute-start(bf16[2,4,128,512]{3,2,1,0:T(8,128)(2,1)} %copy-done.13), channel_id=1, source_target_pairs={{0,1},{1,0},{2,3},{3,2},{4,5},{5,4},{6,7},{7,6},{8,9},{9,8},{10,11... | collective-permute-start | bytes 3145736 | tf_op jit(solution)/shard_map/ppermute | solution.py:348
  170.1 57.3 %collective-permute-start.5 = (bf16[2,4,128,512]{3,2,1,0:T(8,128)(2,1)}, bf16[2,4,128,512]{3,2,1,0:T(8,128)(2,1)}, u32[]{:S(2)}, u32[]{:S(2)}) collective-permute-start(bf16[2,4,128,512]{3,2,1,0:T(8,128)(2,1)} %collective-permute-done.2.refs_12_), channel_id=1, source_target_pairs={{0,1},{1,0},{2,3},{3,2},{4,5},{5,4},{6,7},{7,6},{8,9},{9,8},{10,11... | collective-permute-start | bytes 3145736 | tf_op jit(solution)/shard_map/ppermute | solution.py:348
  170.1 57.7 %collective-permute-start.6 = (bf16[2,4,128,512]{3,2,1,0:T(8,128)(2,1)}, bf16[2,4,128,512]{3,2,1,0:T(8,128)(2,1)}, u32[]{:S(2)}, u32[]{:S(2)}) collective-permute-start(bf16[2,4,128,512]{3,2,1,0:T(8,128)(2,1)} %collective-permute-done.3.refs_13_), channel_id=1, source_target_pairs={{0,1},{1,0},{2,3},{3,2},{4,5},{5,4},{6,7},{7,6},{8,9},{9,8},{10,11... | collective-permute-start | bytes 3145736 | tf_op jit(solution)/shard_map/ppermute | solution.py:348
  208.0 38.0 %collective-permute-start.42 = (bf16[2,288,128]{2,1,0:T(8,128)(2,1)S(1)}, bf16[2,288,128]{2,1,0:T(8,128)(2,1)S(1)}, u32[]{:S(2)}, u32[]{:S(2)}) collective-permute-start(bf16[2,288,128]{2,1,0:T(8,128)(2,1)S(1)} %get-tuple-element.39), channel_id=1, source_target_pairs={{0,16},{8,24},{16,0},{24,8},{1,17},{9,25},{17,1},{25,9},{2,18},{10... | collective-permute-start | bytes 442376 | tf_op jit(solution)/shard_map/ppermute | solution.py:372
  209.7 37.9 %collective-permute-start.40 = (bf16[2,288,128]{2,1,0:T(8,128)(2,1)S(1)}, bf16[2,288,128]{2,1,0:T(8,128)(2,1)S(1)}, u32[]{:S(2)}, u32[]{:S(2)}) collective-permute-start(bf16[2,288,128]{2,1,0:T(8,128)(2,1)S(1)} %get-tuple-element.38), channel_id=1, source_target_pairs={{0,8},{8,0},{16,24},{24,16},{1,9},{9,1},{17,25},{25,17},{2,10},{10... | collective-permute-start | bytes 442376 | tf_op jit(solution)/shard_map/ppermute | solution.py:372
  227.8 22.7 %collective-permute-start.34 = (bf16[2,288,128]{2,1,0:T(8,128)(2,1)S(1)}, bf16[2,288,128]{2,1,0:T(8,128)(2,1)S(1)}, u32[]{:S(2)}, u32[]{:S(2)}) collective-permute-start(bf16[2,288,128]{2,1,0:T(8,128)(2,1)S(1)} %get-tuple-element.35), channel_id=1, source_target_pairs={{0,16},{8,24},{16,0},{24,8},{1,17},{9,25},{17,1},{25,9},{2,18},{10... | collective-permute-start | bytes 442376 | tf_op jit(solution)/shard_map/ppermute | solution.py:372
  247.7 57.5 %collective-permute-start.30 = (bf16[2,288,128]{2,1,0:T(8,128)(2,1)}, bf16[2,288,128]{2,1,0:T(8,128)(2,1)}, u32[]{:S(2)}, u32[]{:S(2)}) collective-permute-start(bf16[2,288,128]{2,1,0:T(8,128)(2,1)} %get-tuple-element.33), channel_id=1, source_target_pairs={{0,16},{8,24},{16,0},{24,8},{1,17},{9,25},{17,1},{25,9},{2,18},{10... | collective-permute-start | bytes 442376 | tf_op jit(solution)/shard_map/ppermute | solution.py:372
  248.3 59.0 %collective-permute-start.28 = (bf16[2,288,128]{2,1,0:T(8,128)(2,1)}, bf16[2,288,128]{2,1,0:T(8,128)(2,1)}, u32[]{:S(2)}, u32[]{:S(2)}) collective-permute-start(bf16[2,288,128]{2,1,0:T(8,128)(2,1)} %get-tuple-element.32), channel_id=1, source_target_pairs={{0,8},{8,0},{16,24},{24,16},{1,9},{9,1},{17,25},{25,17},{2,10},{10... | collective-permute-start | bytes 442376 | tf_op jit(solution)/shard_map/ppermute | solution.py:372
  252.8 21.5 %collective-permute-start.39 = (bf16[2,288,128]{2,1,0:T(8,128)(2,1)S(1)}, bf16[2,288,128]{2,1,0:T(8,128)(2,1)S(1)}, u32[]{:S(2)}, u32[]{:S(2)}) collective-permute-start(bf16[2,288,128]{2,1,0:T(8,128)(2,1)S(1)} %add_convert_fusion.17), channel_id=1, source_target_pairs={{0,8},{8,0},{16,24},{24,16},{1,9},{9,1},{17,25},{25,17},{2,10},{10... | collective-permute-start | bytes 442376 | tf_op jit(solution)/shard_map/ppermute | solution.py:372
  259.7 31.4 %collective-permute-start.35 = (bf16[2,288,128]{2,1,0:T(8,128)(2,1)S(1)}, bf16[2,288,128]{2,1,0:T(8,128)(2,1)S(1)}, u32[]{:S(2)}, u32[]{:S(2)}) collective-permute-start(bf16[2,288,128]{2,1,0:T(8,128)(2,1)S(1)} %add_convert_fusion.21), channel_id=1, source_target_pairs={{0,8},{8,0},{16,24},{24,16},{1,9},{9,1},{17,25},{25,17},{2,10},{10... | collective-permute-start | bytes 442376 | tf_op jit(solution)/shard_map/ppermute | solution.py:372
  305.1 24.3 %collective-permute-start.54 = (bf16[7,4,128,512]{3,2,1,0:T(8,128)(2,1)}, bf16[7,4,128,512]{3,2,1,0:T(8,128)(2,1)}, u32[]{:S(2)}, u32[]{:S(2)}) collective-permute-start(bf16[7,4,128,512]{3,2,1,0:T(8,128)(2,1)} %get-tuple-element.50), channel_id=1, source_target_pairs={{0,1},{1,0},{2,3},{3,2},{4,5},{5,4},{6,7},{7,6},{8,9},{9,8},{10,11... | collective-permute-start | bytes 11010056 | tf_op jit(solution)/shard_map/ppermute | solution.py:348
  309.7 23.7 %collective-permute-start.44 = (bf16[7,4,128,512]{3,2,1,0:T(8,128)(2,1)S(1)}, bf16[7,4,128,512]{3,2,1,0:T(8,128)(2,1)}, u32[]{:S(2)}, u32[]{:S(2)}) collective-permute-start(bf16[7,4,128,512]{3,2,1,0:T(8,128)(2,1)S(1)} %get-tuple-element.46), channel_id=1, source_target_pairs={{0,1},{1,0},{2,3},{3,2},{4,5},{5,4},{6,7},{7,6},{8,9},{9,8},{10,11... | collective-permute-start | bytes 11010056 | tf_op jit(solution)/shard_map/ppermute | solution.py:348
  309.7 26.6 %collective-permute-start.49 = (bf16[7,4,128,512]{3,2,1,0:T(8,128)(2,1)}, bf16[7,4,128,512]{3,2,1,0:T(8,128)(2,1)}, u32[]{:S(2)}, u32[]{:S(2)}) collective-permute-start(bf16[7,4,128,512]{3,2,1,0:T(8,128)(2,1)} %get-tuple-element.48), channel_id=1, source_target_pairs={{0,1},{1,0},{2,3},{3,2},{4,5},{5,4},{6,7},{7,6},{8,9},{9,8},{10,11... | collective-permute-start | bytes 11010056 | tf_op jit(solution)/shard_map/ppermute | solution.py:348
  334.9 21.9 %collective-permute-start.45 = (bf16[2,4,128,512]{3,2,1,0:T(8,128)(2,1)S(1)}, bf16[2,4,128,512]{3,2,1,0:T(8,128)(2,1)S(1)}, u32[]{:S(2)}, u32[]{:S(2)}) collective-permute-start(bf16[2,4,128,512]{3,2,1,0:T(8,128)(2,1)S(1)} %add_convert_fusion.11), channel_id=1, source_target_pairs={{0,2},{7,5},{8,10},{15,13},{16,18},{23,21},{24,26},{31,29}} | collective-permute-start | bytes 3145736 | tf_op jit(solution)/shard_map/ppermute | solution.py:358
  337.8 30.2 %collective-permute-start.50 = (bf16[2,4,128,512]{3,2,1,0:T(8,128)(2,1)S(1)}, bf16[2,4,128,512]{3,2,1,0:T(8,128)(2,1)S(1)}, u32[]{:S(2)}, u32[]{:S(2)}) collective-permute-start(bf16[2,4,128,512]{3,2,1,0:T(8,128)(2,1)S(1)} %add_convert_fusion.8), channel_id=1, source_target_pairs={{0,2},{7,5},{8,10},{15,13},{16,18},{23,21},{24,26},{31,29}} | collective-permute-start | bytes 3145736 | tf_op jit(solution)/shard_map/ppermute | solution.py:358
  339.5 39.8 %collective-permute-start.60 = (bf16[2,4,128,512]{3,2,1,0:T(8,128)(2,1)S(1)}, bf16[2,4,128,512]{3,2,1,0:T(8,128)(2,1)S(1)}, u32[]{:S(2)}, u32[]{:S(2)}) collective-permute-start(bf16[2,4,128,512]{3,2,1,0:T(8,128)(2,1)S(1)} %add_convert_fusion.2), channel_id=1, source_target_pairs={{0,2},{7,5},{8,10},{15,13},{16,18},{23,21},{24,26},{31,29}} | collective-permute-start | bytes 3145736 | tf_op jit(solution)/shard_map/ppermute | solution.py:358
  347.3 43.3 %collective-permute-start.56 = (bf16[2,4,128,512]{3,2,1,0:T(8,128)(2,1)S(1)}, bf16[2,4,128,512]{3,2,1,0:T(8,128)(2,1)S(1)}, u32[]{:S(2)}, u32[]{:S(2)}) collective-permute-start(bf16[2,4,128,512]{3,2,1,0:T(8,128)(2,1)S(1)} %add_convert_fusion.4), channel_id=1, source_target_pairs={{0,2},{7,5},{2,4},{5,3},{8,10},{15,13},{10,12},{13,11},{16,18},{23... | collective-permute-start | bytes 3145736 | tf_op jit(solution)/shard_map/ppermute | solution.py:358
  358.5 43.3 %collective-permute-start.46 = (bf16[2,4,128,512]{3,2,1,0:T(8,128)(2,1)S(1)}, bf16[2,4,128,512]{3,2,1,0:T(8,128)(2,1)S(1)}, u32[]{:S(2)}, u32[]{:S(2)}) collective-permute-start(bf16[2,4,128,512]{3,2,1,0:T(8,128)(2,1)S(1)} %add_convert_fusion.10), channel_id=1, source_target_pairs={{0,2},{7,5},{2,4},{5,3},{8,10},{15,13},{10,12},{13,11},{16,18},{23... | collective-permute-start | bytes 3145736 | tf_op jit(solution)/shard_map/ppermute | solution.py:358
  369.7 43.3 %collective-permute-start.51 = (bf16[2,4,128,512]{3,2,1,0:T(8,128)(2,1)S(1)}, bf16[2,4,128,512]{3,2,1,0:T(8,128)(2,1)S(1)}, u32[]{:S(2)}, u32[]{:S(2)}) collective-permute-start(bf16[2,4,128,512]{3,2,1,0:T(8,128)(2,1)S(1)} %add_convert_fusion.7), channel_id=1, source_target_pairs={{0,2},{7,5},{2,4},{5,3},{8,10},{15,13},{10,12},{13,11},{16,18},{23... | collective-permute-start | bytes 3145736 | tf_op jit(solution)/shard_map/ppermute | solution.py:358
  379.8 44.5 %collective-permute-start.61 = (bf16[2,4,128,512]{3,2,1,0:T(8,128)(2,1)S(1)}, bf16[2,4,128,512]{3,2,1,0:T(8,128)(2,1)S(1)}, u32[]{:S(2)}, u32[]{:S(2)}) collective-permute-start(bf16[2,4,128,512]{3,2,1,0:T(8,128)(2,1)S(1)} %add_convert_fusion.1), channel_id=1, source_target_pairs={{0,2},{7,5},{2,4},{5,3},{8,10},{15,13},{10,12},{13,11},{16,18},{23... | collective-permute-start | bytes 3145736 | tf_op jit(solution)/shard_map/ppermute | solution.py:358
  393.2 50.5 %collective-permute-start.57 = (bf16[2,4,128,512]{3,2,1,0:T(8,128)(2,1)}, bf16[2,4,128,512]{3,2,1,0:T(8,128)(2,1)S(1)}, u32[]{:S(2)}, u32[]{:S(2)}) collective-permute-start(bf16[2,4,128,512]{3,2,1,0:T(8,128)(2,1)} %add_convert_fusion.3), channel_id=1, source_target_pairs={{0,2},{7,5},{2,4},{5,3},{4,6},{3,1},{8,10},{15,13},{10,12},{13,11}... | collective-permute-start | bytes 3145736 | tf_op jit(solution)/shard_map/ppermute | solution.py:358
  404.4 42.4 %collective-permute-start.47 = (bf16[2,4,128,512]{3,2,1,0:T(8,128)(2,1)}, bf16[2,4,128,512]{3,2,1,0:T(8,128)(2,1)}, u32[]{:S(2)}, u32[]{:S(2)}) collective-permute-start(bf16[2,4,128,512]{3,2,1,0:T(8,128)(2,1)} %add_convert_fusion.9), channel_id=1, source_target_pairs={{0,2},{7,5},{2,4},{5,3},{4,6},{3,1},{8,10},{15,13},{10,12},{13,11}... | collective-permute-start | bytes 3145736 | tf_op jit(solution)/shard_map/ppermute | solution.py:358
  415.7 42.4 %collective-permute-start.52 = (bf16[2,4,128,512]{3,2,1,0:T(8,128)(2,1)}, bf16[2,4,128,512]{3,2,1,0:T(8,128)(2,1)}, u32[]{:S(2)}, u32[]{:S(2)}) collective-permute-start(bf16[2,4,128,512]{3,2,1,0:T(8,128)(2,1)} %add_convert_fusion.6), channel_id=1, source_target_pairs={{0,2},{7,5},{2,4},{5,3},{4,6},{3,1},{8,10},{15,13},{10,12},{13,11}... | collective-permute-start | bytes 3145736 | tf_op jit(solution)/shard_map/ppermute | solution.py:358
  425.7 43.6 %collective-permute-start.62 = (bf16[2,4,128,512]{3,2,1,0:T(8,128)(2,1)}, bf16[2,4,128,512]{3,2,1,0:T(8,128)(2,1)}, u32[]{:S(2)}, u32[]{:S(2)}) collective-permute-start(bf16[2,4,128,512]{3,2,1,0:T(8,128)(2,1)} %add_convert_fusion), channel_id=1, source_target_pairs={{0,2},{7,5},{2,4},{5,3},{4,6},{3,1},{8,10},{15,13},{10,12},{13,11}... | collective-permute-start | bytes 3145736 | tf_op jit(solution)/shard_map/ppermute | solution.py:358
  443.8 52.9 %collective-permute-start.58 = (bf16[4,128,512]{2,1,0:T(8,128)(2,1)S(1)}, bf16[4,128,512]{2,1,0:T(8,128)(2,1)S(1)}, u32[]{:S(2)}, u32[]{:S(2)}) collective-permute-start(bf16[4,128,512]{2,1,0:T(8,128)(2,1)S(1)} %slice_bitcast_fusion.1), channel_id=1, source_target_pairs={{0,1},{1,0},{2,3},{3,2},{4,5},{5,4},{6,7},{7,6},{8,9},{9,8},{10,11... | collective-permute-start | bytes 1572872 | tf_op jit(solution)/shard_map/ppermute | solution.py:348
  447.9 50.4 %collective-permute-start.48 = (bf16[4,128,512]{2,1,0:T(8,128)(2,1)S(1)}, bf16[4,128,512]{2,1,0:T(8,128)(2,1)S(1)}, u32[]{:S(2)}, u32[]{:S(2)}) collective-permute-start(bf16[4,128,512]{2,1,0:T(8,128)(2,1)S(1)} %slice_bitcast_fusion.3), channel_id=1, source_target_pairs={{0,1},{1,0},{2,3},{3,2},{4,5},{5,4},{6,7},{7,6},{8,9},{9,8},{10,11... | collective-permute-start | bytes 1572872 | tf_op jit(solution)/shard_map/ppermute | solution.py:348
  459.1 39.2 %collective-permute-start.53 = (bf16[4,128,512]{2,1,0:T(8,128)(2,1)S(1)}, bf16[4,128,512]{2,1,0:T(8,128)(2,1)S(1)}, u32[]{:S(2)}, u32[]{:S(2)}) collective-permute-start(bf16[4,128,512]{2,1,0:T(8,128)(2,1)S(1)} %slice_bitcast_fusion.2), channel_id=1, source_target_pairs={{0,1},{1,0},{2,3},{3,2},{4,5},{5,4},{6,7},{7,6},{8,9},{9,8},{10,11... | collective-permute-start | bytes 1572872 | tf_op jit(solution)/shard_map/ppermute | solution.py:348
  470.4 28.0 %collective-permute-start.63 = (bf16[4,128,512]{2,1,0:T(8,128)(2,1)S(1)}, bf16[4,128,512]{2,1,0:T(8,128)(2,1)S(1)}, u32[]{:S(2)}, u32[]{:S(2)}) collective-permute-start(bf16[4,128,512]{2,1,0:T(8,128)(2,1)S(1)} %slice_bitcast_fusion), channel_id=1, source_target_pairs={{0,1},{1,0},{2,3},{3,2},{4,5},{5,4},{6,7},{7,6},{8,9},{9,8},{10,11... | collective-permute-start | bytes 1572872 | tf_op jit(solution)/shard_map/ppermute | solution.py:348
  (59 other events, 1447.2 us)

commit v2 on v1

v2 whole, which is shorter than its diff:
```python
import functools

import jax
import jax.numpy as jnp
import numpy as np
from jax import lax
from jax.experimental import pallas as pl
from jax.experimental.pallas import tpu as pltpu
from jax.sharding import PartitionSpec as P

F32 = jnp.float32
BF16 = jnp.bfloat16
NT = (((1,), (1,)), ((), ()))
NN = (((1,), (0,)), ((), ()))


def dot(a, b, dims=NN):
    return lax.dot_general(a, b, dims, preferred_element_type=F32)


def params(limit_mib):
    return pltpu.CompilerParams(vmem_limit_bytes=limit_mib * 2**20)


VMEM_MIB = 56
LIGHT = pl.CostEstimate(flops=1, bytes_accessed=1, transcendentals=0)


def pair_list(layers):
    return [(s, t) for s in range(layers) for t in range(s, layers)]


def gather_table(chips):
    table = np.full((2 * chips, 2 * chips - 1, 2), -1, np.int32)
    for me in range(2 * chips):
        chip, core = divmod(me, 2)
        way = 1 - 2 * core
        places = [(chip, core)]
        places += [(chip - way * j, core) for j in range(1, chips)]
        places += [(chip + way * j, 1 - core) for j in range(1, chips)]
        for piece, (place, order) in enumerate(places):
            if 0 <= place < chips:
                for half in range(2):
                    table[me, piece, half] = 2 * place + (order ^ half)
    return table.reshape(2 * chips, -1)


def scatter_table(chips):
    table = np.zeros((2 * chips, 3, 2 * chips), np.int32)
    last = 2 * (chips - 1)
    for me in range(2 * chips):
        chip, core = divmod(me, 2)
        way = 1 - 2 * core
        gives, keeps = [], []
        for dist in range(chips - 1, 0, -1):
            slot = 2 * (chips - 1 - dist)
            for half in range(2):
                if 0 <= chip - way * dist < chips:
                    gives.append((2 * (chip - way * dist) + ((1 - core) ^ half), slot + half))
                if 0 <= chip + way * dist < chips:
                    keeps.append((2 * (chip + way * dist) + (core ^ half), slot + half))
        gives.append((2 * chip + 1 - core, last))
        keeps.append((2 * chip + core, last))
        for step, (tile, slot) in enumerate(gives):
            table[me, :, step] = (tile, slot, keeps[0][1])
        for step, (tile, slot) in enumerate(keeps):
            table[me, :, len(gives) + step] = (tile, gives[-1][1], slot)
    return table.reshape(2 * chips, -1)


def encode_kernel(res_ref, weight_ref, bias_ref, active_ref, out_ref):
    pre = dot(res_ref[0], weight_ref[0]) + bias_ref[pl.ds(pl.program_id(0), 1)]
    out_ref[0] = (pre * active_ref[0].astype(F32)).astype(BF16)


def encode(residual, enc_weight, bias, active, start, rows):
    layers, _, width = residual.shape
    own = enc_weight.shape[2]
    at = start // rows
    return pl.pallas_call(
        encode_kernel,
        grid=(layers,),
        in_specs=[
            pl.BlockSpec((1, rows, width), lambda s: (s, at, 0)),
            pl.BlockSpec((1, width, own), lambda s: (s, 0, 0)),
            pl.BlockSpec((layers, own), lambda s: (0, 0)),
            pl.BlockSpec((1, rows, own), lambda s: (s, at, 0)),
        ],
        out_specs=pl.BlockSpec((1, rows, own), lambda s: (s, 0, 0)),
        out_shape=jax.ShapeDtypeStruct((layers, rows, own), BF16),
        compiler_params=params(VMEM_MIB),
        cost_estimate=LIGHT,
        name="encode",
    )(residual, enc_weight, bias, active)


def recon_sum(pairs, weights, lat_tile, total):
    for t in range(total.shape[0]):
        term = total[t]
        for p, (source, target) in enumerate(pairs):
            if target == t:
                term = term + dot(weights[p][0], lat_tile(source), NT)
        total[t] = term


def recon_ends(low_ref, high_ref, total):
    @pl.when(pl.program_id(0) == pl.num_programs(0) - 1)
    def _():
        half = low_ref.shape[0]
        low_ref[...] = total[:half].astype(BF16)
        high_ref[...] = total[half:].astype(BF16)


def recon_whole_kernel(pairs, meta, *refs):
    weights = refs[: len(pairs)]
    lat_ref, low_ref, high_ref, total = refs[len(pairs) :]

    @pl.when(pl.program_id(0) == 0)
    def _():
        total[...] = jnp.zeros_like(total)

    recon_sum(pairs, weights, lambda source: lat_ref[0, source], total)
    recon_ends(low_ref, high_ref, total)


def recon_pieces_kernel(pairs, pieces, meta, *refs):
    npairs = len(pairs)
    weights = refs[:npairs]
    piece_refs = refs[npairs : npairs + pieces]
    low_ref, high_ref, lat_out, lat, total, in_sem, out_sem = refs[npairs + pieces :]
    step = pl.program_id(0)

    def fetch(piece, half):
        slot = meta[npairs + 2 * piece + half]
        return slot, pltpu.make_async_copy(
            piece_refs[piece].at[half], lat.at[jnp.maximum(slot, 0)], in_sem.at[2 * piece + half]
        )

    def keep():
        return pltpu.make_async_copy(lat, lat_out, out_sem)

    @pl.when(step == 0)
    def _():
        for piece in range(pieces):
            for half in range(2):
                slot, copy = fetch(piece, half)
                pl.when(slot >= 0)(copy.start)
        total[...] = jnp.zeros_like(total)
        for piece in range(pieces):
            for half in range(2):
                slot, copy = fetch(piece, half)
                pl.when(slot >= 0)(copy.wait)
        keep().start()

    recon_sum(pairs, weights, lambda source: lat[step, source], total)
    recon_ends(low_ref, high_ref, total)

    @pl.when(step == pl.num_programs(0) - 1)
    def _():
        keep().wait()


def weight_specs(npairs, feat, own, column):
    return [
        pl.BlockSpec((1, feat, own), functools.partial(lambda p, i, meta: (meta[p], 0, column(i, meta)), p))
        for p in range(npairs)
    ]


def recon(meta, dec_weight, lat):
    npairs, feat, cols = dec_weight.shape
    gathered = not isinstance(lat, list)
    *_, layers, rows, own = lat.shape if gathered else lat[0].shape
    tiles = cols // own
    pairs = pair_list(layers)
    half = layers // 2
    any_spec = pl.BlockSpec(memory_space=pl.ANY)
    outs = [
        jax.ShapeDtypeStruct((half, feat, rows), BF16),
        jax.ShapeDtypeStruct((layers - half, feat, rows), BF16),
    ]
    out_specs = [pl.BlockSpec(o.shape, lambda i, meta: (0, 0, 0)) for o in outs]
    scratch = [pltpu.VMEM((layers, feat, rows), F32)]
    if gathered:
        body = functools.partial(recon_whole_kernel, pairs)
        lat_specs = [pl.BlockSpec((1, layers, rows, own), lambda i, meta: (i, 0, 0, 0))]
    else:
        body = functools.partial(recon_pieces_kernel, pairs, len(lat))
        lat_specs = [any_spec] * len(lat)
        outs.append(jax.ShapeDtypeStruct((tiles, layers, rows, own), BF16))
        out_specs.append(any_spec)
        scratch = (
            [pltpu.VMEM((tiles, layers, rows, own), BF16)]
            + scratch
            + [pltpu.SemaphoreType.DMA((2 * len(lat),)), pltpu.SemaphoreType.DMA]
        )
    return pl.pallas_call(
        body,
        grid_spec=pltpu.PrefetchScalarGridSpec(
            num_scalar_prefetch=1,
            grid=(tiles,),
            in_specs=weight_specs(npairs, feat, own, lambda i, meta: i) + lat_specs,
            out_specs=out_specs,
            scratch_shapes=scratch,
        ),
        out_shape=outs,
        compiler_params=params(VMEM_MIB),
        cost_estimate=LIGHT,
        name="recon",
    )(meta, *([dec_weight] * npairs), *([lat] if gathered else lat))


def grad_kernel(pairs, layers, split, meta, *refs):
    npairs = len(pairs)
    weights = refs[:npairs]
    low_ref, high_ref, bias_ref, target_ref = refs[npairs : npairs + 4]
    outs = refs[npairs + 4 : -3]
    error_out, error_t, error_rest = refs[-3:]
    step = pl.program_id(0)
    feat, rows = target_ref.shape[1:]
    main = feat // 256 * 256
    rest = feat - main

    @pl.when(step == 0)
    def _():
        half = low_ref.shape[0]
        for t in range(layers):
            whole = low_ref[t] if t < half else high_ref[t - half]
            error = (whole.astype(F32) + bias_ref[t] - target_ref[t].astype(F32)).astype(BF16)
            error_out[t] = error
            turned = error.astype(F32).T.astype(BF16)
            if main:
                error_t[t] = turned[:, :main]
            if rest:
                for s in range(layers):
                    piece = turned[:, main:]
                    error_rest[s, :, t * rest : (t + 1) * rest] = piece if t >= s else jnp.zeros_like(piece)

    tiles = []
    for s in range(layers):
        total = None
        mine = [(p, t) for p, (source, t) in enumerate(pairs) if source == s]
        if main:
            for p, t in mine:
                term = dot(error_t[t], weights[p][0, :main])
                total = term if total is None else total + term
        if rest:
            stack = [weights[p][0, main:] for p, _ in mine]
            term = dot(error_rest[s][:, s * rest :], jnp.concatenate(stack, 0))
            total = term if total is None else total + term
        tiles.append(total.astype(BF16))

    def write(out_ref):
        for s in range(layers):
            out_ref[0, s] = tiles[s]

    if split:
        gives = meta[npairs + 3 * pl.num_programs(0)]
        early = meta[npairs + pl.num_programs(0) + step] < 2
        pl.when((step < gives) & early)(functools.partial(write, outs[0]))
        pl.when((step < gives) & ~early)(functools.partial(write, outs[1]))
        pl.when(step >= gives)(functools.partial(write, outs[2]))
    else:
        write(outs[0])


def grad(meta, dec_weight, low, high, bias, targets, own, split):
    npairs, feat, cols = dec_weight.shape
    layers, _, rows = targets.shape
    tiles = cols // own
    pairs = pair_list(layers)
    main = feat // 256 * 256
    rest = feat - main
    block = (1, layers, rows, own)
    if split:
        outs = [jax.ShapeDtypeStruct((count, layers, rows, own), BF16) for count in (2, tiles - 3, tiles - 1)]
        out_specs = [
            pl.BlockSpec(block, lambda i, meta: (jnp.minimum(meta[npairs + tiles + i], 1), 0, 0, 0)),
            pl.BlockSpec(block, lambda i, meta: (jnp.maximum(meta[npairs + tiles + i] - 2, 0), 0, 0, 0)),
            pl.BlockSpec(block, lambda i, meta: (meta[npairs + 2 * tiles + i], 0, 0, 0)),
        ]
        column = lambda i, meta: meta[npairs + i]
    else:
        outs = [jax.ShapeDtypeStruct((tiles, layers, rows, own), BF16)]
        out_specs = [pl.BlockSpec(block, lambda i, meta: (i, 0, 0, 0))]
        column = lambda i, meta: i
    whole = lambda shape: pl.BlockSpec(shape, lambda i, meta: (0,) * len(shape))
    return pl.pallas_call(
        functools.partial(grad_kernel, pairs, layers, split),
        grid_spec=pltpu.PrefetchScalarGridSpec(
            num_scalar_prefetch=1,
            grid=(tiles,),
            in_specs=weight_specs(npairs, feat, own, column)
            + [
                whole(low.shape),
                whole(high.shape),
                whole(bias.shape),
                whole(targets.shape),
            ],
            out_specs=out_specs + [whole((layers, feat, rows))],
            scratch_shapes=[
                pltpu.VMEM((layers, rows, max(main, 128)), BF16),
                pltpu.VMEM((layers, rows, max(layers * rest, 128)), BF16),
            ],
        ),
        out_shape=outs + [jax.ShapeDtypeStruct((layers, feat, rows), BF16)],
        compiler_params=params(VMEM_MIB),
        cost_estimate=LIGHT,
        name="latent_grad",
    )(meta, *([dec_weight] * npairs), low, high, bias, targets)


def dec_grad_kernel(pairs, parts, perm, *refs):
    errors, lats, out_ref = refs[:parts], refs[parts : 2 * parts], refs[-1]
    for p, (source, target) in enumerate(pairs):
        total = None
        for error, lat in zip(errors, lats):
            term = dot(error[target], lat[0, source])
            total = term if total is None else total + term
        out_ref[perm[p]] = total.astype(BF16)


def decoder_grad(perm, errors, lats):
    layers, feat, _ = errors[0].shape
    tiles, _, _, own = lats[0].shape
    pairs = pair_list(layers)
    npairs = len(pairs)
    return pl.pallas_call(
        functools.partial(dec_grad_kernel, pairs, len(errors)),
        grid_spec=pltpu.PrefetchScalarGridSpec(
            num_scalar_prefetch=1,
            grid=(tiles,),
            in_specs=[pl.BlockSpec(e.shape, lambda i, m: (0, 0, 0)) for e in errors]
            + [pl.BlockSpec((1,) + lat.shape[1:], lambda i, m: (i, 0, 0, 0)) for lat in lats],
            out_specs=pl.BlockSpec((npairs, feat, own), lambda i, m: (0, 0, i)),
        ),
        out_shape=jax.ShapeDtypeStruct((npairs, feat, tiles * own), BF16),
        compiler_params=params(VMEM_MIB),
        cost_estimate=LIGHT,
        name="dec_grad",
    )(perm, *errors, *lats)


def enc_grad_kernel(parts, res_ref, *refs):
    last_ref, active_ref, out_ref, bias_ref = refs[parts:]
    last = (last_ref[0].astype(F32) * active_ref[0].astype(F32)).astype(BF16)
    whole = jnp.concatenate([part[0] for part in refs[:parts]] + [last], 0)
    out_ref[0] = dot(res_ref[0], whole).astype(BF16)
    bias_ref[pl.ds(pl.program_id(0), 1)] = jnp.sum(whole.astype(F32), axis=0, keepdims=True)


def encoder_grad(residual_t, grads, last, active, start):
    layers, width, tok = residual_t.shape
    _, rows, own = last.shape
    at = start // rows
    part = lambda value: pl.BlockSpec((1,) + value.shape[1:], lambda s: (s, 0, 0))
    return pl.pallas_call(
        functools.partial(enc_grad_kernel, len(grads)),
        grid=(layers,),
        in_specs=[part(residual_t)]
        + [part(g) for g in grads]
        + [part(last), pl.BlockSpec((1, rows, own), lambda s: (s, at, 0))],
        out_specs=[
            pl.BlockSpec((1, width, own), lambda s: (s, 0, 0)),
            pl.BlockSpec((layers, own), lambda s: (0, 0)),
        ],
        out_shape=(
            jax.ShapeDtypeStruct((layers, width, own), BF16),
            jax.ShapeDtypeStruct((layers, own), F32),
        ),
        compiler_params=params(24),
        cost_estimate=LIGHT,
        name="enc_grad",
    )(residual_t, *grads, last, active)


def swap_cores(value, devices):
    return lax.ppermute(value, "tgt", [(i, i ^ 1) for i in range(devices)])


def hop(value, chips, first):
    perm = []
    for chip in first:
        if chip + 1 < chips:
            perm.append((2 * chip, 2 * chip + 2))
            other = chips - 1 - chip
            perm.append((2 * other + 1, 2 * other - 1))
    return lax.ppermute(value, "tgt", perm)


def after(value, *others):
    return lax.optimization_barrier((value,) + others)[0]


def add(*values):
    total = values[0].astype(F32)
    for value in values[1:]:
        total = total + value.astype(F32)
    return total.astype(BF16)


def sum_over_src(value, size, bits):
    if size & (size - 1):
        return lax.psum(value, "src")
    for bit in bits:
        value = add(value, lax.ppermute(value, "src", [(i, i ^ (1 << bit)) for i in range(size)]))
    return value


def token_chunks(tok):
    parts = [4, 2, 2]
    unit = tok // sum(parts)
    return [(unit * sum(parts[:i]), unit * part) for i, part in enumerate(parts)]


def shards(blocks, devices, residual, targets, enc_weight, enc_bias, active, dec_weight, dec_bias, tile_pairs):
    layers, tok, _ = residual.shape
    own = enc_weight.shape[2]
    chips = devices // 2
    chunks = token_chunks(tok)
    pairs = np.array(pair_list(layers), np.int32)
    me = lax.axis_index("tgt")

    same = jnp.all(tile_pairs[None, :, :] == pairs[:, None, :], axis=2)
    perm = jnp.sum(jnp.where(same, jnp.arange(len(pairs), dtype=jnp.int32)[None, :], 0), axis=1, dtype=jnp.int32)
    chip, core = me // 2, me % 2
    gives = 1 + 2 * jnp.where(core == 0, chip, chips - 1 - chip)
    scatter_meta = jnp.concatenate([perm, jnp.asarray(scatter_table(chips))[me], gives[None].astype(jnp.int32)])
    dec_bias3 = dec_bias[:, :, None]
    residual_t = jnp.swapaxes(residual, 1, 2)
    bits = [b for b in range(blocks.bit_length()) if (1 << b) < blocks]

    def scatter(slots):
        early, rest, keep = slots
        early, rest = swap_cores(early, devices), swap_cores(rest, devices)
        last = 2 * (chips - 1)
        gate, carry = [], None
        for j in range(1, chips):
            at = slice(2 * (j - 1), 2 * j)
            terms = [keep[at], early if j == 1 else rest[2 * j - 4 : 2 * j - 2]]
            terms += [] if carry is None else [after(carry, *gate)]
            carry = hop(add(*terms), chips, range(0, j))
            gate = yield carry
            gate = gate or []
        total = add(keep[last], rest[last - 2], carry[0], swap_cores(carry[1], devices))
        while True:
            yield total

    order, lats, parts = [], [], []
    for start, rows in chunks:
        block = encode(after(residual, *order), enc_weight, enc_bias, active, start, rows)
        order = [block]
        lats.append(lax.all_gather(block, "tgt", axis=0))
        parts.append(targets[:, :, start : start + rows])
    order += [residual_t] + parts

    errors, running = [], []
    final = len(chunks) - 1
    for c in range(final + 1):
        order += [next(steps) for steps in running[: max(c - 1, 0)]]
        low, high = recon(perm, dec_weight, after(lats[c], *order))
        order = [low, high]
        order += [next(steps) for steps in running[: c if c == final else max(c - 1, 0)]]
        low = sum_over_src(low, blocks, bits)
        high = sum_over_src(high, blocks, bits[::-1])
        *slots, error = grad(scatter_meta, dec_weight, after(low, *order), high, dec_bias3, parts[c], own, c < final)
        errors.append(error)
        order = [error]
        if c < final:
            running.append(scatter(slots))
    last = lax.psum_scatter(slots[0], "tgt", scatter_dimension=0)
    values = [next(steps, None) for steps in running]
    dec_grad = decoder_grad(after(perm, *order), errors, lats)
    grads = []
    for c, (steps, value) in enumerate(zip(running, values)):
        if value.ndim == 4:
            value = steps.send([dec_grad])
        while value.ndim == 4:
            value = next(steps)
        start, rows = chunks[c]
        grads.append((value.astype(F32) * active[:, start : start + rows].astype(F32)).astype(BF16))
    last = after(last, dec_grad)
    enc_grad, bias_grad = encoder_grad(residual_t, grads, last, active, chunks[-1][0])
    return (dec_grad, enc_grad, bias_grad)


def solution(mesh):
    in_specs = (
        P(),
        P(None, "tgt", None),
        P(None, None, ("src", "tgt")),
        P(None, ("src", "tgt")),
        P(None, None, ("src", "tgt")),
        P("src", "tgt", None),
        P(None, "tgt"),
        P("src", None),
    )
    out_specs = (P("src", "tgt", None), P(None, None, ("src", "tgt")), P(None, ("src", "tgt")))
    body = functools.partial(shards, mesh.shape["src"], mesh.shape["tgt"])
    return jax.shard_map(body, mesh=mesh, in_specs=in_specs, out_specs=out_specs, check_vma=False)
```

time: 516 us -> 395 us (0.77)
  starting transfers between devices: 164 us -> 36.8 us
  waiting for transfers between devices: 99.5 us -> 136 us
  Pallas kernels: 171 us -> 150 us
  local copies, waits for them, and re-layouts: 43.6 us -> 23.4 us
  between operations: 1.52 us -> 14 us
    ppermute x24 -> x6, starting transfers between devices: 74.8 us -> 0.85 us  [swap_cores(): return lax.ppermute(value, 'tgt', [(i, i ^ 1) for i in range(devices)])]
    all_gather x0 -> x3, waiting for transfers between devices: none -> 54.3 us  [shards(): lats.append(lax.all_gather(block, 'tgt', axis=0))]
    ppermute x24 -> x6, waiting for transfers between devices: 91.1 us -> 40.5 us  [hop(): return lax.ppermute(value, 'tgt', perm)]
    ppermute x24 -> x6, starting transfers between devices: 70.1 us -> 20.7 us  [hop(): return lax.ppermute(value, 'tgt', perm)]
    pallas_call x9 -> x7, Pallas kernels: 144 us -> 119 us  [the longest x3 49.2 us: grad(): pl.pallas_call(functools.partial(grad_kernel, pairs, layers, split), grid...]
    ppermute x24 -> x6, waiting for transfers between devices: 0.06 us -> 18.5 us  [swap_cores(): return lax.ppermute(value, 'tgt', [(i, i ^ 1) for i in range(devices)])]
    unnamed x88 -> x23, local copies, waits for them, and re-layouts: 38 us -> 19.7 us
    ppermute x16 -> x12, waiting for transfers between devices: 8.31 us -> 23 us  [sum_over_src(): lax.ppermute(value, 'src', [(i, i ^ 1 << bit) for i in range(size)])]
  transfers between devices with their start and end apart: 64 -> 28, of which waited for: 19 -> 17; matrix products, arithmetic and copies ran while one was open for 9% -> 12% of each run, Pallas kernels for 31% -> 31%
where the time goes in v2:
time: 395 us; the launch traced here: 392 us
  Pallas kernels  150 us (38%)
  waiting for transfers between devices  136 us (34%)
  starting transfers between devices  36.8 us (9%)
  other arithmetic  31.3 us (8%)
  local copies, waits for them, and re-layouts  23.4 us (6%)
  between operations  14 us (4%)
    all_gather x3, waiting for transfers between devices, shards(): lats.append(lax.all_gather(block, 'tgt', axis=0))  54.3 us
    pallas_call x3, Pallas kernels, grad(): pl.pallas_call(functools.partial(grad_kernel, pairs, layers, split), grid...  49.2 us
    pallas_call x3, Pallas kernels, recon(): pl.pallas_call(body, grid_spec=pltpu.PrefetchScalarGridSpec(num_scalar_pr...  45.9 us
    ppermute x6, waiting for transfers between devices, hop(): return lax.ppermute(value, 'tgt', perm)  40.5 us
    convert_element_type x18, other arithmetic, add(): return total.astype(BF16)  26.2 us
    pallas_call x1, Pallas kernels, decoder_grad(): pl.pallas_call(functools.partial(dec_grad_kernel, pairs, len(errors)), gr...  24.4 us
    pallas_call x3, Pallas kernels, encode(): pl.pallas_call(encode_kernel, grid=(layers,), in_specs=[pl.BlockSpec((1,...  23.8 us
    ppermute x12, waiting for transfers between devices, sum_over_src(): lax.ppermute(value, 'src', [(i, i ^ 1 << bit) for i in range(size)])  23 us
  transfers between devices with their start and end apart: 28, of which 17 were waited for; matrix products, arithmetic and copies ran while one was open for 12% of the time, Pallas kernels for 31%

profile of v2, /device:TPU:0, one launch (start us, length us, event | category | flops | bytes accessed | tf_op | source)
XLA Modules:
  0.0 392.2 jit_solution(15456753966517346295)
XLA Ops:
  7.2 8.6 %encode.3 = bf16[4,256,512]{2,1,0:T(8,128)(2,1)} custom-call(bf16[4,512,2304]{2,1,0:T(8,128)(2,1)} %res_ref.2, bf16[4,2304,512]{2,1,0:T(8,128)(2,1)} %weight_ref.5, f32[4,512]{1,0:T(4,128)} %bias_ref.5, s32[4,512,512]{2,1,0:T(8,128)} %refs_3_.13), custom_call_target="tpu_custom_call" | custom-call | flops 1 | bytes 1 | tf_op jit(solution)/shard_map/encode/pallas_call | solution.py:80
  15.9 7.1 %encode.4 = bf16[4,128,512]{2,1,0:T(8,128)(2,1)} custom-call(bf16[4,512,2304]{2,1,0:T(8,128)(2,1)} %res_ref.2, bf16[4,2304,512]{2,1,0:T(8,128)(2,1)} %weight_ref.5, f32[4,512]{1,0:T(4,128)} %bias_ref.5, s32[4,512,512]{2,1,0:T(8,128)} %refs_3_.13), custom_call_target="tpu_custom_call" | custom-call | flops 1 | bytes 1 | tf_op jit(solution)/shard_map/encode/pallas_call | solution.py:80
  23.1 8.1 %encode.5 = bf16[4,128,512]{2,1,0:T(8,128)(2,1)} custom-call(bf16[4,512,2304]{2,1,0:T(8,128)(2,1)} %res_ref.2, bf16[4,2304,512]{2,1,0:T(8,128)(2,1)} %weight_ref.5, f32[4,512]{1,0:T(4,128)} %bias_ref.5, s32[4,512,512]{2,1,0:T(8,128)} %refs_3_.13), custom_call_target="tpu_custom_call" | custom-call | flops 1 | bytes 1 | tf_op jit(solution)/shard_map/encode/pallas_call | solution.py:80
  31.2 12.8 %copy.25 = bf16[4,512,2304]{1,2,0:T(8,128)(2,1)} copy(bf16[4,512,2304]{2,1,0:T(8,128)(2,1)} %res_ref.2) | data formatting | bytes 18874368 | tf_op args[0]
  46.5 54.3 %all-gather.11.cloned.1.call-done = bf16[32,256,512]{2,1,0:T(8,128)(2,1)} async-done(((bf16[4,256,512]{2,1,0:T(8,128)(2,1)}), bf16[32,256,512]{2,1,0:T(8,128)(2,1)}) %all-gather.11.cloned.1.call-update) | async-done | bytes 8388624 | tf_op jit(solution)/shard_map/all_gather | solution.py:453
  100.8 16.1 %recon.3 = (bf16[2,288,256]{2,1,0:T(8,128)(2,1)}, bf16[2,288,256]{2,1,0:T(8,128)(2,1)}) custom-call(s32[10]{0:T(128)} %select_reduce_fusion.meta.perm, bf16[10,288,4096]{2,1,0:T(8,128)(2,1)} %refs_9_.11, bf16[10,288,4096]{2,1,0:T(8,128)(2,1)} %refs_9_.11, bf16[10,288,4096]{2,1,0:T(8,128)(2,1)} %refs_9_.11, bf16[10,288,4096]{2,1,0:T(8,128)(2,1)} %refs_9_.11, ...), custom_call_target="tpu_custom_call" | custom-call | flops 1 | bytes 1 | tf_op jit(solution)/shard_map/recon/pallas_call | solution.py:197
  116.9 1.7 collective-permute-start
  118.6 1.5 collective-permute-start.2
  120.9 5.5 %collective-permute-done = bf16[2,288,256]{2,1,0:T(8,128)(2,1)S(1)} collective-permute-done((bf16[2,288,256]{2,1,0:T(8,128)(2,1)}, bf16[2,288,256]{2,1,0:T(8,128)(2,1)S(1)}, u32[]{:S(2)}, u32[]{:S(2)}) %collective-permute-start) | collective-permute-done | bytes 294944 | tf_op jit(solution)/shard_map/ppermute | solution.py:406
  127.4 1.6 collective-permute-start.1
  130.1 1.5 collective-permute-start.3
  133.4 2.6 collective-permute-done.1
  136.8 1.5 collective-permute-done.3
  139.1 19.1 %latent_grad.3 = (bf16[2,4,256,512]{3,2,1,0:T(8,128)(2,1)}, bf16[5,4,256,512]{3,2,1,0:T(8,128)(2,1)}, bf16[7,4,256,512]{3,2,1,0:T(8,128)(2,1)}, bf16[4,288,256]{2,1,0:T(8,128)(2,1)}) custom-call(s32[35]{0:T(128)} %pad_add_fusion.meta, bf16[10,288,4096]{2,1,0:T(8,128)(2,1)} %refs_9_.11, bf16[10,288,4096]{2,1,0:T(8,128)(2,1)} %refs_9_.11, ...), custom_call_target="tpu_custom_call" | custom-call | flops 1 | bytes 1 | tf_op jit(solution)/shard_map/latent_grad/pallas_call | solution.py:288
  158.8 11.5 %collective-permute-done.8 = bf16[2,4,256,512]{3,2,1,0:T(8,128)(2,1)S(1)} collective-permute-done((bf16[2,4,256,512]{3,2,1,0:T(8,128)(2,1)}, bf16[2,4,256,512]{3,2,1,0:T(8,128)(2,1)S(1)}, u32[]{:S(2)}, u32[]{:S(2)}) %collective-permute-start.8) | collective-permute-done | bytes 2097184 | tf_op jit(solution)/shard_map/ppermute | solution.py:378
  170.3 2.2 add_convert_fusion.2
  172.5 2.6 collective-permute-start.9
  175.1 14.9 %recon.4 = (bf16[2,288,128]{2,1,0:T(8,128)(2,1)}, bf16[2,288,128]{2,1,0:T(8,128)(2,1)}) custom-call(s32[10]{0:T(128)} %select_reduce_fusion.meta.perm, bf16[10,288,4096]{2,1,0:T(8,128)(2,1)} %refs_9_.11, bf16[10,288,4096]{2,1,0:T(8,128)(2,1)} %refs_9_.11, bf16[10,288,4096]{2,1,0:T(8,128)(2,1)} %refs_9_.11, bf16[10,288,4096]{2,1,0:T(8,128)(2,1)} %refs_9_.11, ...), custom_call_target="tpu_custom_call" | custom-call | flops 1 | bytes 1 | tf_op jit(solution)/shard_map/recon/pallas_call | solution.py:197
  192.1 3.5 collective-permute-done.4
  198.1 1.5 collective-permute-start.7
  199.7 2.1 collective-permute-done.5
  204.0 15.3 %latent_grad.4 = (bf16[2,4,128,512]{3,2,1,0:T(8,128)(2,1)}, bf16[5,4,128,512]{3,2,1,0:T(8,128)(2,1)}, bf16[7,4,128,512]{3,2,1,0:T(8,128)(2,1)}, bf16[4,288,128]{2,1,0:T(8,128)(2,1)}) custom-call(s32[35]{0:T(128)} %pad_add_fusion.meta, bf16[10,288,4096]{2,1,0:T(8,128)(2,1)} %refs_9_.11, bf16[10,288,4096]{2,1,0:T(8,128)(2,1)} %refs_9_.11, ...), custom_call_target="tpu_custom_call" | custom-call | flops 1 | bytes 1 | tf_op jit(solution)/shard_map/latent_grad/pallas_call | solution.py:288
  219.5 5.1 %add_convert_fusion.1 = bf16[2,4,256,512]{3,2,1,0:T(8,128)(2,1)} fusion(bf16[2,4,256,512]{3,2,1,0:T(8,128)(2,1)} %collective-permute-done.9, bf16[5,4,256,512]{3,2,1,0:T(8,128)(2,1)} %collective-permute-done.12, bf16[7,4,256,512]{3,2,1,0:T(8,128)(2,1)} %get-tuple-element.44), kind=kLoop, calls=%fused_computation.1 | loop fusion | flops 6291456 | bytes 8388608 | tf_op jit(solution)/shard_map/convert_element_type | solution.py:399
  224.6 1.6 collective-permute-start.13
  226.2 14.8 %recon.5 = (bf16[2,288,128]{2,1,0:T(8,128)(2,1)}, bf16[2,288,128]{2,1,0:T(8,128)(2,1)}) custom-call(s32[10]{0:T(128)} %select_reduce_fusion.meta.perm, bf16[10,288,4096]{2,1,0:T(8,128)(2,1)} %refs_9_.11, bf16[10,288,4096]{2,1,0:T(8,128)(2,1)} %refs_9_.11, bf16[10,288,4096]{2,1,0:T(8,128)(2,1)} %refs_9_.11, bf16[10,288,4096]{2,1,0:T(8,128)(2,1)} %refs_9_.11, ...), custom_call_target="tpu_custom_call" | custom-call | flops 1 | bytes 1 | tf_op jit(solution)/shard_map/recon/pallas_call | solution.py:197
  241.0 1.7 collective-permute-start.10
  242.7 1.5 add_convert_fusion.5
  244.2 4.3 %collective-permute-start.15 = (bf16[2,4,128,512]{3,2,1,0:T(8,128)(2,1)S(1)}, bf16[2,4,128,512]{3,2,1,0:T(8,128)(2,1)S(1)}, u32[]{:S(2)}, u32[]{:S(2)}) collective-permute-start(bf16[2,4,128,512]{3,2,1,0:T(8,128)(2,1)S(1)} %add_convert_fusion.5), channel_id=1, source_target_pairs={{0,2},{7,5},{8,10},{15,13},{16,18},{23,21},{24,26},{31,29}} | collective-permute-start | bytes 3145736 | tf_op jit(solution)/shard_map/ppermute | solution.py:388
  248.7 2.1 collective-permute-start.11
  250.7 3.0 collective-permute-done.16
  256.0 3.0 collective-permute-done.17
  260.8 14.7 %latent_grad.5 = (bf16[8,4,128,512]{3,2,1,0:T(8,128)(2,1)}, bf16[4,288,128]{2,1,0:T(8,128)(2,1)}) custom-call(s32[35]{0:T(128)} %pad_add_fusion.meta, bf16[10,288,4096]{2,1,0:T(8,128)(2,1)} %refs_9_.11, bf16[10,288,4096]{2,1,0:T(8,128)(2,1)} %refs_9_.11, bf16[10,288,4096]{2,1,0:T(8,128)(2,1)} %refs_9_.11, bf16[10,288,4096]{2,1,0:T(8,128)(2,1)} %refs_9_.11, ...), custom_call_target="tpu_custom_call" | custom-call | flops 1 | bytes 1 | tf_op jit(solution)/shard_map/latent_grad/pallas_call | solution.py:288
  275.6 5.1 %collective-permute-done.20 = bf16[5,4,128,512]{3,2,1,0:T(8,128)(2,1)S(1)} collective-permute-done((bf16[5,4,128,512]{3,2,1,0:T(8,128)(2,1)}, bf16[5,4,128,512]{3,2,1,0:T(8,128)(2,1)S(1)}, u32[]{:S(2)}, u32[]{:S(2)}) %collective-permute-start.20) | collective-permute-done | bytes 2621472 | tf_op jit(solution)/shard_map/ppermute | solution.py:378
  280.7 2.8 add_convert_fusion.4
  283.5 4.5 %collective-permute-start.21 = (bf16[2,4,128,512]{3,2,1,0:T(8,128)(2,1)}, bf16[2,4,128,512]{3,2,1,0:T(8,128)(2,1)S(1)}, u32[]{:S(2)}, u32[]{:S(2)}) collective-permute-start(bf16[2,4,128,512]{3,2,1,0:T(8,128)(2,1)} %add_convert_fusion.4), channel_id=1, source_target_pairs={{0,2},{7,5},{2,4},{5,3},{8,10},{15,13},{10,12},{13,11},{16,18},{23... | collective-permute-start | bytes 3145736 | tf_op jit(solution)/shard_map/ppermute | solution.py:388
  288.0 4.5 %add_convert_fusion = bf16[2,4,256,512]{3,2,1,0:T(8,128)(2,1)} fusion(bf16[2,4,256,512]{3,2,1,0:T(8,128)(2,1)S(1)} %collective-permute-done.13, bf16[5,4,256,512]{3,2,1,0:T(8,128)(2,1)} %collective-permute-done.12, bf16[7,4,256,512]{3,2,1,0:T(8,128)(2,1)} %get-tuple-element.44), kind=kLoop, calls=%fused_computation | loop fusion | flops 6291456 | bytes 8388608 | tf_op jit(solution)/shard_map/convert_element_type | solution.py:399
  292.4 3.5 collective-permute-start.18
  295.9 24.4 %dec_grad.1 = bf16[10,288,4096]{2,1,0:T(8,128)(2,1)} custom-call(s32[10]{0:T(128)} %select_reduce_fusion.meta.perm, bf16[4,288,256]{2,1,0:T(8,128)(2,1)} %get-tuple-element.38.refs_0_, bf16[4,288,128]{2,1,0:T(8,128)(2,1)} %get-tuple-element.43.refs_1_, bf16[4,288,128]{2,1,0:T(8,128)(2,1)} %get-tuple-element.53.refs_2_, bf16[8,4,256,512]{3,2,1,0:T(8,128)(2,1)} %bitcast.28, ...), custom_call_target="tpu_custom_call" | custom-call | flops 1 | bytes 1 | tf_op jit(solution)/shard_map/dec_grad/pallas_call | solution.py:328
  320.3 2.6 collective-permute-done.21
  322.9 1.8 add_convert_fusion.3
  324.8 4.3 %collective-permute-start.22 = (bf16[2,4,128,512]{3,2,1,0:T(8,128)(2,1)S(1)}, bf16[2,4,128,512]{3,2,1,0:T(8,128)(2,1)S(1)}, u32[]{:S(2)}, u32[]{:S(2)}) collective-permute-start(bf16[2,4,128,512]{3,2,1,0:T(8,128)(2,1)S(1)} %add_convert_fusion.3), channel_id=1, source_target_pairs={{0,2},{7,5},{2,4},{5,3},{4,6},{3,1},{8,10},{15,13},{10,12},{13,11}... | collective-permute-start | bytes 3145736 | tf_op jit(solution)/shard_map/ppermute | solution.py:388
  329.1 25.8 %collective-permute-done.18 = bf16[2,4,256,512]{3,2,1,0:T(8,128)(2,1)S(1)} collective-permute-done((bf16[2,4,256,512]{3,2,1,0:T(8,128)(2,1)}, bf16[2,4,256,512]{3,2,1,0:T(8,128)(2,1)S(1)}, u32[]{:S(2)}, u32[]{:S(2)}) %collective-permute-start.18) | collective-permute-done | bytes 2097184 | tf_op jit(solution)/shard_map/ppermute | solution.py:388
  355.0 11.0 %collective-permute-done.22 = bf16[2,4,128,512]{3,2,1,0:T(8,128)(2,1)S(1)} collective-permute-done((bf16[2,4,128,512]{3,2,1,0:T(8,128)(2,1)S(1)}, bf16[2,4,128,512]{3,2,1,0:T(8,128)(2,1)S(1)}, u32[]{:S(2)}, u32[]{:S(2)}) %collective-permute-start.22) | collective-permute-done | bytes 1048608 | tf_op jit(solution)/shard_map/ppermute | solution.py:388
  366.1 1.9 collective-permute-done.23
  369.5 2.3 multiply_convert_fusion.refs_0_
  371.8 2.2 copy-done.1
  374.0 3.7 copy-done.2
  378.7 7.0 %enc_grad.1 = (bf16[4,2304,512]{2,1,0:T(8,128)(2,1)}, f32[4,512]{1,0:T(4,128)}) custom-call(bf16[4,2304,512]{2,1,0:T(8,128)(2,1)S(1)} %bitcast.25, bf16[4,256,512]{2,1,0:T(8,128)(2,1)S(1)} %multiply_convert_fusion.refs_0_, bf16[4,128,512]{2,1,0:T(8,128)(2,1)S(1)} %multiply_convert_fusion.1.refs_1_, bf16[4,128,512]{2,1,0:T(8,128)(2,1)S(1)} %bitcast.26, ...), custom_call_target="tpu_custom_call" | custom-call | flops 1 | bytes 1 | tf_op jit(solution)/shard_map/enc_grad/pallas_call | solution.py:357
  (75 shorter events, 23.5 us)
Async XLA Ops:
  7.2 93.6 %all-gather.11.cloned.1.call-start = ((), (), s32[]{:S(2)}) async-start(), calls=%async_computation.4 | async-start | bytes 9437184 | tf_op jit(solution)/shard_map/all_gather | solution.py:453
  15.9 159.2 %all-gather.9.cloned.1.call-start = ((), (), s32[]{:S(2)}) async-start(), calls=%async_computation.3 | async-start | bytes 4718592 | tf_op jit(solution)/shard_map/all_gather | solution.py:453
  23.1 203.1 %all-gather.7.cloned.1.call-start = ((), (), s32[]{:S(2)}) async-start(), calls=%async_computation.2 | async-start | bytes 4718592 | tf_op jit(solution)/shard_map/all_gather | solution.py:453
  31.2 12.8 %copy-start.4 = (bf16[4,288,512]{2,1,0:T(8,128)(2,1)S(1)}, bf16[4,288,512]{2,1,0:T(8,128)(2,1)}, u32[]{:S(2)}) copy-start(bf16[4,288,512]{2,1,0:T(8,128)(2,1)} %param.11) | copy-start | bytes 3538948
  31.2 13.7 %copy-start.9 = (s32[10,2]{0,1:T(2,128)S(1)}, s32[10,2]{0,1:T(2,128)}, u32[]{:S(2)}) copy-start(s32[10,2]{0,1:T(2,128)} %param.17) | copy-start | bytes 244
  31.2 13.7 %copy-start.10 = (s32[10,2]{0,1:T(2,128)S(1)}, s32[10,2]{0,1:T(2,128)}, u32[]{:S(2)}) copy-start(s32[10,2]{0,1:T(2,128)} %constant.44) | copy-start | bytes 244
  116.9 14.7 %copy-start.7 = (s32[10]{0:T(128)S(1)}, s32[10]{0:T(128)}, u32[]{:S(2)}) copy-start(s32[10]{0:T(128)} %select_reduce_fusion.meta.perm) | copy-start | bytes 124
  116.9 15.4 %copy-start.8 = (f32[4,288]{1,0:T(4,128)S(1)}, f32[4,288]{1,0:T(4,128)}, u32[]{:S(2)}) copy-start(f32[4,288]{1,0:T(4,128)} %param.16) | copy-start | bytes 13828
  116.9 9.5 %collective-permute-start = (bf16[2,288,256]{2,1,0:T(8,128)(2,1)}, bf16[2,288,256]{2,1,0:T(8,128)(2,1)S(1)}, u32[]{:S(2)}, u32[]{:S(2)}) collective-permute-start(bf16[2,288,256]{2,1,0:T(8,128)(2,1)} %get-tuple-element.35), channel_id=1, source_target_pairs={{0,8},{8,0},{16,24},{24,16},{1,9},{9,1},{17,25},{25,17},{2,10},{10... | collective-permute-start | bytes 884744 | tf_op jit(solution)/shard_map/ppermute | solution.py:406
  118.6 253.2 %reduce-scatter.2.cloned.1.call-start = ((), (), s32[]{:S(2)}) async-start(), calls=%async_computation.1 | async-start | bytes 4718592 | tf_op jit(solution)/shard_map/reduce_scatter | solution.py:471
  118.6 10.4 %collective-permute-start.2 = (bf16[2,288,256]{2,1,0:T(8,128)(2,1)}, bf16[2,288,256]{2,1,0:T(8,128)(2,1)S(1)}, u32[]{:S(2)}, u32[]{:S(2)}) collective-permute-start(bf16[2,288,256]{2,1,0:T(8,128)(2,1)} %get-tuple-element.36), channel_id=1, source_target_pairs={{0,16},{8,24},{16,0},{24,8},{1,17},{9,25},{17,1},{25,9},{2,18},{10... | collective-permute-start | bytes 884744 | tf_op jit(solution)/shard_map/ppermute | solution.py:406
  127.4 8.6 %collective-permute-start.1 = (bf16[2,288,256]{2,1,0:T(8,128)(2,1)S(1)}, bf16[2,288,256]{2,1,0:T(8,128)(2,1)S(1)}, u32[]{:S(2)}, u32[]{:S(2)}) collective-permute-start(bf16[2,288,256]{2,1,0:T(8,128)(2,1)S(1)} %add_convert_fusion.9), channel_id=1, source_target_pairs={{0,16},{8,24},{16,0},{24,8},{1,17},{9,25},{17,1},{25,9},{2,18},{10... | collective-permute-start | bytes 884744 | tf_op jit(solution)/shard_map/ppermute | solution.py:406
  130.1 8.2 %collective-permute-start.3 = (bf16[2,288,256]{2,1,0:T(8,128)(2,1)S(1)}, bf16[2,288,256]{2,1,0:T(8,128)(2,1)S(1)}, u32[]{:S(2)}, u32[]{:S(2)}) collective-permute-start(bf16[2,288,256]{2,1,0:T(8,128)(2,1)S(1)} %add_convert_fusion.7), channel_id=1, source_target_pairs={{0,8},{8,0},{16,24},{24,16},{1,9},{9,1},{17,25},{25,17},{2,10},{10... | collective-permute-start | bytes 884744 | tf_op jit(solution)/shard_map/ppermute | solution.py:406
  158.2 61.3 %collective-permute-start.12 = (bf16[5,4,256,512]{3,2,1,0:T(8,128)(2,1)}, bf16[5,4,256,512]{3,2,1,0:T(8,128)(2,1)}, u32[]{:S(2)}, u32[]{:S(2)}) collective-permute-start(bf16[5,4,256,512]{3,2,1,0:T(8,128)(2,1)} %get-tuple-element.49), channel_id=1, source_target_pairs={{0,1},{1,0},{2,3},{3,2},{4,5},{5,4},{6,7},{7,6},{8,9},{9,8},{10,11... | collective-permute-start | bytes 15728648 | tf_op jit(solution)/shard_map/ppermute | solution.py:378
  158.3 12.0 %collective-permute-start.8 = (bf16[2,4,256,512]{3,2,1,0:T(8,128)(2,1)}, bf16[2,4,256,512]{3,2,1,0:T(8,128)(2,1)S(1)}, u32[]{:S(2)}, u32[]{:S(2)}) collective-permute-start(bf16[2,4,256,512]{3,2,1,0:T(8,128)(2,1)} %get-tuple-element.45), channel_id=1, source_target_pairs={{0,1},{1,0},{2,3},{3,2},{4,5},{5,4},{6,7},{7,6},{8,9},{9,8},{10,11... | collective-permute-start | bytes 6291464 | tf_op jit(solution)/shard_map/ppermute | solution.py:378
  172.5 47.0 %collective-permute-start.9 = (bf16[2,4,256,512]{3,2,1,0:T(8,128)(2,1)S(1)}, bf16[2,4,256,512]{3,2,1,0:T(8,128)(2,1)}, u32[]{:S(2)}, u32[]{:S(2)}) collective-permute-start(bf16[2,4,256,512]{3,2,1,0:T(8,128)(2,1)S(1)} %add_convert_fusion.2), channel_id=1, source_target_pairs={{0,2},{7,5},{8,10},{15,13},{16,18},{23,21},{24,26},{31,29}} | collective-permute-start | bytes 6291464 | tf_op jit(solution)/shard_map/ppermute | solution.py:388
  190.0 5.6 %collective-permute-start.4 = (bf16[2,288,128]{2,1,0:T(8,128)(2,1)}, bf16[2,288,128]{2,1,0:T(8,128)(2,1)S(1)}, u32[]{:S(2)}, u32[]{:S(2)}) collective-permute-start(bf16[2,288,128]{2,1,0:T(8,128)(2,1)} %get-tuple-element.40), channel_id=1, source_target_pairs={{0,8},{8,0},{16,24},{24,16},{1,9},{9,1},{17,25},{25,17},{2,10},{10... | collective-permute-start | bytes 442376 | tf_op jit(solution)/shard_map/ppermute | solution.py:406
  191.4 5.7 %collective-permute-start.6 = (bf16[2,288,128]{2,1,0:T(8,128)(2,1)}, bf16[2,288,128]{2,1,0:T(8,128)(2,1)S(1)}, u32[]{:S(2)}, u32[]{:S(2)}) collective-permute-start(bf16[2,288,128]{2,1,0:T(8,128)(2,1)} %get-tuple-element.41), channel_id=1, source_target_pairs={{0,16},{8,24},{16,0},{24,8},{1,17},{9,25},{17,1},{25,9},{2,18},{10... | collective-permute-start | bytes 442376 | tf_op jit(solution)/shard_map/ppermute | solution.py:406
  196.6 5.2 %collective-permute-start.5 = (bf16[2,288,128]{2,1,0:T(8,128)(2,1)S(1)}, bf16[2,288,128]{2,1,0:T(8,128)(2,1)S(1)}, u32[]{:S(2)}, u32[]{:S(2)}) collective-permute-start(bf16[2,288,128]{2,1,0:T(8,128)(2,1)S(1)} %add_convert_fusion.17), channel_id=1, source_target_pairs={{0,16},{8,24},{16,0},{24,8},{1,17},{9,25},{17,1},{25,9},{2,18},{10... | collective-permute-start | bytes 442376 | tf_op jit(solution)/shard_map/ppermute | solution.py:406
  198.1 5.2 %collective-permute-start.7 = (bf16[2,288,128]{2,1,0:T(8,128)(2,1)S(1)}, bf16[2,288,128]{2,1,0:T(8,128)(2,1)S(1)}, u32[]{:S(2)}, u32[]{:S(2)}) collective-permute-start(bf16[2,288,128]{2,1,0:T(8,128)(2,1)S(1)} %add_convert_fusion.15), channel_id=1, source_target_pairs={{0,8},{8,0},{16,24},{24,16},{1,9},{9,1},{17,25},{25,17},{2,10},{10... | collective-permute-start | bytes 442376 | tf_op jit(solution)/shard_map/ppermute | solution.py:406
  219.4 23.3 %collective-permute-start.14 = (bf16[2,4,128,512]{3,2,1,0:T(8,128)(2,1)}, bf16[2,4,128,512]{3,2,1,0:T(8,128)(2,1)S(1)}, u32[]{:S(2)}, u32[]{:S(2)}) collective-permute-start(bf16[2,4,128,512]{3,2,1,0:T(8,128)(2,1)} %get-tuple-element.51), channel_id=1, source_target_pairs={{0,1},{1,0},{2,3},{3,2},{4,5},{5,4},{6,7},{7,6},{8,9},{9,8},{10,11... | collective-permute-start | bytes 3145736 | tf_op jit(solution)/shard_map/ppermute | solution.py:378
  224.6 36.3 %collective-permute-start.13 = (bf16[2,4,256,512]{3,2,1,0:T(8,128)(2,1)}, bf16[2,4,256,512]{3,2,1,0:T(8,128)(2,1)S(1)}, u32[]{:S(2)}, u32[]{:S(2)}) collective-permute-start(bf16[2,4,256,512]{3,2,1,0:T(8,128)(2,1)} %add_convert_fusion.1), channel_id=1, source_target_pairs={{0,2},{7,5},{2,4},{5,3},{8,10},{15,13},{10,12},{13,11},{16,18},{23... | collective-permute-start | bytes 6291464 | tf_op jit(solution)/shard_map/ppermute | solution.py:388
  241.0 7.5 %copy-start.5 = (bf16[2,288,128]{2,1,0:T(8,128)(2,1)S(1)}, bf16[2,288,128]{2,1,0:T(8,128)(2,1)}, u32[]{:S(2)}) copy-start(bf16[2,288,128]{2,1,0:T(8,128)(2,1)} %get-tuple-element.48) | copy-start | bytes 442372
  241.0 7.6 %copy-start.6 = (bf16[2,288,128]{2,1,0:T(8,128)(2,1)S(1)}, bf16[2,288,128]{2,1,0:T(8,128)(2,1)}, u32[]{:S(2)}) copy-start(bf16[2,288,128]{2,1,0:T(8,128)(2,1)} %get-tuple-element.47) | copy-start | bytes 442372
  241.0 7.6 %collective-permute-start.10 = (bf16[2,288,128]{2,1,0:T(8,128)(2,1)}, bf16[2,288,128]{2,1,0:T(8,128)(2,1)S(1)}, u32[]{:S(2)}, u32[]{:S(2)}) collective-permute-start(bf16[2,288,128]{2,1,0:T(8,128)(2,1)} %get-tuple-element.47), channel_id=1, source_target_pairs={{0,8},{8,0},{16,24},{24,16},{1,9},{9,1},{17,25},{25,17},{2,10},{10... | collective-permute-start | bytes 442376 | tf_op jit(solution)/shard_map/ppermute | solution.py:406
  244.2 16.6 %collective-permute-start.15 = (bf16[2,4,128,512]{3,2,1,0:T(8,128)(2,1)S(1)}, bf16[2,4,128,512]{3,2,1,0:T(8,128)(2,1)S(1)}, u32[]{:S(2)}, u32[]{:S(2)}) collective-permute-start(bf16[2,4,128,512]{3,2,1,0:T(8,128)(2,1)S(1)} %add_convert_fusion.5), channel_id=1, source_target_pairs={{0,2},{7,5},{8,10},{15,13},{16,18},{23,21},{24,26},{31,29}} | collective-permute-start | bytes 3145736 | tf_op jit(solution)/shard_map/ppermute | solution.py:388
  248.5 5.2 %collective-permute-start.16 = (bf16[2,288,128]{2,1,0:T(8,128)(2,1)S(1)}, bf16[2,288,128]{2,1,0:T(8,128)(2,1)S(1)}, u32[]{:S(2)}, u32[]{:S(2)}) collective-permute-start(bf16[2,288,128]{2,1,0:T(8,128)(2,1)S(1)} %copy-done.5), channel_id=1, source_target_pairs={{0,16},{8,24},{16,0},{24,8},{1,17},{9,25},{17,1},{25,9},{2,18},{10... | collective-permute-start | bytes 442376 | tf_op jit(solution)/shard_map/ppermute | solution.py:406
  248.7 6.6 %collective-permute-start.11 = (bf16[2,288,128]{2,1,0:T(8,128)(2,1)S(1)}, bf16[2,288,128]{2,1,0:T(8,128)(2,1)S(1)}, u32[]{:S(2)}, u32[]{:S(2)}) collective-permute-start(bf16[2,288,128]{2,1,0:T(8,128)(2,1)S(1)} %add_convert_fusion.13), channel_id=1, source_target_pairs={{0,16},{8,24},{16,0},{24,8},{1,17},{9,25},{17,1},{25,9},{2,18},{10... | collective-permute-start | bytes 442376 | tf_op jit(solution)/shard_map/ppermute | solution.py:406
  253.8 5.2 %collective-permute-start.17 = (bf16[2,288,128]{2,1,0:T(8,128)(2,1)S(1)}, bf16[2,288,128]{2,1,0:T(8,128)(2,1)S(1)}, u32[]{:S(2)}, u32[]{:S(2)}) collective-permute-start(bf16[2,288,128]{2,1,0:T(8,128)(2,1)S(1)} %add_convert_fusion.11), channel_id=1, source_target_pairs={{0,8},{8,0},{16,24},{24,16},{1,9},{9,1},{17,25},{25,17},{2,10},{10... | collective-permute-start | bytes 442376 | tf_op jit(solution)/shard_map/ppermute | solution.py:406
  275.6 5.2 %collective-permute-start.20 = (bf16[5,4,128,512]{3,2,1,0:T(8,128)(2,1)}, bf16[5,4,128,512]{3,2,1,0:T(8,128)(2,1)S(1)}, u32[]{:S(2)}, u32[]{:S(2)}) collective-permute-start(bf16[5,4,128,512]{3,2,1,0:T(8,128)(2,1)} %get-tuple-element.55), channel_id=1, source_target_pairs={{0,1},{1,0},{2,3},{3,2},{4,5},{5,4},{6,7},{7,6},{8,9},{9,8},{10,11... | collective-permute-start | bytes 7864328 | tf_op jit(solution)/shard_map/ppermute | solution.py:378
  283.5 39.4 %collective-permute-start.21 = (bf16[2,4,128,512]{3,2,1,0:T(8,128)(2,1)}, bf16[2,4,128,512]{3,2,1,0:T(8,128)(2,1)S(1)}, u32[]{:S(2)}, u32[]{:S(2)}) collective-permute-start(bf16[2,4,128,512]{3,2,1,0:T(8,128)(2,1)} %add_convert_fusion.4), channel_id=1, source_target_pairs={{0,2},{7,5},{2,4},{5,3},{8,10},{15,13},{10,12},{13,11},{16,18},{23... | collective-permute-start | bytes 3145736 | tf_op jit(solution)/shard_map/ppermute | solution.py:388
  292.4 62.5 %collective-permute-start.18 = (bf16[2,4,256,512]{3,2,1,0:T(8,128)(2,1)}, bf16[2,4,256,512]{3,2,1,0:T(8,128)(2,1)S(1)}, u32[]{:S(2)}, u32[]{:S(2)}) collective-permute-start(bf16[2,4,256,512]{3,2,1,0:T(8,128)(2,1)} %add_convert_fusion), channel_id=1, source_target_pairs={{0,2},{7,5},{2,4},{5,3},{4,6},{3,1},{8,10},{15,13},{10,12},{13,11}... | collective-permute-start | bytes 6291464 | tf_op jit(solution)/shard_map/ppermute | solution.py:388
  322.9 45.1 %copy-start = (s32[4,512,512]{2,1,0:T(8,128)S(1)}, s32[4,512,512]{2,1,0:T(8,128)}, u32[]{:S(2)}) copy-start(s32[4,512,512]{2,1,0:T(8,128)} %refs_3_.13) | copy-start | bytes 12582916
  324.8 41.2 %collective-permute-start.22 = (bf16[2,4,128,512]{3,2,1,0:T(8,128)(2,1)S(1)}, bf16[2,4,128,512]{3,2,1,0:T(8,128)(2,1)S(1)}, u32[]{:S(2)}, u32[]{:S(2)}) collective-permute-start(bf16[2,4,128,512]{3,2,1,0:T(8,128)(2,1)S(1)} %add_convert_fusion.3), channel_id=1, source_target_pairs={{0,2},{7,5},{2,4},{5,3},{4,6},{3,1},{8,10},{15,13},{10,12},{13,11}... | collective-permute-start | bytes 3145736 | tf_op jit(solution)/shard_map/ppermute | solution.py:388
  354.9 14.5 %collective-permute-start.19 = (bf16[4,256,512]{2,1,0:T(8,128)(2,1)S(1)}, bf16[4,256,512]{2,1,0:T(8,128)(2,1)S(1)}, u32[]{:S(2)}, u32[]{:S(2)}) collective-permute-start(bf16[4,256,512]{2,1,0:T(8,128)(2,1)S(1)} %slice_bitcast_fusion), channel_id=1, source_target_pairs={{0,1},{1,0},{2,3},{3,2},{4,5},{5,4},{6,7},{7,6},{8,9},{9,8},{10,11... | collective-permute-start | bytes 3145736 | tf_op jit(solution)/shard_map/ppermute | solution.py:378
  366.0 2.0 collective-permute-start.23
  371.8 2.2 copy-start.1
  374.0 3.7 copy-start.2
  377.7 1.0 copy-start.3
Sparse Core Ops, SparseCore 0:
  16.0 84.7 all-gather.10
  102.4 45.6 all-gather.8
  149.7 48.9 all-gather.6
  275.7 66.9 reduce-scatter.1

commit v3 on v2

--- a/solution.py
+++ b/solution.py
@@ -1,4 +1,5 @@
 import functools
+import math
 
 import jax
 import jax.numpy as jnp
@@ -47,6 +48,7 @@
 
 def scatter_table(chips):
     table = np.zeros((2 * chips, 3, 2 * chips), np.int32)
+    counts = np.zeros((2 * chips, 1), np.int32)
     last = 2 * (chips - 1)
     for me in range(2 * chips):
         chip, core = divmod(me, 2)
@@ -65,7 +67,8 @@
             table[me, :, step] = (tile, slot, keeps[0][1])
         for step, (tile, slot) in enumerate(keeps):
             table[me, :, len(gives) + step] = (tile, gives[-1][1], slot)
-    return table.reshape(2 * chips, -1)
+        counts[me] = len(gives)
+    return np.concatenate([table.reshape(2 * chips, -1), counts], 1)
 
 
 def encode_kernel(res_ref, weight_ref, bias_ref, active_ref, out_ref):
@@ -76,17 +79,18 @@
 def encode(residual, enc_weight, bias, active, start, rows):
     layers, _, width = residual.shape
     own = enc_weight.shape[2]
-    at = start // rows
+    block = math.gcd(start, rows)
+    at = start // block
     return pl.pallas_call(
         encode_kernel,
-        grid=(layers,),
+        grid=(layers, rows // block),
         in_specs=[
-            pl.BlockSpec((1, rows, width), lambda s: (s, at, 0)),
-            pl.BlockSpec((1, width, own), lambda s: (s, 0, 0)),
-            pl.BlockSpec((layers, own), lambda s: (0, 0)),
-            pl.BlockSpec((1, rows, own), lambda s: (s, at, 0)),
+            pl.BlockSpec((1, block, width), lambda s, r: (s, at + r, 0)),
+            pl.BlockSpec((1, width, own), lambda s, r: (s, 0, 0)),
+            pl.BlockSpec((layers, own), lambda s, r: (0, 0)),
+            pl.BlockSpec((1, block, own), lambda s, r: (s, at + r, 0)),
         ],
-        out_specs=pl.BlockSpec((1, rows, own), lambda s: (s, 0, 0)),
+        out_specs=pl.BlockSpec((1, block, own), lambda s, r: (s, r, 0)),
         out_shape=jax.ShapeDtypeStruct((layers, rows, own), BF16),
         compiler_params=params(VMEM_MIB),
         cost_estimate=LIGHT,
@@ -342,36 +346,41 @@
 
 
 def enc_grad_kernel(parts, res_ref, *refs):
-    last_ref, active_ref, out_ref, bias_ref = refs[parts:]
-    last = (last_ref[0].astype(F32) * active_ref[0].astype(F32)).astype(BF16)
-    whole = jnp.concatenate([part[0] for part in refs[:parts]] + [last], 0)
-    out_ref[0] = dot(res_ref[0], whole).astype(BF16)
-    bias_ref[pl.ds(pl.program_id(0), 1)] = jnp.sum(whole.astype(F32), axis=0, keepdims=True)
+    last_ref, active_ref, out_ref, bias_ref, whole = refs[parts:]
+
+    @pl.when(pl.program_id(1) == 0)
+    def _():
+        last = (last_ref[0].astype(F32) * active_ref[...].astype(F32)).astype(BF16)
+        value = jnp.concatenate([part[0] for part in refs[:parts]] + [last], 0)
+        whole[...] = value
+        bias_ref[pl.ds(pl.program_id(0), 1)] = jnp.sum(value.astype(F32), axis=0, keepdims=True)
+
+    out_ref[0] = dot(res_ref[0], whole[...]).astype(BF16)
 
 
 def encoder_grad(residual_t, grads, last, active, start):
     layers, width, tok = residual_t.shape
     _, rows, own = last.shape
-    at = start // rows
-    part = lambda value: pl.BlockSpec((1,) + value.shape[1:], lambda s: (s, 0, 0))
+    part = lambda value: pl.BlockSpec((1,) + value.shape[1:], lambda s, w: (s, 0, 0))
     return pl.pallas_call(
         functools.partial(enc_grad_kernel, len(grads)),
-        grid=(layers,),
-        in_specs=[part(residual_t)]
+        grid=(layers, 1),
+        in_specs=[pl.BlockSpec((1, width, tok), lambda s, w: (s, w, 0))]
         + [part(g) for g in grads]
-        + [part(last), pl.BlockSpec((1, rows, own), lambda s: (s, at, 0))],
+        + [part(last), pl.BlockSpec((pl.Squeezed(), rows, own), lambda s, w: (s, 0, 0))],
         out_specs=[
-            pl.BlockSpec((1, width, own), lambda s: (s, 0, 0)),
-            pl.BlockSpec((layers, own), lambda s: (0, 0)),
+            pl.BlockSpec((1, width, own), lambda s, w: (s, w, 0)),
+            pl.BlockSpec((layers, own), lambda s, w: (0, 0)),
         ],
         out_shape=(
             jax.ShapeDtypeStruct((layers, width, own), BF16),
             jax.ShapeDtypeStruct((layers, own), F32),
         ),
-        compiler_params=params(24),
+        scratch_shapes=[pltpu.VMEM((tok, own), BF16)],
+        compiler_params=params(VMEM_MIB),
         cost_estimate=LIGHT,
         name="enc_grad",
-    )(residual_t, *grads, last, active)
+    )(residual_t, *grads, last, active[:, start : start + rows])
 
 
 def swap_cores(value, devices):
@@ -408,7 +417,7 @@
 
 
 def token_chunks(tok):
-    parts = [4, 2, 2]
+    parts = [2, 3, 3]
     unit = tok // sum(parts)
     return [(unit * sum(parts[:i]), unit * part) for i, part in enumerate(parts)]
 
@@ -418,14 +427,13 @@
     own = enc_weight.shape[2]
     chips = devices // 2
     chunks = token_chunks(tok)
+    hopping = 1
     pairs = np.array(pair_list(layers), np.int32)
     me = lax.axis_index("tgt")
 
     same = jnp.all(tile_pairs[None, :, :] == pairs[:, None, :], axis=2)
     perm = jnp.sum(jnp.where(same, jnp.arange(len(pairs), dtype=jnp.int32)[None, :], 0), axis=1, dtype=jnp.int32)
-    chip, core = me // 2, me % 2
-    gives = 1 + 2 * jnp.where(core == 0, chip, chips - 1 - chip)
-    scatter_meta = jnp.concatenate([perm, jnp.asarray(scatter_table(chips))[me], gives[None].astype(jnp.int32)])
+    scatter_meta = jnp.concatenate([perm, jnp.asarray(scatter_table(chips))[me]])
     dec_bias3 = dec_bias[:, :, None]
     residual_t = jnp.swapaxes(residual, 1, 2)
     bits = [b for b in range(blocks.bit_length()) if (1 << b) < blocks]
@@ -434,17 +442,13 @@
         early, rest, keep = slots
         early, rest = swap_cores(early, devices), swap_cores(rest, devices)
         last = 2 * (chips - 1)
-        gate, carry = [], None
+        sent, carry = [], None
         for j in range(1, chips):
             at = slice(2 * (j - 1), 2 * j)
             terms = [keep[at], early if j == 1 else rest[2 * j - 4 : 2 * j - 2]]
-            terms += [] if carry is None else [after(carry, *gate)]
-            carry = hop(add(*terms), chips, range(0, j))
-            gate = yield carry
-            gate = gate or []
-        total = add(keep[last], rest[last - 2], carry[0], swap_cores(carry[1], devices))
-        while True:
-            yield total
+            sent.append(add(*terms, *([] if carry is None else [carry])))
+            carry = hop(sent[-1], chips, range(0, j))
+        return sent, add(keep[last], rest[last - 2], carry[0], swap_cores(carry[1], devices))
 
     order, lats, parts = [], [], []
     for start, rows in chunks:
@@ -452,34 +456,29 @@
         order = [block]
         lats.append(lax.all_gather(block, "tgt", axis=0))
         parts.append(targets[:, :, start : start + rows])
-    order += [residual_t] + parts
-
-    errors, running = [], []
-    final = len(chunks) - 1
-    for c in range(final + 1):
-        order += [next(steps) for steps in running[: max(c - 1, 0)]]
-        low, high = recon(perm, dec_weight, after(lats[c], *order))
-        order = [low, high]
-        order += [next(steps) for steps in running[: c if c == final else max(c - 1, 0)]]
+    order += [residual_t, scatter_meta, dec_bias3] + parts
+
+    errors, chains, totals = [], [], []
+    for c in range(len(chunks)):
+        stage = lambda ahead: [sent[min(2 * (c - i) - ahead, len(sent)) - 1] for i, (sent, _) in enumerate(chains)]
+        low, high = recon(perm, dec_weight, after(lats[c], *order, *stage(1)))
+        order = [low, high] + stage(0)
         low = sum_over_src(low, blocks, bits)
         high = sum_over_src(high, blocks, bits[::-1])
-        *slots, error = grad(scatter_meta, dec_weight, after(low, *order), high, dec_bias3, parts[c], own, c < final)
+        split = c < hopping
+        *slots, error = grad(scatter_meta, dec_weight, after(low, *order), high, dec_bias3, parts[c], own, split)
         errors.append(error)
         order = [error]
-        if c < final:
-            running.append(scatter(slots))
-    last = lax.psum_scatter(slots[0], "tgt", scatter_dimension=0)
-    values = [next(steps, None) for steps in running]
+        if split:
+            chains.append(scatter(slots))
+            totals.append(chains[-1][1])
+        else:
+            totals.append(lax.psum_scatter(slots[0], "tgt", scatter_dimension=0))
     dec_grad = decoder_grad(after(perm, *order), errors, lats)
     grads = []
-    for c, (steps, value) in enumerate(zip(running, values)):
-        if value.ndim == 4:
-            value = steps.send([dec_grad])
-        while value.ndim == 4:
-            value = next(steps)
-        start, rows = chunks[c]
-        grads.append((value.astype(F32) * active[:, start : start + rows].astype(F32)).astype(BF16))
-    last = after(last, dec_grad)
+    for total, (start, rows) in zip(totals[:-1], chunks):
+        grads.append((total.astype(F32) * active[:, start : start + rows].astype(F32)).astype(BF16))
+    last = after(totals[-1], dec_grad, *grads)
     enc_grad, bias_grad = encoder_grad(residual_t, grads, last, active, chunks[-1][0])
     return (dec_grad, enc_grad, bias_grad)
 

time: 395 us -> 363 us (0.919)
  waiting for transfers between devices: 136 us -> 107 us
  Pallas kernels: 150 us -> 166 us
  other arithmetic: 31.3 us -> 22.8 us
  starting transfers between devices: 36.8 us -> 32.7 us
  local copies, waits for them, and re-layouts: 23.4 us -> 19.4 us
    all_gather x3, waiting for transfers between devices: 54.3 us -> 13.8 us  [shards(): lats.append(lax.all_gather(block, 'tgt', axis=0))]
    reduce_scatter x1 -> x2, waiting for transfers between devices: 0.02 us -> 30.5 us  [shards(): totals.append(lax.psum_scatter(slots[0], 'tgt', scatter_dimension=0))]
    ppermute x6 -> x3, waiting for transfers between devices: 40.5 us -> 27.7 us  [hop(): return lax.ppermute(value, 'tgt', perm)]
    ppermute x6 -> x3, waiting for transfers between devices: 18.5 us -> 6.37 us  [swap_cores(): return lax.ppermute(value, 'tgt', [(i, i ^ 1) for i in range(devices)])]
    pallas_call x3, Pallas kernels: 23.8 us -> 33.6 us  [encode(): pl.pallas_call(encode_kernel, grid=(layers, rows // block), in_specs=[pl....]
    convert_element_type x18 -> x15, other arithmetic: 26.2 us -> 16.7 us  [add(): return total.astype(BF16)]
    ppermute x6 -> x3, starting transfers between devices: 20.7 us -> 12.5 us  [hop(): return lax.ppermute(value, 'tgt', perm)]
    unnamed x23 -> x15, local copies, waits for them, and re-layouts: 19.7 us -> 12.8 us
  transfers between devices with their start and end apart: 28 -> 23, of which waited for: 17 -> 16; matrix products, arithmetic and copies ran while one was open for 12% -> 12% of each run, Pallas kernels for 31% -> 41%
where the time goes in v3:
time: 363 us; the launch traced here: 361 us
  Pallas kernels  166 us (46%)
  waiting for transfers between devices  107 us (29%)
  starting transfers between devices  32.7 us (9%)
  other arithmetic  22.8 us (6%)
  local copies, waits for them, and re-layouts  19.4 us (5%)
  between operations  13.9 us (4%)
    pallas_call x3, Pallas kernels, grad(): pl.pallas_call(functools.partial(grad_kernel, pairs, layers, split), grid...  48.8 us
    pallas_call x3, Pallas kernels, recon(): pl.pallas_call(body, grid_spec=pltpu.PrefetchScalarGridSpec(num_scalar_pr...  47.4 us
    pallas_call x3, Pallas kernels, encode(): pl.pallas_call(encode_kernel, grid=(layers, rows // block), in_specs=[pl....  33.6 us
    reduce_scatter x2, waiting for transfers between devices, shards(): totals.append(lax.psum_scatter(slots[0], 'tgt', scatter_dimension=0))  30.5 us
    ppermute x12, waiting for transfers between devices, sum_over_src(): lax.ppermute(value, 'src', [(i, i ^ 1 << bit) for i in range(size)])  28.3 us
    ppermute x3, waiting for transfers between devices, hop(): return lax.ppermute(value, 'tgt', perm)  27.7 us
    pallas_call x1, Pallas kernels, decoder_grad(): pl.pallas_call(functools.partial(dec_grad_kernel, pairs, len(errors)), gr...  24.7 us
    ppermute x12, starting transfers between devices, sum_over_src(): lax.ppermute(value, 'src', [(i, i ^ 1 << bit) for i in range(size)])  18 us
  transfers between devices with their start and end apart: 23, of which 16 were waited for; matrix products, arithmetic and copies ran while one was open for 12% of the time, Pallas kernels for 41%

profile of v3, /device:TPU:0, one launch (start us, length us, event | category | flops | bytes accessed | tf_op | source)
XLA Modules:
  0.0 361.3 jit_solution(12542640398223724879)
XLA Ops:
  7.2 7.1 %encode.3 = bf16[4,128,512]{2,1,0:T(8,128)(2,1)} custom-call(bf16[4,512,2304]{2,1,0:T(8,128)(2,1)} %res_ref.2, bf16[4,2304,512]{2,1,0:T(8,128)(2,1)} %weight_ref.5, f32[4,512]{1,0:T(4,128)} %bias_ref.5, s32[4,512,512]{2,1,0:T(8,128)} %active_ref.5), custom_call_target="tpu_custom_call" | custom-call | flops 1 | bytes 1 | tf_op jit(solution)/shard_map/encode/pallas_call | solution.py:84
  14.4 13.3 %encode.4 = bf16[4,192,512]{2,1,0:T(8,128)(2,1)} custom-call(bf16[4,512,2304]{2,1,0:T(8,128)(2,1)} %res_ref.2, bf16[4,2304,512]{2,1,0:T(8,128)(2,1)} %weight_ref.5, f32[4,512]{1,0:T(4,128)} %bias_ref.5, s32[4,512,512]{2,1,0:T(8,128)} %active_ref.5), custom_call_target="tpu_custom_call" | custom-call | flops 1 | bytes 1 | tf_op jit(solution)/shard_map/encode/pallas_call | solution.py:84
  27.8 13.1 %encode.5 = bf16[4,192,512]{2,1,0:T(8,128)(2,1)} custom-call(bf16[4,512,2304]{2,1,0:T(8,128)(2,1)} %res_ref.2, bf16[4,2304,512]{2,1,0:T(8,128)(2,1)} %weight_ref.5, f32[4,512]{1,0:T(4,128)} %bias_ref.5, s32[4,512,512]{2,1,0:T(8,128)} %active_ref.5), custom_call_target="tpu_custom_call" | custom-call | flops 1 | bytes 1 | tf_op jit(solution)/shard_map/encode/pallas_call | solution.py:84
  41.1 12.8 %copy.25 = bf16[4,512,2304]{1,2,0:T(8,128)(2,1)} copy(bf16[4,512,2304]{2,1,0:T(8,128)(2,1)} %res_ref.2) | data formatting | bytes 18874368 | tf_op args[0]
  57.4 7.0 %all-gather.11.cloned.1.call-done = bf16[32,128,512]{2,1,0:T(8,128)(2,1)} async-done(((bf16[4,128,512]{2,1,0:T(8,128)(2,1)}), bf16[32,128,512]{2,1,0:T(8,128)(2,1)}) %all-gather.11.cloned.1.call-update) | async-done | bytes 4194320 | tf_op jit(solution)/shard_map/all_gather | solution.py:457
  64.4 15.5 %recon.3 = (bf16[2,288,128]{2,1,0:T(8,128)(2,1)}, bf16[2,288,128]{2,1,0:T(8,128)(2,1)}) custom-call(s32[10]{0:T(128)} %copy-done.3, bf16[10,288,4096]{2,1,0:T(8,128)(2,1)} %refs_9_.11, bf16[10,288,4096]{2,1,0:T(8,128)(2,1)} %refs_9_.11, bf16[10,288,4096]{2,1,0:T(8,128)(2,1)} %refs_9_.11, bf16[10,288,4096]{2,1,0:T(8,128)(2,1)} %refs_9_.11, ...), custom_call_target="tpu_custom_call" | custom-call | flops 1 | bytes 1 | tf_op jit(solution)/shard_map/recon/pallas_call | solution.py:201
  79.9 1.3 collective-permute-start
  82.3 1.4 collective-permute-start.2
  83.7 2.5 collective-permute-done
  87.1 1.4 collective-permute-start.1
  89.4 1.5 collective-permute-start.3
  90.9 1.5 collective-permute-done.1
  93.1 1.5 collective-permute-done.3
  95.3 15.5 %latent_grad.3 = (bf16[2,4,128,512]{3,2,1,0:T(8,128)(2,1)}, bf16[5,4,128,512]{3,2,1,0:T(8,128)(2,1)}, bf16[7,4,128,512]{3,2,1,0:T(8,128)(2,1)}, bf16[4,288,128]{2,1,0:T(8,128)(2,1)}) custom-call(s32[35]{0:T(128)} %pad_add_fusion.meta, bf16[10,288,4096]{2,1,0:T(8,128)(2,1)} %refs_9_.11, bf16[10,288,4096]{2,1,0:T(8,128)(2,1)} %refs_9_.11, ...), custom_call_target="tpu_custom_call" | custom-call | flops 1 | bytes 1 | tf_op jit(solution)/shard_map/latent_grad/pallas_call | solution.py:292
  111.4 6.4 %collective-permute-done.4 = bf16[2,4,128,512]{3,2,1,0:T(8,128)(2,1)S(1)} collective-permute-done((bf16[2,4,128,512]{3,2,1,0:T(8,128)(2,1)}, bf16[2,4,128,512]{3,2,1,0:T(8,128)(2,1)S(1)}, u32[]{:S(2)}, u32[]{:S(2)}) %collective-permute-start.4) | collective-permute-done | bytes 1048608 | tf_op jit(solution)/shard_map/ppermute | solution.py:387
  117.8 2.5 add_convert_fusion.2
  120.3 2.7 collective-permute-start.8
  123.0 6.8 %all-gather.9.cloned.1.call-done = bf16[32,192,512]{2,1,0:T(8,128)(2,1)} async-done(((bf16[4,192,512]{2,1,0:T(8,128)(2,1)}), bf16[32,192,512]{2,1,0:T(8,128)(2,1)}) %all-gather.9.cloned.1.call-update) | async-done | bytes 6291472 | tf_op jit(solution)/shard_map/all_gather | solution.py:457
  129.8 15.8 %recon.4 = (bf16[2,288,192]{2,1,0:T(8,128)(2,1)}, bf16[2,288,192]{2,1,0:T(8,128)(2,1)}) custom-call(s32[10]{0:T(128)} %copy-done.3, bf16[10,288,4096]{2,1,0:T(8,128)(2,1)} %refs_9_.11, bf16[10,288,4096]{2,1,0:T(8,128)(2,1)} %refs_9_.11, bf16[10,288,4096]{2,1,0:T(8,128)(2,1)} %refs_9_.11, bf16[10,288,4096]{2,1,0:T(8,128)(2,1)} %refs_9_.11, ...), custom_call_target="tpu_custom_call" | custom-call | flops 1 | bytes 1 | tf_op jit(solution)/shard_map/recon/pallas_call | solution.py:201
  145.6 1.6 collective-permute-start.5
  147.2 2.9 add_convert_fusion.1
  150.1 1.5 collective-permute-start.9
  151.6 3.4 collective-permute-done.5
  155.1 1.6 collective-permute-start.6
  156.7 3.3 collective-permute-done.9
  160.3 5.0 %collective-permute-done.6 = bf16[2,288,192]{2,1,0:T(8,128)(2,1)S(1)} collective-permute-done((bf16[2,288,192]{2,1,0:T(8,128)(2,1)S(1)}, bf16[2,288,192]{2,1,0:T(8,128)(2,1)S(1)}, u32[]{:S(2)}, u32[]{:S(2)}) %collective-permute-start.6) | collective-permute-done | bytes 221216 | tf_op jit(solution)/shard_map/ppermute | solution.py:415
  168.0 16.5 %latent_grad.4 = (bf16[8,4,192,512]{3,2,1,0:T(8,128)(2,1)}, bf16[4,288,192]{2,1,0:T(8,128)(2,1)}) custom-call(s32[35]{0:T(128)} %pad_add_fusion.meta, bf16[10,288,4096]{2,1,0:T(8,128)(2,1)} %refs_9_.11, bf16[10,288,4096]{2,1,0:T(8,128)(2,1)} %refs_9_.11, bf16[10,288,4096]{2,1,0:T(8,128)(2,1)} %refs_9_.11, bf16[10,288,4096]{2,1,0:T(8,128)(2,1)} %refs_9_.11, ...), custom_call_target="tpu_custom_call" | custom-call | flops 1 | bytes 1 | tf_op jit(solution)/shard_map/latent_grad/pallas_call | solution.py:292
  184.6 3.4 collective-permute-start.11
  188.0 15.1 %collective-permute-done.11 = bf16[2,4,128,512]{3,2,1,0:T(8,128)(2,1)S(1)} collective-permute-done((bf16[2,4,128,512]{3,2,1,0:T(8,128)(2,1)}, bf16[2,4,128,512]{3,2,1,0:T(8,128)(2,1)S(1)}, u32[]{:S(2)}, u32[]{:S(2)}) %collective-permute-start.11) | collective-permute-done | bytes 1048608 | tf_op jit(solution)/shard_map/ppermute | solution.py:397
  203.1 2.6 add_convert_fusion
  205.7 16.1 %recon.5 = (bf16[2,288,192]{2,1,0:T(8,128)(2,1)}, bf16[2,288,192]{2,1,0:T(8,128)(2,1)}) custom-call(s32[10]{0:T(128)} %copy-done.3, bf16[10,288,4096]{2,1,0:T(8,128)(2,1)} %refs_9_.11, bf16[10,288,4096]{2,1,0:T(8,128)(2,1)} %refs_9_.11, bf16[10,288,4096]{2,1,0:T(8,128)(2,1)} %refs_9_.11, bf16[10,288,4096]{2,1,0:T(8,128)(2,1)} %refs_9_.11, ...), custom_call_target="tpu_custom_call" | custom-call | flops 1 | bytes 1 | tf_op jit(solution)/shard_map/recon/pallas_call | solution.py:201
  221.9 1.6 collective-permute-start.12
  223.5 1.5 collective-permute-start.14
  225.0 5.3 %collective-permute-done.12 = bf16[2,288,192]{2,1,0:T(8,128)(2,1)S(1)} collective-permute-done((bf16[2,288,192]{2,1,0:T(8,128)(2,1)}, bf16[2,288,192]{2,1,0:T(8,128)(2,1)S(1)}, u32[]{:S(2)}, u32[]{:S(2)}) %collective-permute-start.12) | collective-permute-done | bytes 221216 | tf_op jit(solution)/shard_map/ppermute | solution.py:415
  231.3 3.1 collective-permute-start.13
  235.5 1.3 collective-permute-start.15
  236.8 2.3 collective-permute-done.13
  239.9 2.3 collective-permute-done.15
  243.0 16.8 %latent_grad.5 = (bf16[8,4,192,512]{3,2,1,0:T(8,128)(2,1)}, bf16[4,288,192]{2,1,0:T(8,128)(2,1)}) custom-call(s32[35]{0:T(128)} %pad_add_fusion.meta, bf16[10,288,4096]{2,1,0:T(8,128)(2,1)} %refs_9_.11, bf16[10,288,4096]{2,1,0:T(8,128)(2,1)} %refs_9_.11, bf16[10,288,4096]{2,1,0:T(8,128)(2,1)} %refs_9_.11, bf16[10,288,4096]{2,1,0:T(8,128)(2,1)} %refs_9_.11, ...), custom_call_target="tpu_custom_call" | custom-call | flops 1 | bytes 1 | tf_op jit(solution)/shard_map/latent_grad/pallas_call | solution.py:292
  259.8 6.4 %collective-permute-start.16 = (bf16[2,4,128,512]{3,2,1,0:T(8,128)(2,1)}, bf16[2,4,128,512]{3,2,1,0:T(8,128)(2,1)S(1)}, u32[]{:S(2)}, u32[]{:S(2)}) collective-permute-start(bf16[2,4,128,512]{3,2,1,0:T(8,128)(2,1)} %add_convert_fusion), channel_id=1, source_target_pairs={{0,2},{7,5},{2,4},{5,3},{4,6},{3,1},{8,10},{15,13},{10,12},{13,11}... | collective-permute-start | bytes 3145736 | tf_op jit(solution)/shard_map/ppermute | solution.py:397
  266.3 12.5 %collective-permute-done.16 = bf16[2,4,128,512]{3,2,1,0:T(8,128)(2,1)S(1)} collective-permute-done((bf16[2,4,128,512]{3,2,1,0:T(8,128)(2,1)}, bf16[2,4,128,512]{3,2,1,0:T(8,128)(2,1)S(1)}, u32[]{:S(2)}, u32[]{:S(2)}) %collective-permute-start.16) | collective-permute-done | bytes 1048608 | tf_op jit(solution)/shard_map/ppermute | solution.py:397
  278.8 1.5 collective-permute-start.17
  280.3 2.7 slice.59.refs_3_
  283.0 24.7 %dec_grad.1 = bf16[10,288,4096]{2,1,0:T(8,128)(2,1)} custom-call(s32[10]{0:T(128)} %copy-done.3, bf16[4,288,128]{2,1,0:T(8,128)(2,1)} %get-tuple-element.35.refs_0_, bf16[4,288,192]{2,1,0:T(8,128)(2,1)} %get-tuple-element.43.refs_1_, bf16[4,288,192]{2,1,0:T(8,128)(2,1)} %get-tuple-element.48.refs_2_, bf16[8,4,128,512]{3,2,1,0:T(8,128)(2,1)} %bitcast.25, ...), custom_call_target="tpu_custom_call" | custom-call | flops 1 | bytes 1 | tf_op jit(solution)/shard_map/dec_grad/pallas_call | solution.py:332
  307.7 2.6 multiply_convert_fusion.refs_0_
  310.3 2.8 fusion.refs_1_
  313.1 30.5 %reduce-scatter.5.cloned.1.call-done = bf16[1,4,192,512]{3,2,1,0:T(8,128)(2,1)} async-done(((bf16[8,4,192,512]{3,2,1,0:T(8,128)(2,1)}), bf16[1,4,192,512]{3,2,1,0:T(8,128)(2,1)}) %reduce-scatter.5.cloned.1.call-update) | async-done | bytes 786448 | tf_op jit(solution)/shard_map/reduce_scatter | solution.py:476
  343.6 11.2 %enc_grad.1 = (bf16[4,2304,512]{2,1,0:T(8,128)(2,1)}, f32[4,512]{1,0:T(4,128)}) custom-call(bf16[4,2304,512]{2,1,0:T(8,128)(2,1)} %bitcast.19, bf16[4,128,512]{2,1,0:T(8,128)(2,1)} %multiply_convert_fusion.refs_0_, bf16[4,192,512]{2,1,0:T(8,128)(2,1)} %fusion.refs_1_, bf16[4,192,512]{2,1,0:T(8,128)(2,1)} %bitcast.26, s32[4,192,512]{2,1,0:T(8,128)} %slice.59.refs_3_), custom_call_target="tpu_custom_call" | custom-call | flops 1 | bytes 1 | tf_op jit(solution)/shard_map/enc_grad/pallas_call | solution.py:365
  (55 shorter events, 15.6 us)
Async XLA Ops:
  7.2 57.2 %all-gather.11.cloned.1.call-start = ((), (), s32[]{:S(2)}) async-start(), calls=%async_computation.6 | async-start | bytes 4718592 | tf_op jit(solution)/shard_map/all_gather | solution.py:457
  14.4 115.4 %all-gather.9.cloned.1.call-start = ((), (), s32[]{:S(2)}) async-start(), calls=%async_computation.5 | async-start | bytes 7077888 | tf_op jit(solution)/shard_map/all_gather | solution.py:457
  27.8 178.0 %all-gather.7.cloned.1.call-start = ((), (), s32[]{:S(2)}) async-start(), calls=%async_computation.4 | async-start | bytes 7077888 | tf_op jit(solution)/shard_map/all_gather | solution.py:457
  41.0 269.3 %reduce-scatter.3.cloned.1.call-start = ((), (), s32[]{:S(2)}) async-start(), calls=%async_computation.2 | async-start | bytes 7077888 | tf_op jit(solution)/shard_map/reduce_scatter | solution.py:476
  41.0 12.8 %copy-start = (bf16[4,288,512]{2,1,0:T(8,128)(2,1)S(1)}, bf16[4,288,512]{2,1,0:T(8,128)(2,1)}, u32[]{:S(2)}) copy-start(bf16[4,288,512]{2,1,0:T(8,128)(2,1)} %param.11) | copy-start | bytes 3538948
  41.1 14.3 %copy-start.5 = (s32[10,2]{0,1:T(2,128)S(1)}, s32[10,2]{0,1:T(2,128)}, u32[]{:S(2)}) copy-start(s32[10,2]{0,1:T(2,128)} %param.17) | copy-start | bytes 244
  41.1 14.2 %copy-start.6 = (s32[10,2]{0,1:T(2,128)S(1)}, s32[10,2]{0,1:T(2,128)}, u32[]{:S(2)}) copy-start(s32[10,2]{0,1:T(2,128)} %constant.18) | copy-start | bytes 244
  55.5 8.9 %copy-start.3 = (s32[10]{0:T(128)}, s32[10]{0:T(128)S(1)}, u32[]{:S(2)}) copy-start(s32[10]{0:T(128)S(1)} %select_reduce_fusion.meta.perm) | copy-start | bytes 124
  64.4 16.8 %copy-start.4 = (f32[4,288]{1,0:T(4,128)S(1)}, f32[4,288]{1,0:T(4,128)}, u32[]{:S(2)}) copy-start(f32[4,288]{1,0:T(4,128)} %param.16) | copy-start | bytes 13828
  79.9 6.2 %collective-permute-start = (bf16[2,288,128]{2,1,0:T(8,128)(2,1)}, bf16[2,288,128]{2,1,0:T(8,128)(2,1)S(1)}, u32[]{:S(2)}, u32[]{:S(2)}) collective-permute-start(bf16[2,288,128]{2,1,0:T(8,128)(2,1)} %get-tuple-element.32), channel_id=1, source_target_pairs={{0,8},{8,0},{16,24},{24,16},{1,9},{9,1},{17,25},{25,17},{2,10},{10... | collective-permute-start | bytes 442376 | tf_op jit(solution)/shard_map/ppermute | solution.py:415
  82.3 6.2 %collective-permute-start.2 = (bf16[2,288,128]{2,1,0:T(8,128)(2,1)}, bf16[2,288,128]{2,1,0:T(8,128)(2,1)S(1)}, u32[]{:S(2)}, u32[]{:S(2)}) collective-permute-start(bf16[2,288,128]{2,1,0:T(8,128)(2,1)} %get-tuple-element.33), channel_id=1, source_target_pairs={{0,16},{8,24},{16,0},{24,8},{1,17},{9,25},{17,1},{25,9},{2,18},{10... | collective-permute-start | bytes 442376 | tf_op jit(solution)/shard_map/ppermute | solution.py:415
  87.1 5.3 %collective-permute-start.1 = (bf16[2,288,128]{2,1,0:T(8,128)(2,1)S(1)}, bf16[2,288,128]{2,1,0:T(8,128)(2,1)S(1)}, u32[]{:S(2)}, u32[]{:S(2)}) collective-permute-start(bf16[2,288,128]{2,1,0:T(8,128)(2,1)S(1)} %add_convert_fusion.14), channel_id=1, source_target_pairs={{0,16},{8,24},{16,0},{24,8},{1,17},{9,25},{17,1},{25,9},{2,18},{10... | collective-permute-start | bytes 442376 | tf_op jit(solution)/shard_map/ppermute | solution.py:415
  89.4 5.2 %collective-permute-start.3 = (bf16[2,288,128]{2,1,0:T(8,128)(2,1)S(1)}, bf16[2,288,128]{2,1,0:T(8,128)(2,1)S(1)}, u32[]{:S(2)}, u32[]{:S(2)}) collective-permute-start(bf16[2,288,128]{2,1,0:T(8,128)(2,1)S(1)} %add_convert_fusion.12), channel_id=1, source_target_pairs={{0,8},{8,0},{16,24},{24,16},{1,9},{9,1},{17,25},{25,17},{2,10},{10... | collective-permute-start | bytes 442376 | tf_op jit(solution)/shard_map/ppermute | solution.py:415
  110.8 36.3 %collective-permute-start.7 = (bf16[5,4,128,512]{3,2,1,0:T(8,128)(2,1)}, bf16[5,4,128,512]{3,2,1,0:T(8,128)(2,1)S(1)}, u32[]{:S(2)}, u32[]{:S(2)}) collective-permute-start(bf16[5,4,128,512]{3,2,1,0:T(8,128)(2,1)} %get-tuple-element.41), channel_id=1, source_target_pairs={{0,1},{1,0},{2,3},{3,2},{4,5},{5,4},{6,7},{7,6},{8,9},{9,8},{10,11... | collective-permute-start | bytes 7864328 | tf_op jit(solution)/shard_map/ppermute | solution.py:387
  110.9 6.9 %collective-permute-start.4 = (bf16[2,4,128,512]{3,2,1,0:T(8,128)(2,1)}, bf16[2,4,128,512]{3,2,1,0:T(8,128)(2,1)S(1)}, u32[]{:S(2)}, u32[]{:S(2)}) collective-permute-start(bf16[2,4,128,512]{3,2,1,0:T(8,128)(2,1)} %get-tuple-element.37), channel_id=1, source_target_pairs={{0,1},{1,0},{2,3},{3,2},{4,5},{5,4},{6,7},{7,6},{8,9},{9,8},{10,11... | collective-permute-start | bytes 3145736 | tf_op jit(solution)/shard_map/ppermute | solution.py:387
  120.3 26.9 %collective-permute-start.8 = (bf16[2,4,128,512]{3,2,1,0:T(8,128)(2,1)}, bf16[2,4,128,512]{3,2,1,0:T(8,128)(2,1)}, u32[]{:S(2)}, u32[]{:S(2)}) collective-permute-start(bf16[2,4,128,512]{3,2,1,0:T(8,128)(2,1)} %add_convert_fusion.2), channel_id=1, source_target_pairs={{0,2},{7,5},{8,10},{15,13},{16,18},{23,21},{24,26},{31,29}} | collective-permute-start | bytes 3145736 | tf_op jit(solution)/shard_map/ppermute | solution.py:397
  145.6 4.6 %copy-start.1 = (bf16[2,288,192]{2,1,0:T(8,128)(2,1)S(1)}, bf16[2,288,192]{2,1,0:T(8,128)(2,1)}, u32[]{:S(2)}) copy-start(bf16[2,288,192]{2,1,0:T(8,128)(2,1)} %get-tuple-element.40) | copy-start | bytes 663556
  145.6 9.4 %copy-start.2 = (bf16[2,288,192]{2,1,0:T(8,128)(2,1)S(1)}, bf16[2,288,192]{2,1,0:T(8,128)(2,1)}, u32[]{:S(2)}) copy-start(bf16[2,288,192]{2,1,0:T(8,128)(2,1)} %get-tuple-element.39) | copy-start | bytes 663556
  145.6 9.4 %collective-permute-start.5 = (bf16[2,288,192]{2,1,0:T(8,128)(2,1)}, bf16[2,288,192]{2,1,0:T(8,128)(2,1)S(1)}, u32[]{:S(2)}, u32[]{:S(2)}) collective-permute-start(bf16[2,288,192]{2,1,0:T(8,128)(2,1)} %get-tuple-element.39), channel_id=1, source_target_pairs={{0,8},{8,0},{16,24},{24,16},{1,9},{9,1},{17,25},{25,17},{2,10},{10... | collective-permute-start | bytes 663560 | tf_op jit(solution)/shard_map/ppermute | solution.py:415
  150.1 9.9 %collective-permute-start.9 = (bf16[2,288,192]{2,1,0:T(8,128)(2,1)S(1)}, bf16[2,288,192]{2,1,0:T(8,128)(2,1)S(1)}, u32[]{:S(2)}, u32[]{:S(2)}) collective-permute-start(bf16[2,288,192]{2,1,0:T(8,128)(2,1)S(1)} %copy-done.1), channel_id=1, source_target_pairs={{0,16},{8,24},{16,0},{24,8},{1,17},{9,25},{17,1},{25,9},{2,18},{10... | collective-permute-start | bytes 663560 | tf_op jit(solution)/shard_map/ppermute | solution.py:415
  155.1 10.2 %collective-permute-start.6 = (bf16[2,288,192]{2,1,0:T(8,128)(2,1)S(1)}, bf16[2,288,192]{2,1,0:T(8,128)(2,1)S(1)}, u32[]{:S(2)}, u32[]{:S(2)}) collective-permute-start(bf16[2,288,192]{2,1,0:T(8,128)(2,1)S(1)} %add_convert_fusion.10), channel_id=1, source_target_pairs={{0,16},{8,24},{16,0},{24,8},{1,17},{9,25},{17,1},{25,9},{2,18},{10... | collective-permute-start | bytes 663560 | tf_op jit(solution)/shard_map/ppermute | solution.py:415
  160.1 7.2 %collective-permute-start.10 = (bf16[2,288,192]{2,1,0:T(8,128)(2,1)S(1)}, bf16[2,288,192]{2,1,0:T(8,128)(2,1)S(1)}, u32[]{:S(2)}, u32[]{:S(2)}) collective-permute-start(bf16[2,288,192]{2,1,0:T(8,128)(2,1)S(1)} %add_convert_fusion.8), channel_id=1, source_target_pairs={{0,8},{8,0},{16,24},{24,16},{1,9},{9,1},{17,25},{25,17},{2,10},{10... | collective-permute-start | bytes 663560 | tf_op jit(solution)/shard_map/ppermute | solution.py:415
  184.6 159.0 %reduce-scatter.5.cloned.1.call-start = ((), (), s32[]{:S(2)}) async-start(), calls=%async_computation.3 | async-start | bytes 7077888 | tf_op jit(solution)/shard_map/reduce_scatter | solution.py:476
  184.6 18.5 %collective-permute-start.11 = (bf16[2,4,128,512]{3,2,1,0:T(8,128)(2,1)}, bf16[2,4,128,512]{3,2,1,0:T(8,128)(2,1)S(1)}, u32[]{:S(2)}, u32[]{:S(2)}) collective-permute-start(bf16[2,4,128,512]{3,2,1,0:T(8,128)(2,1)} %add_convert_fusion.1), channel_id=1, source_target_pairs={{0,2},{7,5},{2,4},{5,3},{8,10},{15,13},{10,12},{13,11},{16,18},{23... | collective-permute-start | bytes 3145736 | tf_op jit(solution)/shard_map/ppermute | solution.py:397
  221.9 8.4 %collective-permute-start.12 = (bf16[2,288,192]{2,1,0:T(8,128)(2,1)}, bf16[2,288,192]{2,1,0:T(8,128)(2,1)S(1)}, u32[]{:S(2)}, u32[]{:S(2)}) collective-permute-start(bf16[2,288,192]{2,1,0:T(8,128)(2,1)} %get-tuple-element.45), channel_id=1, source_target_pairs={{0,8},{8,0},{16,24},{24,16},{1,9},{9,1},{17,25},{25,17},{2,10},{10... | collective-permute-start | bytes 663560 | tf_op jit(solution)/shard_map/ppermute | solution.py:415
  223.5 10.9 %collective-permute-start.14 = (bf16[2,288,192]{2,1,0:T(8,128)(2,1)}, bf16[2,288,192]{2,1,0:T(8,128)(2,1)S(1)}, u32[]{:S(2)}, u32[]{:S(2)}) collective-permute-start(bf16[2,288,192]{2,1,0:T(8,128)(2,1)} %get-tuple-element.46), channel_id=1, source_target_pairs={{0,16},{8,24},{16,0},{24,8},{1,17},{9,25},{17,1},{25,9},{2,18},{10... | collective-permute-start | bytes 663560 | tf_op jit(solution)/shard_map/ppermute | solution.py:415
  231.3 7.8 %collective-permute-start.13 = (bf16[2,288,192]{2,1,0:T(8,128)(2,1)S(1)}, bf16[2,288,192]{2,1,0:T(8,128)(2,1)S(1)}, u32[]{:S(2)}, u32[]{:S(2)}) collective-permute-start(bf16[2,288,192]{2,1,0:T(8,128)(2,1)S(1)} %add_convert_fusion.6), channel_id=1, source_target_pairs={{0,16},{8,24},{16,0},{24,8},{1,17},{9,25},{17,1},{25,9},{2,18},{10... | collective-permute-start | bytes 663560 | tf_op jit(solution)/shard_map/ppermute | solution.py:415
  235.5 6.8 %collective-permute-start.15 = (bf16[2,288,192]{2,1,0:T(8,128)(2,1)S(1)}, bf16[2,288,192]{2,1,0:T(8,128)(2,1)S(1)}, u32[]{:S(2)}, u32[]{:S(2)}) collective-permute-start(bf16[2,288,192]{2,1,0:T(8,128)(2,1)S(1)} %add_convert_fusion.4), channel_id=1, source_target_pairs={{0,8},{8,0},{16,24},{24,16},{1,9},{9,1},{17,25},{25,17},{2,10},{10... | collective-permute-start | bytes 663560 | tf_op jit(solution)/shard_map/ppermute | solution.py:415
  259.8 19.0 %collective-permute-start.16 = (bf16[2,4,128,512]{3,2,1,0:T(8,128)(2,1)}, bf16[2,4,128,512]{3,2,1,0:T(8,128)(2,1)S(1)}, u32[]{:S(2)}, u32[]{:S(2)}) collective-permute-start(bf16[2,4,128,512]{3,2,1,0:T(8,128)(2,1)} %add_convert_fusion), channel_id=1, source_target_pairs={{0,2},{7,5},{2,4},{5,3},{4,6},{3,1},{8,10},{15,13},{10,12},{13,11}... | collective-permute-start | bytes 3145736 | tf_op jit(solution)/shard_map/ppermute | solution.py:397
  278.8 28.9 %collective-permute-start.17 = (bf16[4,128,512]{2,1,0:T(8,128)(2,1)S(1)}, bf16[4,128,512]{2,1,0:T(8,128)(2,1)S(1)}, u32[]{:S(2)}, u32[]{:S(2)}) collective-permute-start(bf16[4,128,512]{2,1,0:T(8,128)(2,1)S(1)} %slice_bitcast_fusion), channel_id=1, source_target_pairs={{0,1},{1,0},{2,3},{3,2},{4,5},{5,4},{6,7},{7,6},{8,9},{9,8},{10,11... | collective-permute-start | bytes 1572872 | tf_op jit(solution)/shard_map/ppermute | solution.py:387
Sparse Core Ops, SparseCore 0:
  14.5 49.8 all-gather.10
  66.0 63.6 all-gather.8
  131.4 67.3 all-gather.6
  201.6 71.3 reduce-scatter.2
  275.1 68.4 reduce-scatter.4

commit v4 on v3

--- a/solution.py
+++ b/solution.py
@@ -397,6 +397,12 @@
     return lax.ppermute(value, "tgt", perm)
 
 
+def far(value, chips, distance):
+    perm = [(2 * chip, 2 * (chip + distance)) for chip in range(chips - distance)]
+    perm += [(2 * chip + 1, 2 * (chip - distance) + 1) for chip in range(distance, chips)]
+    return lax.ppermute(value, "tgt", perm)
+
+
 def after(value, *others):
     return lax.optimization_barrier((value,) + others)[0]
 
@@ -442,13 +448,13 @@
         early, rest, keep = slots
         early, rest = swap_cores(early, devices), swap_cores(rest, devices)
         last = 2 * (chips - 1)
-        sent, carry = [], None
+        sent, come = [], []
         for j in range(1, chips):
             at = slice(2 * (j - 1), 2 * j)
-            terms = [keep[at], early if j == 1 else rest[2 * j - 4 : 2 * j - 2]]
-            sent.append(add(*terms, *([] if carry is None else [carry])))
-            carry = hop(sent[-1], chips, range(0, j))
-        return sent, add(keep[last], rest[last - 2], carry[0], swap_cores(carry[1], devices))
+            sent.append(add(keep[at], early if j == 1 else rest[2 * j - 4 : 2 * j - 2]))
+            come.append(far(sent[-1], chips, chips - j))
+        others = swap_cores(add(*[value[1] for value in come]), devices)
+        return sent, add(keep[last], rest[last - 2], others, *[value[0] for value in come])
 
     order, lats, parts = [], [], []
     for start, rows in chunks:
@@ -460,9 +466,8 @@
 
     errors, chains, totals = [], [], []
     for c in range(len(chunks)):
-        stage = lambda ahead: [sent[min(2 * (c - i) - ahead, len(sent)) - 1] for i, (sent, _) in enumerate(chains)]
-        low, high = recon(perm, dec_weight, after(lats[c], *order, *stage(1)))
-        order = [low, high] + stage(0)
+        low, high = recon(perm, dec_weight, after(lats[c], *order, *[sent[0] for sent, _ in chains]))
+        order = [low, high] + [value for sent, _ in chains for value in sent]
         low = sum_over_src(low, blocks, bits)
         high = sum_over_src(high, blocks, bits[::-1])
         split = c < hopping

time: 363 us -> 395 us (1.088)
  waiting for transfers between devices: 107 us -> 130 us
  starting transfers between devices: 32.7 us -> 39.9 us
    ppermute x3, waiting for transfers between devices: 27.7 us -> 70.6 us  [far(): return lax.ppermute(value, 'tgt', perm)]
    reduce_scatter x2, waiting for transfers between devices: 30.5 us -> 0.01 us  [shards(): totals.append(lax.psum_scatter(slots[0], 'tgt', scatter_dimension=0))]
    ppermute x3, starting transfers between devices: 2.06 us -> 14.6 us  [swap_cores(): return lax.ppermute(value, 'tgt', [(i, i ^ 1) for i in range(devices)])]
    all_gather x3, waiting for transfers between devices: 13.8 us -> 23.3 us  [shards(): lats.append(lax.all_gather(block, 'tgt', axis=0))]
    ppermute x3, starting transfers between devices: 12.5 us -> 6.69 us  [far(): return lax.ppermute(value, 'tgt', perm)]
    unnamed x15 -> x19, local copies, waits for them, and re-layouts: 12.8 us -> 15.4 us
    convert_element_type x15 -> x14, other arithmetic: 16.7 us -> 14.9 us  [add(): return total.astype(BF16)]
  transfers between devices with their start and end apart: 23 -> 23, of which waited for: 16 -> 16; matrix products, arithmetic and copies ran while one was open for 12% -> 10% of each run, Pallas kernels for 41% -> 38%
where the time goes in v4:
time: 395 us; the launch traced here: 393 us
  Pallas kernels  166 us (42%)
  waiting for transfers between devices  130 us (33%)
  starting transfers between devices  39.9 us (10%)
  local copies, waits for them, and re-layouts  21.9 us (6%)
  other arithmetic  21.4 us (5%)
  between operations  14 us (4%)
    ppermute x3, waiting for transfers between devices, far(): return lax.ppermute(value, 'tgt', perm)  70.6 us
    pallas_call x3, Pallas kernels, grad(): pl.pallas_call(functools.partial(grad_kernel, pairs, layers, split), grid...  49.2 us
    pallas_call x3, Pallas kernels, recon(): pl.pallas_call(body, grid_spec=pltpu.PrefetchScalarGridSpec(num_scalar_pr...  47 us
    pallas_call x3, Pallas kernels, encode(): pl.pallas_call(encode_kernel, grid=(layers, rows // block), in_specs=[pl....  33.6 us
    ppermute x12, waiting for transfers between devices, sum_over_src(): lax.ppermute(value, 'src', [(i, i ^ 1 << bit) for i in range(size)])  29.8 us
    pallas_call x1, Pallas kernels, decoder_grad(): pl.pallas_call(functools.partial(dec_grad_kernel, pairs, len(errors)), gr...  24.7 us
    all_gather x3, waiting for transfers between devices, shards(): lats.append(lax.all_gather(block, 'tgt', axis=0))  23.3 us
    ppermute x12, starting transfers between devices, sum_over_src(): lax.ppermute(value, 'src', [(i, i ^ 1 << bit) for i in range(size)])  18.1 us
  transfers between devices with their start and end apart: 23, of which 16 were waited for; matrix products, arithmetic and copies ran while one was open for 10% of the time, Pallas kernels for 38%

profile of v4, /device:TPU:0, one launch (start us, length us, event | category | flops | bytes accessed | tf_op | source)
XLA Modules:
  0.0 393.0 jit_solution(8817810575986748884)
XLA Ops:
  7.2 7.1 %encode.3 = bf16[4,128,512]{2,1,0:T(8,128)(2,1)} custom-call(bf16[4,512,2304]{2,1,0:T(8,128)(2,1)} %res_ref.2, bf16[4,2304,512]{2,1,0:T(8,128)(2,1)} %weight_ref.5, f32[4,512]{1,0:T(4,128)} %bias_ref.5, s32[4,512,512]{2,1,0:T(8,128)} %active_ref.5), custom_call_target="tpu_custom_call" | custom-call | flops 1 | bytes 1 | tf_op jit(solution)/shard_map/encode/pallas_call | solution.py:84
  14.4 13.3 %encode.4 = bf16[4,192,512]{2,1,0:T(8,128)(2,1)} custom-call(bf16[4,512,2304]{2,1,0:T(8,128)(2,1)} %res_ref.2, bf16[4,2304,512]{2,1,0:T(8,128)(2,1)} %weight_ref.5, f32[4,512]{1,0:T(4,128)} %bias_ref.5, s32[4,512,512]{2,1,0:T(8,128)} %active_ref.5), custom_call_target="tpu_custom_call" | custom-call | flops 1 | bytes 1 | tf_op jit(solution)/shard_map/encode/pallas_call | solution.py:84
  27.8 13.1 %encode.5 = bf16[4,192,512]{2,1,0:T(8,128)(2,1)} custom-call(bf16[4,512,2304]{2,1,0:T(8,128)(2,1)} %res_ref.2, bf16[4,2304,512]{2,1,0:T(8,128)(2,1)} %weight_ref.5, f32[4,512]{1,0:T(4,128)} %bias_ref.5, s32[4,512,512]{2,1,0:T(8,128)} %active_ref.5), custom_call_target="tpu_custom_call" | custom-call | flops 1 | bytes 1 | tf_op jit(solution)/shard_map/encode/pallas_call | solution.py:84
  41.0 12.7 %copy.25 = bf16[4,512,2304]{1,2,0:T(8,128)(2,1)} copy(bf16[4,512,2304]{2,1,0:T(8,128)(2,1)} %res_ref.2) | data formatting | bytes 18874368 | tf_op args[0]
  57.3 7.1 %all-gather.11.cloned.1.call-done = bf16[32,128,512]{2,1,0:T(8,128)(2,1)} async-done(((bf16[4,128,512]{2,1,0:T(8,128)(2,1)}), bf16[32,128,512]{2,1,0:T(8,128)(2,1)}) %all-gather.11.cloned.1.call-update) | async-done | bytes 4194320 | tf_op jit(solution)/shard_map/all_gather | solution.py:463
  64.4 15.5 %recon.3 = (bf16[2,288,128]{2,1,0:T(8,128)(2,1)}, bf16[2,288,128]{2,1,0:T(8,128)(2,1)}) custom-call(s32[10]{0:T(128)} %copy-done.5, bf16[10,288,4096]{2,1,0:T(8,128)(2,1)} %refs_9_.11, bf16[10,288,4096]{2,1,0:T(8,128)(2,1)} %refs_9_.11, bf16[10,288,4096]{2,1,0:T(8,128)(2,1)} %refs_9_.11, bf16[10,288,4096]{2,1,0:T(8,128)(2,1)} %refs_9_.11, ...), custom_call_target="tpu_custom_call" | custom-call | flops 1 | bytes 1 | tf_op jit(solution)/shard_map/recon/pallas_call | solution.py:201
  82.3 1.5 collective-permute-start.2
  83.8 2.4 collective-permute-done
  87.1 1.3 collective-permute-start.1
  89.4 1.6 collective-permute-start.3
  90.9 1.5 collective-permute-done.1
  93.1 1.5 collective-permute-done.3
  95.3 15.6 %latent_grad.3 = (bf16[2,4,128,512]{3,2,1,0:T(8,128)(2,1)}, bf16[5,4,128,512]{3,2,1,0:T(8,128)(2,1)}, bf16[7,4,128,512]{3,2,1,0:T(8,128)(2,1)}, bf16[4,288,128]{2,1,0:T(8,128)(2,1)}) custom-call(s32[35]{0:T(128)} %pad_add_fusion.meta, bf16[10,288,4096]{2,1,0:T(8,128)(2,1)} %refs_9_.11, bf16[10,288,4096]{2,1,0:T(8,128)(2,1)} %refs_9_.11, ...), custom_call_target="tpu_custom_call" | custom-call | flops 1 | bytes 1 | tf_op jit(solution)/shard_map/latent_grad/pallas_call | solution.py:292
  111.4 6.4 %collective-permute-done.4 = bf16[2,4,128,512]{3,2,1,0:T(8,128)(2,1)S(1)} collective-permute-done((bf16[2,4,128,512]{3,2,1,0:T(8,128)(2,1)}, bf16[2,4,128,512]{3,2,1,0:T(8,128)(2,1)S(1)}, u32[]{:S(2)}, u32[]{:S(2)}) %collective-permute-start.4) | collective-permute-done | bytes 1048608 | tf_op jit(solution)/shard_map/ppermute | solution.py:387
  117.8 1.5 copy-done
  119.3 4.1 %add_convert_fusion = (bf16[2,4,128,512]{3,2,1,0:T(8,128)(2,1)}, bf16[2,4,128,512]{3,2,1,0:T(8,128)(2,1)}, bf16[2,4,128,512]{3,2,1,0:T(8,128)(2,1)}) fusion(bf16[5,4,128,512]{3,2,1,0:T(8,128)(2,1)S(1)} %collective-permute-done.7, bf16[7,4,128,512]{3,2,1,0:T(8,128)(2,1)} %get-tuple-element.36, bf16[2,4,128,512]{3,2,1,0:T(8,128)(2,1)S(1)} %collective-permute-done.4), kind=kLoop, calls=%fused_computation | loop fusion | flops 6291456 | bytes 9437184 | tf_op jit(solution)/shard_map/convert_element_type | solution.py:414
  123.4 6.4 %all-gather.9.cloned.1.call-done = bf16[32,192,512]{2,1,0:T(8,128)(2,1)} async-done(((bf16[4,192,512]{2,1,0:T(8,128)(2,1)}), bf16[32,192,512]{2,1,0:T(8,128)(2,1)}) %all-gather.9.cloned.1.call-update) | async-done | bytes 6291472 | tf_op jit(solution)/shard_map/all_gather | solution.py:463
  129.8 16.0 %recon.4 = (bf16[2,288,192]{2,1,0:T(8,128)(2,1)}, bf16[2,288,192]{2,1,0:T(8,128)(2,1)}) custom-call(s32[10]{0:T(128)} %copy-done.5, bf16[10,288,4096]{2,1,0:T(8,128)(2,1)} %refs_9_.11, bf16[10,288,4096]{2,1,0:T(8,128)(2,1)} %refs_9_.11, bf16[10,288,4096]{2,1,0:T(8,128)(2,1)} %refs_9_.11, bf16[10,288,4096]{2,1,0:T(8,128)(2,1)} %refs_9_.11, ...), custom_call_target="tpu_custom_call" | custom-call | flops 1 | bytes 1 | tf_op jit(solution)/shard_map/recon/pallas_call | solution.py:201
  145.8 1.5 collective-permute-start.5
  147.3 1.5 collective-permute-start.8
  148.7 6.4 %collective-permute-done.5 = bf16[2,288,192]{2,1,0:T(8,128)(2,1)S(1)} collective-permute-done((bf16[2,288,192]{2,1,0:T(8,128)(2,1)}, bf16[2,288,192]{2,1,0:T(8,128)(2,1)S(1)}, u32[]{:S(2)}, u32[]{:S(2)}) %collective-permute-start.5) | collective-permute-done | bytes 221216 | tf_op jit(solution)/shard_map/ppermute | solution.py:421
  156.2 1.6 collective-permute-start.6
  158.8 1.5 collective-permute-start.9
  160.3 4.4 %collective-permute-done.6 = bf16[2,288,192]{2,1,0:T(8,128)(2,1)S(1)} collective-permute-done((bf16[2,288,192]{2,1,0:T(8,128)(2,1)S(1)}, bf16[2,288,192]{2,1,0:T(8,128)(2,1)S(1)}, u32[]{:S(2)}, u32[]{:S(2)}) %collective-permute-start.6) | collective-permute-done | bytes 221216 | tf_op jit(solution)/shard_map/ppermute | solution.py:421
  165.5 1.5 collective-permute-done.9
  167.8 16.9 %latent_grad.4 = (bf16[8,4,192,512]{3,2,1,0:T(8,128)(2,1)}, bf16[4,288,192]{2,1,0:T(8,128)(2,1)}) custom-call(s32[35]{0:T(128)} %pad_add_fusion.meta, bf16[10,288,4096]{2,1,0:T(8,128)(2,1)} %refs_9_.11, bf16[10,288,4096]{2,1,0:T(8,128)(2,1)} %refs_9_.11, bf16[10,288,4096]{2,1,0:T(8,128)(2,1)} %refs_9_.11, bf16[10,288,4096]{2,1,0:T(8,128)(2,1)} %refs_9_.11, ...), custom_call_target="tpu_custom_call" | custom-call | flops 1 | bytes 1 | tf_op jit(solution)/shard_map/latent_grad/pallas_call | solution.py:292
  185.0 9.9 %all-gather.7.cloned.1.call-done = bf16[32,192,512]{2,1,0:T(8,128)(2,1)} async-done(((bf16[4,192,512]{2,1,0:T(8,128)(2,1)}), bf16[32,192,512]{2,1,0:T(8,128)(2,1)}) %all-gather.7.cloned.1.call-update) | async-done | bytes 6291472 | tf_op jit(solution)/shard_map/all_gather | solution.py:463
  194.9 15.6 %recon.5 = (bf16[2,288,192]{2,1,0:T(8,128)(2,1)}, bf16[2,288,192]{2,1,0:T(8,128)(2,1)}) custom-call(s32[10]{0:T(128)} %copy-done.5, bf16[10,288,4096]{2,1,0:T(8,128)(2,1)} %refs_9_.11, bf16[10,288,4096]{2,1,0:T(8,128)(2,1)} %refs_9_.11, bf16[10,288,4096]{2,1,0:T(8,128)(2,1)} %refs_9_.11, bf16[10,288,4096]{2,1,0:T(8,128)(2,1)} %refs_9_.11, ...), custom_call_target="tpu_custom_call" | custom-call | flops 1 | bytes 1 | tf_op jit(solution)/shard_map/recon/pallas_call | solution.py:201
  210.4 1.7 collective-permute-start.10
  212.1 1.5 collective-permute-start.12
  213.6 6.2 %collective-permute-done.10 = bf16[2,288,192]{2,1,0:T(8,128)(2,1)S(1)} collective-permute-done((bf16[2,288,192]{2,1,0:T(8,128)(2,1)}, bf16[2,288,192]{2,1,0:T(8,128)(2,1)S(1)}, u32[]{:S(2)}, u32[]{:S(2)}) %collective-permute-start.10) | collective-permute-done | bytes 221216 | tf_op jit(solution)/shard_map/ppermute | solution.py:421
  220.9 1.7 collective-permute-start.11
  223.6 1.5 collective-permute-start.13
  225.1 4.3 %collective-permute-done.11 = bf16[2,288,192]{2,1,0:T(8,128)(2,1)S(1)} collective-permute-done((bf16[2,288,192]{2,1,0:T(8,128)(2,1)S(1)}, bf16[2,288,192]{2,1,0:T(8,128)(2,1)S(1)}, u32[]{:S(2)}, u32[]{:S(2)}) %collective-permute-start.11) | collective-permute-done | bytes 221216 | tf_op jit(solution)/shard_map/ppermute | solution.py:421
  230.2 1.6 collective-permute-done.13
  232.6 16.8 %latent_grad.5 = (bf16[8,4,192,512]{3,2,1,0:T(8,128)(2,1)}, bf16[4,288,192]{2,1,0:T(8,128)(2,1)}) custom-call(s32[35]{0:T(128)} %pad_add_fusion.meta, bf16[10,288,4096]{2,1,0:T(8,128)(2,1)} %refs_9_.11, bf16[10,288,4096]{2,1,0:T(8,128)(2,1)} %refs_9_.11, bf16[10,288,4096]{2,1,0:T(8,128)(2,1)} %refs_9_.11, bf16[10,288,4096]{2,1,0:T(8,128)(2,1)} %refs_9_.11, ...), custom_call_target="tpu_custom_call" | custom-call | flops 1 | bytes 1 | tf_op jit(solution)/shard_map/latent_grad/pallas_call | solution.py:292
  250.7 1.4 collective-permute-start.16
  252.0 4.0 %collective-permute-start.15 = (bf16[2,4,128,512]{3,2,1,0:T(8,128)(2,1)S(1)}, bf16[2,4,128,512]{3,2,1,0:T(8,128)(2,1)S(1)}, u32[]{:S(2)}, u32[]{:S(2)}) collective-permute-start(bf16[2,4,128,512]{3,2,1,0:T(8,128)(2,1)S(1)} %copy-done.3), channel_id=1, source_target_pairs={{0,4},{2,6},{5,1},{7,3},{8,12},{10,14},{13,9},{15,11},{16,20},{18,... | collective-permute-start | bytes 3145736 | tf_op jit(solution)/shard_map/ppermute | solution.py:403
  256.0 1.4 collective-permute-start.14
  257.4 14.9 %collective-permute-done.16 = bf16[2,4,128,512]{3,2,1,0:T(8,128)(2,1)S(1)} collective-permute-done((bf16[2,4,128,512]{3,2,1,0:T(8,128)(2,1)S(1)}, bf16[2,4,128,512]{3,2,1,0:T(8,128)(2,1)S(1)}, u32[]{:S(2)}, u32[]{:S(2)}) %collective-permute-start.16) | collective-permute-done | bytes 1048608 | tf_op jit(solution)/shard_map/ppermute | solution.py:403
  272.3 22.0 %collective-permute-done.15 = bf16[2,4,128,512]{3,2,1,0:T(8,128)(2,1)S(1)} collective-permute-done((bf16[2,4,128,512]{3,2,1,0:T(8,128)(2,1)S(1)}, bf16[2,4,128,512]{3,2,1,0:T(8,128)(2,1)S(1)}, u32[]{:S(2)}, u32[]{:S(2)}) %collective-permute-start.15) | collective-permute-done | bytes 1048608 | tf_op jit(solution)/shard_map/ppermute | solution.py:403
  294.3 33.7 %collective-permute-done.14 = bf16[2,4,128,512]{3,2,1,0:T(8,128)(2,1)S(1)} collective-permute-done((bf16[2,4,128,512]{3,2,1,0:T(8,128)(2,1)S(1)}, bf16[2,4,128,512]{3,2,1,0:T(8,128)(2,1)S(1)}, u32[]{:S(2)}, u32[]{:S(2)}) %collective-permute-start.14) | collective-permute-done | bytes 1048608 | tf_op jit(solution)/shard_map/ppermute | solution.py:403
  328.2 14.1 %collective-permute-start.17 = (bf16[4,128,512]{2,1,0:T(8,128)(2,1)S(1)}, bf16[4,128,512]{2,1,0:T(8,128)(2,1)S(1)}, u32[]{:S(2)}, u32[]{:S(2)}) collective-permute-start(bf16[4,128,512]{2,1,0:T(8,128)(2,1)S(1)} %fusion.2), channel_id=1, source_target_pairs={{0,1},{1,0},{2,3},{3,2},{4,5},{5,4},{6,7},{7,6},{8,9},{9,8},{10,11... | collective-permute-start | bytes 1572872 | tf_op jit(solution)/shard_map/ppermute | solution.py:387
  342.3 2.7 slice.75.refs_3_
  345.0 2.8 multiply_convert_fusion.refs_0_
  347.8 24.7 %dec_grad.1 = bf16[10,288,4096]{2,1,0:T(8,128)(2,1)} custom-call(s32[10]{0:T(128)} %copy-done.5, bf16[4,288,128]{2,1,0:T(8,128)(2,1)} %get-tuple-element.35.refs_0_, bf16[4,288,192]{2,1,0:T(8,128)(2,1)} %get-tuple-element.43.refs_1_, bf16[4,288,192]{2,1,0:T(8,128)(2,1)} %get-tuple-element.48.refs_2_, bf16[8,4,128,512]{3,2,1,0:T(8,128)(2,1)} %bitcast.40, ...), custom_call_target="tpu_custom_call" | custom-call | flops 1 | bytes 1 | tf_op jit(solution)/shard_map/dec_grad/pallas_call | solution.py:332
  372.5 2.8 fusion.refs_1_
  375.3 11.2 %enc_grad.1 = (bf16[4,2304,512]{2,1,0:T(8,128)(2,1)}, f32[4,512]{1,0:T(4,128)}) custom-call(bf16[4,2304,512]{2,1,0:T(8,128)(2,1)} %bitcast.34, bf16[4,128,512]{2,1,0:T(8,128)(2,1)} %multiply_convert_fusion.refs_0_, bf16[4,192,512]{2,1,0:T(8,128)(2,1)} %fusion.refs_1_, bf16[4,192,512]{2,1,0:T(8,128)(2,1)} %bitcast.41, s32[4,192,512]{2,1,0:T(8,128)} %slice.75.refs_3_), custom_call_target="tpu_custom_call" | custom-call | flops 1 | bytes 1 | tf_op jit(solution)/shard_map/enc_grad/pallas_call | solution.py:365
  (57 shorter events, 19.0 us)
Async XLA Ops:
  7.2 57.2 %all-gather.11.cloned.1.call-start = ((), (), s32[]{:S(2)}) async-start(), calls=%async_computation.6 | async-start | bytes 4718592 | tf_op jit(solution)/shard_map/all_gather | solution.py:463
  14.4 115.4 %all-gather.9.cloned.1.call-start = ((), (), s32[]{:S(2)}) async-start(), calls=%async_computation.5 | async-start | bytes 7077888 | tf_op jit(solution)/shard_map/all_gather | solution.py:463
  27.8 167.1 %all-gather.7.cloned.1.call-start = ((), (), s32[]{:S(2)}) async-start(), calls=%async_computation.4 | async-start | bytes 7077888 | tf_op jit(solution)/shard_map/all_gather | solution.py:463
  41.0 331.6 %reduce-scatter.3.cloned.1.call-start = ((), (), s32[]{:S(2)}) async-start(), calls=%async_computation.2 | async-start | bytes 7077888 | tf_op jit(solution)/shard_map/reduce_scatter | solution.py:481
  41.0 12.8 %copy-start.1 = (bf16[4,288,512]{2,1,0:T(8,128)(2,1)S(1)}, bf16[4,288,512]{2,1,0:T(8,128)(2,1)}, u32[]{:S(2)}) copy-start(bf16[4,288,512]{2,1,0:T(8,128)(2,1)} %param.11) | copy-start | bytes 3538948
  41.0 14.2 %copy-start.7 = (s32[10,2]{0,1:T(2,128)S(1)}, s32[10,2]{0,1:T(2,128)}, u32[]{:S(2)}) copy-start(s32[10,2]{0,1:T(2,128)} %param.17) | copy-start | bytes 244
  41.0 14.2 %copy-start.8 = (s32[10,2]{0,1:T(2,128)S(1)}, s32[10,2]{0,1:T(2,128)}, u32[]{:S(2)}) copy-start(s32[10,2]{0,1:T(2,128)} %constant.18) | copy-start | bytes 244
  55.4 9.0 %copy-start.5 = (s32[10]{0:T(128)}, s32[10]{0:T(128)S(1)}, u32[]{:S(2)}) copy-start(s32[10]{0:T(128)S(1)} %select_reduce_fusion.meta.perm) | copy-start | bytes 124
  64.4 16.8 %copy-start.6 = (f32[4,288]{1,0:T(4,128)S(1)}, f32[4,288]{1,0:T(4,128)}, u32[]{:S(2)}) copy-start(f32[4,288]{1,0:T(4,128)} %param.16) | copy-start | bytes 13828
  79.9 6.2 %collective-permute-start = (bf16[2,288,128]{2,1,0:T(8,128)(2,1)}, bf16[2,288,128]{2,1,0:T(8,128)(2,1)S(1)}, u32[]{:S(2)}, u32[]{:S(2)}) collective-permute-start(bf16[2,288,128]{2,1,0:T(8,128)(2,1)} %get-tuple-element.32), channel_id=1, source_target_pairs={{0,8},{8,0},{16,24},{24,16},{1,9},{9,1},{17,25},{25,17},{2,10},{10... | collective-permute-start | bytes 442376 | tf_op jit(solution)/shard_map/ppermute | solution.py:421
  82.3 6.1 %collective-permute-start.2 = (bf16[2,288,128]{2,1,0:T(8,128)(2,1)}, bf16[2,288,128]{2,1,0:T(8,128)(2,1)S(1)}, u32[]{:S(2)}, u32[]{:S(2)}) collective-permute-start(bf16[2,288,128]{2,1,0:T(8,128)(2,1)} %get-tuple-element.33), channel_id=1, source_target_pairs={{0,16},{8,24},{16,0},{24,8},{1,17},{9,25},{17,1},{25,9},{2,18},{10... | collective-permute-start | bytes 442376 | tf_op jit(solution)/shard_map/ppermute | solution.py:421
  87.1 5.3 %collective-permute-start.1 = (bf16[2,288,128]{2,1,0:T(8,128)(2,1)S(1)}, bf16[2,288,128]{2,1,0:T(8,128)(2,1)S(1)}, u32[]{:S(2)}, u32[]{:S(2)}) collective-permute-start(bf16[2,288,128]{2,1,0:T(8,128)(2,1)S(1)} %add_convert_fusion.15), channel_id=1, source_target_pairs={{0,16},{8,24},{16,0},{24,8},{1,17},{9,25},{17,1},{25,9},{2,18},{10... | collective-permute-start | bytes 442376 | tf_op jit(solution)/shard_map/ppermute | solution.py:421
  89.4 5.2 %collective-permute-start.3 = (bf16[2,288,128]{2,1,0:T(8,128)(2,1)S(1)}, bf16[2,288,128]{2,1,0:T(8,128)(2,1)S(1)}, u32[]{:S(2)}, u32[]{:S(2)}) collective-permute-start(bf16[2,288,128]{2,1,0:T(8,128)(2,1)S(1)} %add_convert_fusion.13), channel_id=1, source_target_pairs={{0,8},{8,0},{16,24},{24,16},{1,9},{9,1},{17,25},{25,17},{2,10},{10... | collective-permute-start | bytes 442376 | tf_op jit(solution)/shard_map/ppermute | solution.py:421
  110.9 6.9 %collective-permute-start.7 = (bf16[5,4,128,512]{3,2,1,0:T(8,128)(2,1)}, bf16[5,4,128,512]{3,2,1,0:T(8,128)(2,1)S(1)}, u32[]{:S(2)}, u32[]{:S(2)}) collective-permute-start(bf16[5,4,128,512]{3,2,1,0:T(8,128)(2,1)} %get-tuple-element.41), channel_id=1, source_target_pairs={{0,1},{1,0},{2,3},{3,2},{4,5},{5,4},{6,7},{7,6},{8,9},{9,8},{10,11... | collective-permute-start | bytes 7864328 | tf_op jit(solution)/shard_map/ppermute | solution.py:387
  110.9 6.8 %collective-permute-start.4 = (bf16[2,4,128,512]{3,2,1,0:T(8,128)(2,1)}, bf16[2,4,128,512]{3,2,1,0:T(8,128)(2,1)S(1)}, u32[]{:S(2)}, u32[]{:S(2)}) collective-permute-start(bf16[2,4,128,512]{3,2,1,0:T(8,128)(2,1)} %get-tuple-element.37), channel_id=1, source_target_pairs={{0,1},{1,0},{2,3},{3,2},{4,5},{5,4},{6,7},{7,6},{8,9},{9,8},{10,11... | collective-permute-start | bytes 3145736 | tf_op jit(solution)/shard_map/ppermute | solution.py:387
  117.8 1.5 copy-start
  145.8 9.4 %collective-permute-start.5 = (bf16[2,288,192]{2,1,0:T(8,128)(2,1)}, bf16[2,288,192]{2,1,0:T(8,128)(2,1)S(1)}, u32[]{:S(2)}, u32[]{:S(2)}) collective-permute-start(bf16[2,288,192]{2,1,0:T(8,128)(2,1)} %get-tuple-element.39), channel_id=1, source_target_pairs={{0,8},{8,0},{16,24},{24,16},{1,9},{9,1},{17,25},{25,17},{2,10},{10... | collective-permute-start | bytes 663560 | tf_op jit(solution)/shard_map/ppermute | solution.py:421
  147.3 10.5 %collective-permute-start.8 = (bf16[2,288,192]{2,1,0:T(8,128)(2,1)}, bf16[2,288,192]{2,1,0:T(8,128)(2,1)S(1)}, u32[]{:S(2)}, u32[]{:S(2)}) collective-permute-start(bf16[2,288,192]{2,1,0:T(8,128)(2,1)} %get-tuple-element.40), channel_id=1, source_target_pairs={{0,16},{8,24},{16,0},{24,8},{1,17},{9,25},{17,1},{25,9},{2,18},{10... | collective-permute-start | bytes 663560 | tf_op jit(solution)/shard_map/ppermute | solution.py:421
  156.2 8.5 %collective-permute-start.6 = (bf16[2,288,192]{2,1,0:T(8,128)(2,1)S(1)}, bf16[2,288,192]{2,1,0:T(8,128)(2,1)S(1)}, u32[]{:S(2)}, u32[]{:S(2)}) collective-permute-start(bf16[2,288,192]{2,1,0:T(8,128)(2,1)S(1)} %add_convert_fusion.11), channel_id=1, source_target_pairs={{0,16},{8,24},{16,0},{24,8},{1,17},{9,25},{17,1},{25,9},{2,18},{10... | collective-permute-start | bytes 663560 | tf_op jit(solution)/shard_map/ppermute | solution.py:421
  158.8 8.2 %collective-permute-start.9 = (bf16[2,288,192]{2,1,0:T(8,128)(2,1)S(1)}, bf16[2,288,192]{2,1,0:T(8,128)(2,1)S(1)}, u32[]{:S(2)}, u32[]{:S(2)}) collective-permute-start(bf16[2,288,192]{2,1,0:T(8,128)(2,1)S(1)} %add_convert_fusion.9), channel_id=1, source_target_pairs={{0,8},{8,0},{16,24},{24,16},{1,9},{9,1},{17,25},{25,17},{2,10},{10... | collective-permute-start | bytes 663560 | tf_op jit(solution)/shard_map/ppermute | solution.py:421
  184.7 190.6 %reduce-scatter.5.cloned.1.call-start = ((), (), s32[]{:S(2)}) async-start(), calls=%async_computation.3 | async-start | bytes 7077888 | tf_op jit(solution)/shard_map/reduce_scatter | solution.py:481
  210.4 9.4 %collective-permute-start.10 = (bf16[2,288,192]{2,1,0:T(8,128)(2,1)}, bf16[2,288,192]{2,1,0:T(8,128)(2,1)S(1)}, u32[]{:S(2)}, u32[]{:S(2)}) collective-permute-start(bf16[2,288,192]{2,1,0:T(8,128)(2,1)} %get-tuple-element.45), channel_id=1, source_target_pairs={{0,8},{8,0},{16,24},{24,16},{1,9},{9,1},{17,25},{25,17},{2,10},{10... | collective-permute-start | bytes 663560 | tf_op jit(solution)/shard_map/ppermute | solution.py:421
  212.1 10.5 %collective-permute-start.12 = (bf16[2,288,192]{2,1,0:T(8,128)(2,1)}, bf16[2,288,192]{2,1,0:T(8,128)(2,1)S(1)}, u32[]{:S(2)}, u32[]{:S(2)}) collective-permute-start(bf16[2,288,192]{2,1,0:T(8,128)(2,1)} %get-tuple-element.46), channel_id=1, source_target_pairs={{0,16},{8,24},{16,0},{24,8},{1,17},{9,25},{17,1},{25,9},{2,18},{10... | collective-permute-start | bytes 663560 | tf_op jit(solution)/shard_map/ppermute | solution.py:421
  220.9 8.6 %collective-permute-start.11 = (bf16[2,288,192]{2,1,0:T(8,128)(2,1)S(1)}, bf16[2,288,192]{2,1,0:T(8,128)(2,1)S(1)}, u32[]{:S(2)}, u32[]{:S(2)}) collective-permute-start(bf16[2,288,192]{2,1,0:T(8,128)(2,1)S(1)} %add_convert_fusion.7), channel_id=1, source_target_pairs={{0,16},{8,24},{16,0},{24,8},{1,17},{9,25},{17,1},{25,9},{2,18},{10... | collective-permute-start | bytes 663560 | tf_op jit(solution)/shard_map/ppermute | solution.py:421
  223.6 8.2 %collective-permute-start.13 = (bf16[2,288,192]{2,1,0:T(8,128)(2,1)S(1)}, bf16[2,288,192]{2,1,0:T(8,128)(2,1)S(1)}, u32[]{:S(2)}, u32[]{:S(2)}) collective-permute-start(bf16[2,288,192]{2,1,0:T(8,128)(2,1)S(1)} %add_convert_fusion.5), channel_id=1, source_target_pairs={{0,8},{8,0},{16,24},{24,16},{1,9},{9,1},{17,25},{25,17},{2,10},{10... | collective-permute-start | bytes 663560 | tf_op jit(solution)/shard_map/ppermute | solution.py:421
  249.4 1.2 copy-start.4
  249.5 2.6 copy-start.3
  249.5 6.6 %copy-start.2 = (bf16[2,4,128,512]{3,2,1,0:T(8,128)(2,1)S(1)}, bf16[2,4,128,512]{3,2,1,0:T(8,128)(2,1)}, u32[]{:S(2)}) copy-start(bf16[2,4,128,512]{3,2,1,0:T(8,128)(2,1)} %get-tuple-element.57) | copy-start | bytes 3145732
  250.7 21.6 %collective-permute-start.16 = (bf16[2,4,128,512]{3,2,1,0:T(8,128)(2,1)S(1)}, bf16[2,4,128,512]{3,2,1,0:T(8,128)(2,1)S(1)}, u32[]{:S(2)}, u32[]{:S(2)}) collective-permute-start(bf16[2,4,128,512]{3,2,1,0:T(8,128)(2,1)S(1)} %copy-done.4), channel_id=1, source_target_pairs={{0,2},{2,4},{4,6},{3,1},{5,3},{7,5},{8,10},{10,12},{12,14},{11,9},... | collective-permute-start | bytes 3145736 | tf_op jit(solution)/shard_map/ppermute | solution.py:403
  252.0 42.2 %collective-permute-start.15 = (bf16[2,4,128,512]{3,2,1,0:T(8,128)(2,1)S(1)}, bf16[2,4,128,512]{3,2,1,0:T(8,128)(2,1)S(1)}, u32[]{:S(2)}, u32[]{:S(2)}) collective-permute-start(bf16[2,4,128,512]{3,2,1,0:T(8,128)(2,1)S(1)} %copy-done.3), channel_id=1, source_target_pairs={{0,4},{2,6},{5,1},{7,3},{8,12},{10,14},{13,9},{15,11},{16,20},{18,... | collective-permute-start | bytes 3145736 | tf_op jit(solution)/shard_map/ppermute | solution.py:403
  256.0 72.0 %collective-permute-start.14 = (bf16[2,4,128,512]{3,2,1,0:T(8,128)(2,1)S(1)}, bf16[2,4,128,512]{3,2,1,0:T(8,128)(2,1)S(1)}, u32[]{:S(2)}, u32[]{:S(2)}) collective-permute-start(bf16[2,4,128,512]{3,2,1,0:T(8,128)(2,1)S(1)} %copy-done.2), channel_id=1, source_target_pairs={{0,6},{7,1},{8,14},{15,9},{16,22},{23,17},{24,30},{31,25}} | collective-permute-start | bytes 3145736 | tf_op jit(solution)/shard_map/ppermute | solution.py:403
  328.2 16.8 %collective-permute-start.17 = (bf16[4,128,512]{2,1,0:T(8,128)(2,1)S(1)}, bf16[4,128,512]{2,1,0:T(8,128)(2,1)S(1)}, u32[]{:S(2)}, u32[]{:S(2)}) collective-permute-start(bf16[4,128,512]{2,1,0:T(8,128)(2,1)S(1)} %fusion.2), channel_id=1, source_target_pairs={{0,1},{1,0},{2,3},{3,2},{4,5},{5,4},{6,7},{7,6},{8,9},{9,8},{10,11... | collective-permute-start | bytes 1572872 | tf_op jit(solution)/shard_map/ppermute | solution.py:387
Sparse Core Ops, SparseCore 0:
  14.5 49.8 all-gather.10
  66.0 63.6 all-gather.8
  131.4 63.3 all-gather.6
  197.6 73.8 reduce-scatter.2
  273.6 87.5 reduce-scatter.4
